TPU v7x, 32 devices: a whole 2x2x4 slice. The times are simulated.
32 devices in a mesh: region: 8 (over y, x, core), ctx: 4 (over z).
Axes of the slice: x: 2, y: 2, z: 4, core: 2. Of those that a mesh axis runs over, the one named last changes fastest.
Arguments:
- tokens: bfloat16 [8, 2048, 1152], P('region', 'ctx'), may hold values from -6 to 6
- element_ids: int32 [8, 2048], P('region', 'ctx'), may hold values from 0 to 4095, as said below
- element_slot: int32 [4096], replicated, may hold values from 0 to 4095, as said below
- live_count: int32 [8, 4], P('region', 'ctx'), may hold values from 128 to 512
- cond_table: bfloat16 [4096, 1152], P(('region', 'ctx')), may hold values from -6 to 6
- w_ada: bfloat16 [1152, 3456], replicated, may hold values from -0.1875 to 0.1875
- b_ada: float32 [3456], replicated, may hold values from -3 to 3
- w_qkv: bfloat16 [1152, 3456], replicated, may hold values from -8 to 8
- w_out: bfloat16 [1152, 1152], replicated, may hold values from -0.1875 to 0.1875
Outputs:
- block_out: bfloat16 [8, 2048, 1152], P('region', 'ctx')
Inputs may be any that keep to these rules, and one draw needn't show every extreme that they name: element_ids: within each device's block of 512 patches (region r, positions c * 512 to (c + 1) * 512 - 1, device r * 4 + c of region+ctx), at most 24 patches name elements whose table row lies on one device (rows o * 128 to (o + 1) * 128 - 1); in every block some device is named by exactly 24 solid patches. element_slot is a permutation: element e is row element_slot[e] of cond_table.
All inputs are finite; a program needn't handle non-finite values.
Results may differ from a plain program's by a relative error of at most 0.027.
Values may be sent and summed in bfloat16 or wider, within the bound.
No kernel may reach another device: no remote copies, remote signals or barrier semaphores. Data moves between devices by JAX's collectives and lax.ppermute only.
A program may use at most 192 MiB of HBM per device.

v0:
```python
import math

import jax
import jax.numpy as jnp
from jax import lax
from jax.sharding import PartitionSpec as P

HEADS = 16


def layer_modulate(device_tokens, mods, width):
    values = device_tokens.astype(jnp.float32)
    center = jnp.mean(values, axis=1, keepdims=True)
    spread = jnp.mean((values - center) ** 2, axis=1, keepdims=True)
    normed = (values - center) * lax.rsqrt(spread + 1e-06)
    shift = mods[:, :width]
    scale = mods[:, width : 2 * width]
    return (normed * (1.0 + scale) + shift).astype(jnp.bfloat16)


def per_device(
    tokens, element_ids, element_slot, live_count, cond_table, w_ada, b_ada, w_qkv, w_out
):
    device_tokens = tokens[0]
    tok_rows, width = device_tokens.shape
    owners = lax.axis_size(("region", "ctx"))
    elem_rows = cond_table.shape[0]
    capacity = max(2, 3 * tok_rows // (2 * owners))
    slots = element_slot[element_ids[0]]
    owner_index = slots // elem_rows
    local_row = slots % elem_rows
    position = jnp.arange(tok_rows, dtype=jnp.int32)
    solid = position < live_count[0, 0]
    earlier = (
        (owner_index[:, None] == owner_index[None, :])
        & (position[None, :] < position[:, None])
        & solid[None, :]
    )
    place_rank = jnp.sum(earlier.astype(jnp.int32), axis=1)
    target = jnp.where(solid, owner_index * capacity + place_rank, owners * capacity)
    requests = jnp.zeros((owners * capacity,), jnp.int32).at[target].set(local_row, mode="drop")
    asked = lax.all_to_all(
        requests.reshape(owners, capacity),
        ("region", "ctx"),
        split_axis=0,
        concat_axis=0,
        tiled=True,
    ).reshape(-1)
    pick_at = jnp.minimum(target, owners * capacity - 1)
    served = cond_table[asked].reshape(owners, capacity, width)
    replies = lax.all_to_all(served, ("region", "ctx"), split_axis=0, concat_axis=0, tiled=True)
    picked = replies.reshape(owners * capacity, width)[pick_at]
    activated = jnp.where(solid[:, None], jax.nn.silu(picked.astype(jnp.float32)), 0.0).astype(
        jnp.bfloat16
    )
    mods = (jnp.dot(activated, w_ada, preferred_element_type=jnp.float32) + b_ada).astype(
        jnp.bfloat16
    )
    mods = mods.astype(jnp.float32)
    modulated = layer_modulate(device_tokens, mods, width)
    qkv = jnp.dot(modulated, w_qkv, preferred_element_type=jnp.float32).astype(jnp.bfloat16)
    queries = qkv[:, :width]
    keys_here = qkv[:, width : 2 * width]
    values_here = qkv[:, 2 * width :]
    head_dim = width // HEADS
    inverse_root = 1.0 / math.sqrt(head_dim)
    query_heads = queries.reshape(tok_rows, HEADS, head_dim)
    initial = (
        jnp.full((HEADS, tok_rows), -1e30, jnp.float32),
        jnp.zeros((HEADS, tok_rows), jnp.float32),
        jnp.zeros((HEADS, tok_rows, head_dim), jnp.float32),
    )
    keys_piece = lax.all_gather(keys_here, "ctx", axis=0, tiled=True)
    values_piece = lax.all_gather(values_here, "ctx", axis=0, tiled=True)
    piece_rows = keys_piece.shape[0]
    block_rows = math.gcd(piece_rows, 512)
    key_blocks = keys_piece.reshape(piece_rows // block_rows, block_rows, HEADS, head_dim)
    value_blocks = values_piece.reshape(piece_rows // block_rows, block_rows, HEADS, head_dim)

    def advance(state, blocks):
        running_max, denominator, weighted = state
        key_block, value_block = blocks
        scores = (
            jnp.einsum("qhe,khe->hqk", query_heads, key_block, preferred_element_type=jnp.float32)
            * inverse_root
        )
        new_max = jnp.maximum(running_max, jnp.max(scores, axis=2))
        shrink = jnp.exp(running_max - new_max)
        expo = jnp.exp(scores - new_max[:, :, None])
        denominator = denominator * shrink + jnp.sum(expo, axis=2)
        weighted = weighted * shrink[:, :, None] + jnp.einsum(
            "hqk,khe->hqe",
            expo.astype(jnp.bfloat16),
            value_block,
            preferred_element_type=jnp.float32,
        )
        return ((new_max, denominator, weighted), None)

    result, _ = lax.scan(advance, initial, (key_blocks, value_blocks))
    final_max, denominator, weighted = result
    result = weighted / denominator[:, :, None]
    attended = jnp.transpose(result, (1, 0, 2)).reshape(tok_rows, width).astype(jnp.bfloat16)
    projected = jnp.dot(attended, w_out, preferred_element_type=jnp.float32)
    gate = mods[:, 2 * width :]
    output = (device_tokens.astype(jnp.float32) + gate * projected).astype(jnp.bfloat16)
    return output[None]


def solution(mesh):
    placed = (
        P("region", "ctx", None),
        P("region", "ctx"),
        P(),
        P("region", "ctx"),
        P(("region", "ctx"), None),
        P(),
        P(),
        P(),
        P(),
    )
    return jax.shard_map(
        per_device, mesh=mesh, in_specs=placed, out_specs=P("region", "ctx", None), check_vma=False
    )
```

profile of v0, /device:TPU:17, one launch (start us, length us, event | category | flops | bytes accessed | tf_op | source)
XLA Modules:
  0.0 440.7 jit_solution(17174782127484296034)
XLA Ops:
  6.5 0.0 copy-start
  6.5 0.8 compare_select_fusion.3
  7.4 3.4 gather_fusion
  11.5 0.3 convert_reduce_fusion.1
  11.8 2.4 scatter_custom_fusion
  14.3 0.1 all_to_all.9
  14.4 10.7 %all_to_all.14 = s32[32,1,24]{2,1,0:T(1,128)S(1)} all-to-all(s32[32,1,24]{2,1,0:T(1,128)S(1)} %bitcast.80), channel_id=1, replica_groups=mesh['region'=8,'ctx'=4] {'region','ctx'}, dimensions={0} | all-to-all | bytes 6144 | tf_op jit(solution)/shard_map/all_to_all | solution.py:42
  25.1 0.5 broadcast.337
  25.6 0.7 reduce.6
  26.3 0.1 reshape.222
  26.4 0.0 copy-done.1
  26.4 3.7 gather_fusion.1
  30.1 5.9 %all-to-all-start.1 = ((bf16[32,24,1152]{2,1,0:T(8,128)(2,1)}), bf16[32,24,1152]{2,1,0:T(8,128)(2,1)}, u32[]{:S(2)}, u32[]{:S(2)}) async-start(bf16[32,24,1152]{2,1,0:T(8,128)(2,1)} %bitcast.78), calls=%async_computation.1 | async-start | bytes 3538944 | tf_op jit(solution)/shard_map/all_to_all | solution.py:51
  36.0 0.0 all-gather.3.cloned.1.call-start
  36.0 1.5 convert_reduce_fusion
  37.5 1.7 fusion.26
  39.2 36.9 %all-to-all-done.1 = bf16[32,24,1152]{2,1,0:T(8,128)(2,1)} async-done(((bf16[32,24,1152]{2,1,0:T(8,128)(2,1)}), bf16[32,24,1152]{2,1,0:T(8,128)(2,1)}, u32[]{:S(2)}, u32[]{:S(2)}) %all-to-all-start.1) | async-done | bytes 1769504 | tf_op jit(solution)/shard_map/all_to_all | solution.py:51
  76.1 5.4 %gather_fusion.2 = bf16[512,1152]{1,0:T(8,128)(2,1)} fusion(bf16[768,1152]{1,0:T(8,128)(2,1)} %bitcast.9, s32[1024]{0:T(1024)S(1)} %pad_clamp_fusion), kind=kCustom, calls=%fused_computation.2 | custom fusion | bytes 2361344 | tf_op jit(solution)/shard_map/gather | solution.py:52
  81.5 0.0 copy-done.4
  81.5 8.0 %fusion.19 = f32[512,3456]{1,0:T(8,128)S(1)} fusion(bf16[1152,3456]{1,0:T(8,128)(2,1)} %param.16, f32[3456]{0:T(1024)S(1)} %copy-done.4, bf16[512,1152]{1,0:T(8,128)(2,1)} %gather_fusion.2, pred[512]{0:T(512)(128)(4,1)S(1)} %iota_compare_fusion.1), kind=kOutput, calls=%fused_computation.27 | convolution fusion | flops 4086300672 | bytes 16234496 | tf_op jit(solution)/shard_map/dot_general | solution.py:56
  89.5 0.0 copy-done.2
  89.6 11.4 %convolution_convert_fusion = bf16[512,3456]{1,0:T(8,128)(2,1)S(1)} fusion(bf16[1152,3456]{1,0:T(8,128)(2,1)} %param.18, bf16[1,512,1152]{2,1,0:T(8,128)(2,1)S(1)} %copy-done.2, f32[512,3456]{1,0:T(8,128)S(1)} %fusion.19, f32[512]{0:T(512)S(1)} %add_rsqrt_fusion, f32[512]{0:T(512)S(1)} %broadcast_multiply_fusion), kind=kOutput, calls=%fused_computation.28 | convolution fusion | flops 4082761728 | bytes 17403904 | tf_op jit(solution)/shard_map/dot_general | solution.py:61
  101.0 1.9 fusion.52
  102.9 0.0 all-gather.3.cloned.1.call-update
  102.9 0.2 all-gather.5.cloned.1.call-start
  103.2 0.5 all-gather.5.cloned.1.call-update
  103.7 2.4 copy.30
  106.1 84.1 %all-gather.3.cloned.1.call-done = bf16[2048,1152]{1,0:T(8,128)(2,1)} async-done(((bf16[512,1152]{1,0:T(8,128)(2,1)}), bf16[2048,1152]{1,0:T(8,128)(2,1)}) %all-gather.3.cloned.1.call-update) | async-done | bytes 4718608 | tf_op jit(solution)/shard_map/all_gather | solution.py:73
  190.3 17.4 %reshape.260 = bf16[4,512,16,72]{3,2,1,0:T(8,128)(2,1)} reshape(bf16[2048,1152]{1,0:T(8,128)(2,1)} %all-gather.3.cloned.1.call-done) | data formatting | bytes 9437184 | tf_op jit(solution)/shard_map/reshape | solution.py:77
  207.7 13.1 %copy.32 = bf16[4,512,16,72]{1,3,2,0:T(8,128)(2,1)} copy(bf16[4,512,16,72]{3,2,1,0:T(8,128)(2,1)} %reshape.260) | data formatting | bytes 9437184
  220.8 58.9 %all-gather.5.cloned.1.call-done = bf16[2048,1152]{1,0:T(8,128)(2,1)} async-done(((bf16[512,1152]{1,0:T(8,128)(2,1)}), bf16[2048,1152]{1,0:T(8,128)(2,1)}) %all-gather.5.cloned.1.call-update) | async-done | bytes 4718608 | tf_op jit(solution)/shard_map/all_gather | solution.py:74
  279.7 17.4 %reshape.261 = bf16[4,512,16,72]{3,2,1,0:T(8,128)(2,1)} reshape(bf16[2048,1152]{1,0:T(8,128)(2,1)} %all-gather.5.cloned.1.call-done) | data formatting | bytes 9437184 | tf_op jit(solution)/shard_map/reshape | solution.py:78
  297.2 13.1 %copy.33 = bf16[4,512,16,72]{1,3,2,0:T(8,128)(2,1)} copy(bf16[4,512,16,72]{3,2,1,0:T(8,128)(2,1)} %reshape.261) | data formatting | bytes 9437184
  310.2 116.9 %while.15 = (s32[]{:T(128)}, f32[16,512]{1,0:T(8,128)S(1)}, f32[16,512]{1,0:T(8,128)S(1)}, f32[16,512,72]{1,2,0:T(8,128)}, bf16[4,512,16,72]{1,3,2,0:T(8,128)(2,...) while((s32[]{:T(128)}, f32[16,512]{1,0:T(8,128)S(1)}, ...), condition=%wide.region_7.8_spmd.clone, body=%wide.region_4.7_spmd.clone.sunk | while | flops 1243324416 | bytes 59114596 | solution.py:99
  310.2 9.7 %bitcast_reduce_fusion.2 = (f32[16,512]{1,0:T(8,128)S(1)}, f32[16,512,512]{2,1,0:T(8,128)}) fusion(bf16[512,16,72]{0,2,1:T(8,128)(2,1)} %get-tuple-element.196, bf16[4,512,16,72]{1,3,2,0:T(8,128)(2,1)} %get-tuple-element.195, s32[]{:T(128)} %get-tuple-element.182), kind=kOutput, calls=%fused_computation.5.clone.1 | convolution fusion | flops 612360192 | bytes 19169792 | tf_op jit(solution)/shard_map/while/body/eval_jaxpr/qhe,khe->hqk/dot_general | solution.py:84
  320.0 8.6 %fusion.67 = f32[16,512]{1,0:T(8,128)S(1)} fusion(f32[16,512,512]{2,1,0:T(8,128)} %get-tuple-element.170, f32[16,512]{1,0:T(8,128)S(1)} %select_maximum_fusion.2), kind=kLoop, calls=%fused_computation.8.clone.1 | loop fusion | flops 12574720 | bytes 16842752 | tf_op jit(solution)/shard_map/while/body/eval_jaxpr/reduce_sum | solution.py:90
  328.6 10.3 %fusion.69 = f32[16,512,72]{1,2,0:T(8,128)} fusion(f32[16,512,72]{1,2,0:T(8,128)} %get-tuple-element.185, f32[16,512,512]{2,1,0:T(8,128)} %get-tuple-element.170, f32[16,512]{1,0:T(8,128)S(1)} %select_maximum_fusion.2, bf16[4,512,16,72]{1,3,2,0:T(8,128)(2,1)} %get-tuple-element.197, s32[]{:T(128)} %get-tuple-element.182, ...), kind=kOutput, calls=%fused_computation.13.clone.1 | convolution fusion | flops 618332160 | bytes 22741504 | tf_op jit(solution)/shard_map/while/body/eval_jaxpr/hqk,khe->hqe/dot_general | solution.py:91
  338.9 9.7 %bitcast_reduce_fusion.2 = (f32[16,512]{1,0:T(8,128)S(1)}, f32[16,512,512]{2,1,0:T(8,128)}) fusion(bf16[512,16,72]{0,2,1:T(8,128)(2,1)} %get-tuple-element.196, bf16[4,512,16,72]{1,3,2,0:T(8,128)(2,1)} %get-tuple-element.195, s32[]{:T(128)} %get-tuple-element.182), kind=kOutput, calls=%fused_computation.5.clone.1 | convolution fusion | flops 612360192 | bytes 19169792 | tf_op jit(solution)/shard_map/while/body/eval_jaxpr/qhe,khe->hqk/dot_general | solution.py:84
  348.7 8.6 %fusion.67 = f32[16,512]{1,0:T(8,128)S(1)} fusion(f32[16,512,512]{2,1,0:T(8,128)} %get-tuple-element.170, f32[16,512]{1,0:T(8,128)S(1)} %select_maximum_fusion.2), kind=kLoop, calls=%fused_computation.8.clone.1 | loop fusion | flops 12574720 | bytes 16842752 | tf_op jit(solution)/shard_map/while/body/eval_jaxpr/reduce_sum | solution.py:90
  357.2 11.1 %fusion.69 = f32[16,512,72]{1,2,0:T(8,128)} fusion(f32[16,512,72]{1,2,0:T(8,128)} %get-tuple-element.185, f32[16,512,512]{2,1,0:T(8,128)} %get-tuple-element.170, f32[16,512]{1,0:T(8,128)S(1)} %select_maximum_fusion.2, bf16[4,512,16,72]{1,3,2,0:T(8,128)(2,1)} %get-tuple-element.197, s32[]{:T(128)} %get-tuple-element.182, ...), kind=kOutput, calls=%fused_computation.13.clone.1 | convolution fusion | flops 618332160 | bytes 22741504 | tf_op jit(solution)/shard_map/while/body/eval_jaxpr/hqk,khe->hqe/dot_general | solution.py:91
  368.3 9.7 %bitcast_reduce_fusion.2 = (f32[16,512]{1,0:T(8,128)S(1)}, f32[16,512,512]{2,1,0:T(8,128)}) fusion(bf16[512,16,72]{0,2,1:T(8,128)(2,1)} %get-tuple-element.196, bf16[4,512,16,72]{1,3,2,0:T(8,128)(2,1)} %get-tuple-element.195, s32[]{:T(128)} %get-tuple-element.182), kind=kOutput, calls=%fused_computation.5.clone.1 | convolution fusion | flops 612360192 | bytes 19169792 | tf_op jit(solution)/shard_map/while/body/eval_jaxpr/qhe,khe->hqk/dot_general | solution.py:84
  378.1 8.6 %fusion.67 = f32[16,512]{1,0:T(8,128)S(1)} fusion(f32[16,512,512]{2,1,0:T(8,128)} %get-tuple-element.170, f32[16,512]{1,0:T(8,128)S(1)} %select_maximum_fusion.2), kind=kLoop, calls=%fused_computation.8.clone.1 | loop fusion | flops 12574720 | bytes 16842752 | tf_op jit(solution)/shard_map/while/body/eval_jaxpr/reduce_sum | solution.py:90
  386.6 11.1 %fusion.69 = f32[16,512,72]{1,2,0:T(8,128)} fusion(f32[16,512,72]{1,2,0:T(8,128)} %get-tuple-element.185, f32[16,512,512]{2,1,0:T(8,128)} %get-tuple-element.170, f32[16,512]{1,0:T(8,128)S(1)} %select_maximum_fusion.2, bf16[4,512,16,72]{1,3,2,0:T(8,128)(2,1)} %get-tuple-element.197, s32[]{:T(128)} %get-tuple-element.182, ...), kind=kOutput, calls=%fused_computation.13.clone.1 | convolution fusion | flops 618332160 | bytes 22741504 | tf_op jit(solution)/shard_map/while/body/eval_jaxpr/hqk,khe->hqe/dot_general | solution.py:91
  397.7 9.7 %bitcast_reduce_fusion.2 = (f32[16,512]{1,0:T(8,128)S(1)}, f32[16,512,512]{2,1,0:T(8,128)}) fusion(bf16[512,16,72]{0,2,1:T(8,128)(2,1)} %get-tuple-element.196, bf16[4,512,16,72]{1,3,2,0:T(8,128)(2,1)} %get-tuple-element.195, s32[]{:T(128)} %get-tuple-element.182), kind=kOutput, calls=%fused_computation.5.clone.1 | convolution fusion | flops 612360192 | bytes 19169792 | tf_op jit(solution)/shard_map/while/body/eval_jaxpr/qhe,khe->hqk/dot_general | solution.py:84
  407.5 8.6 %fusion.67 = f32[16,512]{1,0:T(8,128)S(1)} fusion(f32[16,512,512]{2,1,0:T(8,128)} %get-tuple-element.170, f32[16,512]{1,0:T(8,128)S(1)} %select_maximum_fusion.2), kind=kLoop, calls=%fused_computation.8.clone.1 | loop fusion | flops 12574720 | bytes 16842752 | tf_op jit(solution)/shard_map/while/body/eval_jaxpr/reduce_sum | solution.py:90
  416.0 11.1 %fusion.69 = f32[16,512,72]{1,2,0:T(8,128)} fusion(f32[16,512,72]{1,2,0:T(8,128)} %get-tuple-element.185, f32[16,512,512]{2,1,0:T(8,128)} %get-tuple-element.170, f32[16,512]{1,0:T(8,128)S(1)} %select_maximum_fusion.2, bf16[4,512,16,72]{1,3,2,0:T(8,128)(2,1)} %get-tuple-element.197, s32[]{:T(128)} %get-tuple-element.182, ...), kind=kOutput, calls=%fused_computation.13.clone.1 | convolution fusion | flops 618332160 | bytes 22741504 | tf_op jit(solution)/shard_map/while/body/eval_jaxpr/hqk,khe->hqe/dot_general | solution.py:91
  427.1 2.1 divide_convert_fusion
  429.2 4.6 %fusion.25 = bf16[1,512,1152]{2,1,0:T(8,128)(2,1)} fusion(bf16[512,1152]{0,1:T(8,128)(2,1)S(1)} %bitcast.79, bf16[1152,1152]{1,0:T(8,128)(2,1)S(1)} %copy-done, bf16[1,512,1152]{2,1,0:T(8,128)(2,1)S(1)} %copy-done.3, f32[512,3456]{1,0:T(8,128)} %copy-done.5), kind=kOutput, calls=%fused_computation.39 | convolution fusion | flops 1361313792 | bytes 8552448 | tf_op jit(solution)/shard_map/dot_general | solution.py:103
  (33 shorter events, 0.2 us)
Async XLA Ops:
  6.5 422.7 %copy-start = (bf16[1152,1152]{1,0:T(8,128)(2,1)S(1)}, bf16[1152,1152]{1,0:T(8,128)(2,1)}, u32[]{:S(2)}) copy-start(bf16[1152,1152]{1,0:T(8,128)(2,1)} %param.19) | copy-start | bytes 7962628
  6.5 19.9 %copy-start.1 = (bf16[128,1152]{1,0:T(8,128)(2,1)S(1)}, bf16[128,1152]{1,0:T(8,128)(2,1)}, u32[]{:S(2)}) copy-start(bf16[128,1152]{1,0:T(8,128)(2,1)} %param.15) | copy-start | bytes 884740
  30.1 46.1 %all-to-all-start.1 = ((bf16[32,24,1152]{2,1,0:T(8,128)(2,1)}), bf16[32,24,1152]{2,1,0:T(8,128)(2,1)}, u32[]{:S(2)}, u32[]{:S(2)}) async-start(bf16[32,24,1152]{2,1,0:T(8,128)(2,1)} %bitcast.78), calls=%async_computation.1 | async-start | bytes 3538944 | tf_op jit(solution)/shard_map/all_to_all | solution.py:51
  36.0 154.3 %all-gather.3.cloned.1.call-start = ((), (), s32[]{:S(2)}) async-start(), calls=%async_computation.2 | async-start | bytes 5898240 | tf_op jit(solution)/shard_map/all_gather | solution.py:73
  76.1 5.4 %copy-start.4 = (f32[3456]{0:T(1024)S(1)}, f32[3456]{0:T(1024)}, u32[]{:S(2)}) copy-start(f32[3456]{0:T(1024)} %param.17) | copy-start | bytes 41476
  81.5 8.0 %copy-start.2 = (bf16[1,512,1152]{2,1,0:T(8,128)(2,1)S(1)}, bf16[1,512,1152]{2,1,0:T(8,128)(2,1)}, u32[]{:S(2)}) copy-start(bf16[1,512,1152]{2,1,0:T(8,128)(2,1)} %param.11) | copy-start | bytes 3538948
  89.6 11.5 %copy-start.5 = (f32[512,3456]{1,0:T(8,128)}, f32[512,3456]{1,0:T(8,128)S(1)}, u32[]{:S(2)}) copy-start(f32[512,3456]{1,0:T(8,128)S(1)} %fusion.19) | copy-start | bytes 21233668
  102.9 176.8 %all-gather.5.cloned.1.call-start = ((), (), s32[]{:S(2)}) async-start(), calls=%async_computation.3 | async-start | bytes 5898240 | tf_op jit(solution)/shard_map/all_gather | solution.py:74
  427.1 2.1 copy-start.3
Sparse Core Ops, SparseCore 0:
  103.1 87.1 all-gather.2
  191.8 87.8 all-gather.4
where the time goes:
time: 446 us; the launch traced here: 441 us
  waiting for transfers between devices  180 us (40%)
  matrix products  107 us (24%)
  local copies, waits for them, and re-layouts  81 us (18%)
  other arithmetic  41.5 us (9%)
  between operations  14.2 us (3%)
  blocking collectives  10.7 us (2%)
  starting transfers between devices  6.14 us (1%)
    all_gather x1, waiting for transfers between devices, per_device(): keys_piece = lax.all_gather(keys_here, 'ctx', axis=0, tiled=True)  84.1 us
    all_gather x1, waiting for transfers between devices, per_device(): values_piece = lax.all_gather(values_here, 'ctx', axis=0, tiled=True)  58.9 us
    dot_general x4, matrix products, advance(): jnp.einsum('hqk,khe->hqe', expo.astype(jnp.bfloat16), value_block, prefer...  43.5 us
    dot_general x4, matrix products, advance(): jnp.einsum('qhe,khe->hqk', query_heads, key_block, preferred_element_type...  39 us
    all_to_all x1, waiting for transfers between devices, per_device(): lax.all_to_all(served, ('region', 'ctx'), split_axis=0, concat_axis=0, ti...  36.9 us
    reduce_sum x4, other arithmetic, advance(): denominator = denominator * shrink + jnp.sum(expo, axis=2)  34.2 us
    unnamed x14, local copies, waits for them, and re-layouts  26.2 us
    reshape x1, local copies, waits for them, and re-layouts, per_device(): keys_piece.reshape(piece_rows // block_rows, block_rows, HEADS, head_dim)  17.4 us
  transfers between devices with their start and end apart: 3, of which 3 were waited for; matrix products, arithmetic and copies ran while one was open for 8% of the time, Pallas kernels for 0%

commit v1 on v0

v1 whole, which is shorter than its diff:
```python
import functools
import math

import jax
import jax.numpy as jnp
from jax import lax
from jax.experimental import pallas as pl
from jax.experimental.pallas import tpu as pltpu
from jax.sharding import PartitionSpec as P

HEADS = 16
F32 = jnp.float32
BF16 = jnp.bfloat16
VMEM_LIMIT = 56 * 2**20


def contract(a, b, dims):
    return lax.dot_general(a, b, (dims, ((), ())), preferred_element_type=F32)


def pick_kernel(bases, count, idx_ref, acc_ref, *refs):
    pieces, (out_ref, rows_ref) = refs[:-2], refs[-2:]
    rows = pieces[0].shape[0]

    @pl.when(pl.program_id(0) == 0)
    def _():
        for n, piece in enumerate(pieces):
            rows_ref[n * rows : (n + 1) * rows, :] = piece[...]

    idx = idx_ref[...]
    lane = lax.broadcasted_iota(jnp.int32, (1, rows), 1)
    hot = jnp.concatenate(
        [jnp.where(idx == lane + base, 1.0, 0.0).astype(BF16) for base in bases], axis=1
    )
    picked = contract(hot, rows_ref[...], ((1,), (0,)))
    out_ref[...] = (picked + acc_ref[...].astype(F32)).astype(BF16)


def pick_rows(idx, acc, pieces, bases, block):
    count, width = acc.shape
    rows = pieces[0].shape[0]
    return pl.pallas_call(
        functools.partial(pick_kernel, bases, count),
        grid=(count // block,),
        in_specs=[
            pl.BlockSpec((block, 1), lambda i: (i, 0)),
            pl.BlockSpec((block, width), lambda i: (i, 0)),
        ]
        + [
            pl.BlockSpec((rows, width), lambda i: (0, 0), pipeline_mode=pl.Buffered(1))
            for _ in pieces
        ],
        out_specs=pl.BlockSpec((block, width), lambda i: (i, 0)),
        out_shape=jax.ShapeDtypeStruct((count, width), BF16),
        scratch_shapes=[pltpu.VMEM((len(pieces) * rows, width), BF16)],
        input_output_aliases={1: 0},
        compiler_params=pltpu.CompilerParams(vmem_limit_bytes=VMEM_LIMIT),
        cost_estimate=pl.CostEstimate(
            flops=2 * count * len(pieces) * rows * width,
            bytes_accessed=2 * width * (2 * count + len(pieces) * rows),
            transcendentals=0,
        ),
        name="pick",
    )(idx, acc, *pieces)


def project_kernel(
    query_scale, place_ref, tok_ref, act_ref, wada_ref, bada_ref, wt_ref, kv_ref, q_ref, gate_ref
):
    width = tok_ref.shape[1]
    values = tok_ref[...].astype(F32)
    center = jnp.mean(values, axis=1, keepdims=True)
    moved = values - center
    spread = jnp.mean(moved * moved, axis=1, keepdims=True)
    normed = moved * lax.rsqrt(spread + 1e-06)
    act = jax.nn.silu(act_ref[...].astype(F32)).astype(BF16)

    def mods(lo):
        part = contract(act, wada_ref[:, lo : lo + width], ((1,), (0,)))
        return (part + bada_ref[:, lo : lo + width]).astype(BF16)

    shift = mods(0).astype(F32)
    scale = mods(width).astype(F32)
    modulated = (normed * (1.0 + scale) + shift).astype(BF16)
    kv_ref[...] = contract(wt_ref[width:, :], modulated, ((1,), (1,))).astype(BF16)
    i = pl.program_id(0)

    @pl.when((i >= place_ref[0]) & (i < place_ref[0] + 2))
    def _():
        gate_ref[...] = mods(2 * width)
        q_ref[...] = (contract(wt_ref[:width, :], modulated, ((1,), (1,))) * query_scale).astype(
            BF16
        )


def project(place, tok, act, w_ada, b_ada, wt, block):
    count, width = tok.shape
    query_scale = math.log2(math.e) / math.sqrt(width // HEADS)

    def mine(i, place):
        return jnp.clip(i - place[0], 0, 1) ^ place[1]

    def fixed(shape):
        return pl.BlockSpec(shape, lambda i, place: (0, 0), pipeline_mode=pl.Buffered(1))

    return pl.pallas_call(
        functools.partial(project_kernel, query_scale),
        grid_spec=pltpu.PrefetchScalarGridSpec(
            num_scalar_prefetch=1,
            grid=(count // block,),
            in_specs=[
                pl.BlockSpec((block, width), lambda i, place: (i, 0)),
                pl.BlockSpec((block, width), lambda i, place: (i, 0)),
                fixed(w_ada.shape),
                fixed(b_ada.shape),
                fixed(wt.shape),
            ],
            out_specs=[
                pl.BlockSpec((2 * width, block), lambda i, place: (0, i)),
                pl.BlockSpec((width, block), lambda i, place: (0, mine(i, place))),
                pl.BlockSpec((block, width), lambda i, place: (mine(i, place), 0)),
            ],
        ),
        out_shape=[
            jax.ShapeDtypeStruct((2 * width, count), BF16),
            jax.ShapeDtypeStruct((width, 2 * block), BF16),
            jax.ShapeDtypeStruct((2 * block, width), BF16),
        ],
        compiler_params=pltpu.CompilerParams(vmem_limit_bytes=VMEM_LIMIT),
        name="project",
    )(place, tok, act, w_ada, b_ada, wt)


def attend_kernel(head_dim, chunk, q_ref, ka_ref, kb_ref, va_ref, vb_ref, o_ref, s_ref):
    pair = q_ref.shape[0]
    row = lax.broadcasted_iota(jnp.int32, (pair, 1), 0)
    q = q_ref[...]
    parts = [(ka_ref, va_ref, i) for i in range(0, ka_ref.shape[1], chunk)]
    parts += [(kb_ref, vb_ref, i) for i in range(0, kb_ref.shape[1], chunk)]
    results = []
    for j in range(2):
        own = (row >= head_dim) if j else (row < head_dim)
        head_q = jnp.where(own, q, jnp.zeros_like(q))
        top = None
        for n, (k_ref, _, i) in enumerate(parts):
            scores = contract(k_ref[:, i : i + chunk], head_q, ((0,), (0,)))
            s_ref[j, n * chunk : (n + 1) * chunk, :] = scores
            peak = jnp.max(scores, axis=0, keepdims=True)
            top = peak if top is None else jnp.maximum(top, peak)
        weighted = denominator = None
        for n, (_, v_ref, i) in enumerate(parts):
            expo = jnp.exp2(s_ref[j, n * chunk : (n + 1) * chunk, :] - top)
            total = jnp.sum(expo, axis=0, keepdims=True)
            part = contract(v_ref[:, i : i + chunk], expo.astype(BF16), ((1,), (0,)))
            weighted = part if weighted is None else weighted + part
            denominator = total if denominator is None else denominator + total
        results.append(weighted / denominator)
    o_ref[...] = jnp.where(row < head_dim, results[0], results[1]).astype(BF16)


def attend(qt, kv_here, kv_there):
    width, queries = qt.shape
    keys = kv_here.shape[1]
    head_dim = width // HEADS
    pair, pairs = 2 * head_dim, HEADS // 2
    chunk = math.gcd(keys, 1024)
    first = pl.BlockSpec((pair, keys), lambda p: (p, 0))
    second = pl.BlockSpec((pair, keys), lambda p: (p + pairs, 0))
    return pl.pallas_call(
        functools.partial(attend_kernel, head_dim, chunk),
        grid=(pairs,),
        in_specs=[pl.BlockSpec((pair, queries), lambda p: (p, 0)), first, first, second, second],
        out_specs=pl.BlockSpec((pair, queries), lambda p: (p, 0)),
        out_shape=jax.ShapeDtypeStruct((width, queries), BF16),
        scratch_shapes=[pltpu.VMEM((2, 2 * keys, queries), F32)],
        compiler_params=pltpu.CompilerParams(vmem_limit_bytes=VMEM_LIMIT),
        name="attend",
    )(qt, kv_here, kv_there, kv_here, kv_there)


def finish_kernel(place_ref, att_ref, tok_ref, gate_ref, w_ref, o_ref):
    projected = contract(att_ref[...], w_ref[...], ((0,), (0,)))
    o_ref[...] = (tok_ref[...].astype(F32) + gate_ref[...].astype(F32) * projected).astype(BF16)


def finish(place, attended, tok, gate, w_out, block):
    width, queries = attended.shape
    return pl.pallas_call(
        finish_kernel,
        grid_spec=pltpu.PrefetchScalarGridSpec(
            num_scalar_prefetch=1,
            grid=(queries // block,),
            in_specs=[
                pl.BlockSpec((width, block), lambda i, place: (0, i)),
                pl.BlockSpec((block, width), lambda i, place: (place[0] + (i ^ place[1]), 0)),
                pl.BlockSpec((block, width), lambda i, place: (i, 0)),
                pl.BlockSpec((width, width), lambda i, place: (0, 0)),
            ],
            out_specs=pl.BlockSpec((block, width), lambda i, place: (i, 0)),
        ),
        out_shape=jax.ShapeDtypeStruct((queries, width), BF16),
        compiler_params=pltpu.CompilerParams(vmem_limit_bytes=VMEM_LIMIT),
        name="finish",
    )(place, attended, tok, gate, w_out)


def swap(x, axis, bits):
    return lax.ppermute(x, axis, [(i, i ^ bits) for i in range(lax.axis_size(axis))])


def spread_table(own):
    size = lax.axis_size("region")
    bits = [1 << n for n in range(1, size.bit_length() - 1)]
    blocks = {0: own}
    for bit in bits[2:]:
        blocks.update({o ^ bit: swap(b, "region", bit) for o, b in list(blocks.items())})
    if len(bits) >= 2:
        first, second = bits[:2]
        half = own.shape[0] // 2
        for o, b in list(blocks.items()):
            one, two = swap(b, "region", first), swap(b, "region", second)
            low = swap(two[:half], "region", first)
            high = swap(one[half:], "region", second)
            blocks[o ^ first], blocks[o ^ second] = one, two
            blocks[o ^ first ^ second] = jnp.concatenate([low, high], axis=0)
    elif bits:
        blocks.update({o ^ bits[0]: swap(b, "region", bits[0]) for o, b in list(blocks.items())})
    blocks.update({o ^ 1: swap(b, "region", 1) for o, b in list(blocks.items())})
    return [blocks[o] for o in range(size)]


def per_device(
    tokens, element_ids, element_slot, live_count, cond_table, w_ada, b_ada, w_qkv, w_out
):
    device_tokens = tokens[0]
    tok_rows, width = device_tokens.shape
    elem_rows = cond_table.shape[0]
    n = lax.axis_size("ctx")
    h = n // 2
    block = tok_rows // 2
    r, c = lax.axis_index("region"), lax.axis_index("ctx")
    core, upper = r % 2, (c >= h).astype(jnp.int32)
    m = jnp.where(upper == 1, n - 1 - c, c)

    slot = element_slot[element_ids[0]]
    position = jnp.arange(tok_rows, dtype=jnp.int32)
    slot = jnp.where(position < live_count[0, 0], slot, -1)
    slots = jnp.stack([slot] + [swap(slot, "ctx", d) for d in range(1, n)])
    slots = jnp.where(core == upper, slots, swap(slots, "region", 1))
    slots = lax.dynamic_slice_in_dim(slots, core * block, block, axis=1)
    shard = jnp.arange(n, dtype=jnp.int32)
    shard = jnp.where(shard < h, shard ^ m, shard)
    shard_ctx = jnp.where(upper == 1, n - 1 - shard, shard)
    slots = jnp.take(slots, shard_ctx ^ c, axis=0).reshape(n * block, 1)
    owner = slots // elem_rows
    relative = ((((owner // n) ^ r) * n) + ((owner % n) ^ c)) * elem_rows + slots % elem_rows
    relative = jnp.where(slots < 0, -1, relative)

    mine = lax.dynamic_slice_in_dim(device_tokens, core * block, block)
    other = lax.dynamic_slice_in_dim(device_tokens, (1 - core) * block, block)
    got = swap(other, "region", 1)
    even, odd = jnp.where(core == 0, mine, got), jnp.where(core == 0, got, mine)
    work, pass_on = jnp.where(upper == 0, even, odd), jnp.where(upper == 0, odd, even)
    arrived = [work] + [swap(work, "ctx", d) for d in range(1, h)]
    for j in range(h):
        piece = lax.ppermute(pass_on, "ctx", [(h + j, h - 1), (h - 1 - j, h)])
        held = piece
        for k in range(h - 1, 0, -1):
            piece = lax.ppermute(piece, "ctx", [(k, k - 1), (n - 1 - k, n - k)])
            held = jnp.where(m == k - 1, piece, held)
        arrived.append(held)
    tok = jnp.concatenate(arrived, axis=0)

    picked = jnp.zeros((n * block, width), BF16)
    near = spread_table(cond_table)
    far = spread_table(
        jnp.concatenate([swap(cond_table, "ctx", d) for d in range(1, n)], axis=0)
    )
    size = lax.axis_size("region")
    near_bases = [o * n * elem_rows for o in range(size)]
    picked = pick_rows(relative, picked, near, near_bases, block)
    step = len(far) if n == 4 else 4
    for lo in range(0, len(far), step):
        far_bases = [(o * n + 1) * elem_rows for o in range(lo, lo + step)]
        picked = pick_rows(relative, picked, far[lo : lo + step], far_bases, block)

    base = jnp.where(2 * m < h, (2 * m) ^ m, 2 * m) & ~1
    flip = jnp.where(2 * m < h, m & 1, 0)
    place = jnp.stack([base, flip]).astype(jnp.int32)
    kv, qt, gate = project(place, tok, picked, w_ada, b_ada.reshape(1, -1), w_qkv.T, block)
    attended = attend(qt, kv, swap(kv, "region", 1))
    result = finish(place, attended, tok, gate, w_out, block)

    home = []
    for i in range(2):
        pairs = [(k, 2 * k + i) for k in range(h)]
        pairs += [(n - 1 - a, n - 1 - b) for a, b in pairs]
        home.append(lax.ppermute(result[i * block : (i + 1) * block], "ctx", pairs))
    parity = c % 2
    even = jnp.where(parity == 0, home[0], home[1])
    odd = jnp.where(parity == 0, home[1], home[0])
    mine = jnp.where(core == 0, even, odd)
    got = swap(jnp.where(core == 0, odd, even), "region", 1)
    low, high = jnp.where(core == 0, mine, got), jnp.where(core == 0, got, mine)
    return jnp.concatenate([low, high], axis=0)[None]


def solution(mesh):
    placed = (
        P("region", "ctx", None),
        P("region", "ctx"),
        P(),
        P("region", "ctx"),
        P(("region", "ctx"), None),
        P(),
        P(),
        P(),
        P(),
    )
    return jax.shard_map(
        per_device, mesh=mesh, in_specs=placed, out_specs=P("region", "ctx", None), check_vma=False
    )
```

time: 446 us -> 250 us (0.56); the launches traced: 441 us -> 249 us
  matrix products: 107 us -> 0 us
  waiting for transfers between devices: 180 us -> 100 us
  Pallas kernels: 0 us -> 78.1 us
  local copies, waits for them, and re-layouts: 81 us -> 27.7 us
  other arithmetic: 41.5 us -> 6.77 us
  starting transfers between devices: 6.14 us -> 35.6 us
  between operations: 14.2 us -> 1.18 us
  blocking collectives: 10.7 us -> 0 us
    all_gather x2 -> x0, waiting for transfers between devices: 143 us -> none  [the longest x1 84.1 us: per_device(): keys_piece = lax.all_gather(keys_here, 'ctx', axis=0, tiled=True)]
    dot_general x11 -> x0, matrix products: 107 us -> none  [the longest x4 43.5 us: advance(): jnp.einsum('hqk,khe->hqe', expo.astype(jnp.bfloat16), value_block, prefer...]
    ppermute x0 -> x33, waiting for transfers between devices: none -> 100 us  [the longest x27 41.3 us: swap(): lax.ppermute(x, axis, [(i, i ^ bits) for i in range(lax.axis_size(axis))])]
    pallas_call x0 -> x5, Pallas kernels: none -> 78.1 us  [the longest x1 25.8 us: project(): pl.pallas_call(functools.partial(project_kernel, query_scale), grid_spec=...]
    reduce_sum x7 -> x0, other arithmetic: 37.7 us -> none  [the longest x4 34.2 us: advance(): denominator = denominator * shrink + jnp.sum(expo, axis=2)]
    all_to_all x1 -> x0, waiting for transfers between devices: 36.9 us -> none  [per_device(): lax.all_to_all(served, ('region', 'ctx'), split_axis=0, concat_axis=0, ti...]
    ppermute x0 -> x33, starting transfers between devices: none -> 35.6 us  [the longest x27 24.1 us: swap(): lax.ppermute(x, axis, [(i, i ^ bits) for i in range(lax.axis_size(axis))])]
    reshape x3 -> x1, local copies, waits for them, and re-layouts: 34.9 us -> 0.6 us  [per_device(): b_ada.reshape(1, -1)]
  transfers between devices with their start and end apart: 3 -> 33, of which waited for: 3 -> 9; matrix products, arithmetic and copies ran while one was open for 8% -> 9% of each run, Pallas kernels for 0% -> 3%
where the time goes in v1:
time: 250 us; the launch traced here: 249 us
  waiting for transfers between devices  100 us (40%)
  Pallas kernels  78.1 us (31%)
  starting transfers between devices  35.6 us (14%)
  local copies, waits for them, and re-layouts  27.7 us (11%)
  other arithmetic  6.77 us (3%)
    ppermute x27, waiting for transfers between devices, swap(): lax.ppermute(x, axis, [(i, i ^ bits) for i in range(lax.axis_size(axis))])  41.3 us
    pallas_call x1, Pallas kernels, project(): pl.pallas_call(functools.partial(project_kernel, query_scale), grid_spec=...  25.8 us
    pallas_call x1, Pallas kernels, attend(): pl.pallas_call(functools.partial(attend_kernel, head_dim, chunk), grid=(p...  25.3 us
    ppermute x2, waiting for transfers between devices, per_device(): home.append(lax.ppermute(result[i * block:(i + 1) * block], 'ctx', pairs))  24.1 us
    ppermute x27, starting transfers between devices, swap(): lax.ppermute(x, axis, [(i, i ^ bits) for i in range(lax.axis_size(axis))])  24.1 us
    ppermute x2, waiting for transfers between devices, per_device(): piece = lax.ppermute(piece, 'ctx', [(k, k - 1), (n - 1 - k, n - k)])  22.8 us
    pallas_call x2, Pallas kernels, pick_rows(): pl.pallas_call(functools.partial(pick_kernel, bases, count), grid=(count...  20.9 us
    unnamed x43, local copies, waits for them, and re-layouts  18.5 us
  transfers between devices with their start and end apart: 33, of which 9 were waited for; matrix products, arithmetic and copies ran while one was open for 9% of the time, Pallas kernels for 3%

profile of v1, /device:TPU:17, one launch (start us, length us, event | category | flops | bytes accessed | tf_op | source)
XLA Modules:
  0.0 249.3 jit_solution(14080933873930030490)
XLA Ops:
  1.5 3.1 %gather_fusion = s32[512]{0:T(512)S(1)} fusion(s32[4096]{0:T(1024)S(1)} %copy-done, s32[1024]{0:T(1024)S(1)} %pad_clamp_fusion.1), kind=kCustom, calls=%fused_computation | custom fusion | bytes 6144 | tf_op jit(solution)/shard_map/gather | solution.py:245
  4.9 3.2 %collective-permute-start.7 = (s32[512]{0:T(512)S(1)}, s32[512]{0:T(512)S(1)}, u32[]{:S(2)}, u32[]{:S(2)}) collective-permute-start(s32[512]{0:T(512)S(1)} %fusion.14), channel_id=1, source_target_pairs={{0,2},{1,3},{2,0},{3,1},{4,6},{5,7},{6,4},{7,5},{8,10},{9,11},{10,... | collective-permute-start | bytes 6152 | tf_op jit(solution)/shard_map/ppermute | solution.py:208
  8.1 1.5 collective-permute-start.18
  9.5 1.2 collective-permute-start.13
  10.9 1.3 collective-permute-start.11
  12.2 2.4 collective-permute-start.9
  15.9 11.5 %copy.17 = bf16[1152,3456]{0,1:T(8,128)(2,1)} copy(bf16[1152,3456]{1,0:T(8,128)(2,1)} %param.16) | data formatting | bytes 15925248 | tf_op args[7]
  27.4 2.1 collective-permute-start.19
  30.8 0.7 constant_dynamic-update-slice_fusion.4
  31.5 11.1 %collective-permute-done.19 = bf16[128,1152]{1,0:T(8,128)(2,1)S(1)} collective-permute-done((bf16[128,1152]{1,0:T(8,128)(2,1)}, bf16[128,1152]{1,0:T(8,128)(2,1)S(1)}, u32[]{:S(2)}, u32[]{:S(2)}) %collective-permute-start.19) | collective-permute-done | bytes 294944 | tf_op jit(solution)/shard_map/ppermute | solution.py:208
  42.6 0.8 collective-permute-start.10
  44.1 0.7 constant_dynamic-update-slice_fusion.2.refs_0_
  45.6 1.3 collective-permute-start.15
  46.9 0.9 slice.29
  47.8 1.1 collective-permute-start.16
  49.2 20.5 %collective-permute-done.15 = bf16[64,1152]{1,0:T(8,128)(2,1)S(1)} collective-permute-done((bf16[64,1152]{1,0:T(8,128)(2,1)S(1)}, bf16[64,1152]{1,0:T(8,128)(2,1)S(1)}, u32[]{:S(2)}, u32[]{:S(2)}) %collective-permute-start.15) | collective-permute-done | bytes 147488 | tf_op jit(solution)/shard_map/ppermute | solution.py:208
  69.6 1.1 collective-permute-start.14
  70.7 1.3 collective-permute-start.4
  73.1 1.9 collective-permute-start.2
  75.7 1.8 fusion.5.idx_ref
  77.6 1.0 collective-permute-start.21
  78.6 0.9 collective-permute-start.27
  79.5 9.1 %collective-permute-done.4 = bf16[256,1152]{1,0:T(8,128)(2,1)S(1)} collective-permute-done((bf16[256,1152]{1,0:T(8,128)(2,1)S(1)}, bf16[256,1152]{1,0:T(8,128)(2,1)S(1)}, u32[]{:S(2)}, u32[]{:S(2)}) %collective-permute-start.4) | collective-permute-done | bytes 589856 | tf_op jit(solution)/shard_map/ppermute | solution.py:266
  88.6 1.3 collective-permute-start.5
  89.9 1.6 broadcast_in_dim.32.acc_ref
  91.5 7.1 %pick.2.acc_ref = bf16[1024,1152]{1,0:T(8,128)(2,1)} custom-call(s32[1024,1]{1,0:T(8,128)} %fusion.5.idx_ref, bf16[1024,1152]{1,0:T(8,128)(2,1)} %broadcast_in_dim.32.acc_ref, bf16[128,1152]{1,0:T(8,128)(2,1)} %refs_0_.1, bf16[128,1152]{1,0:T(8,128)(2,1)} %copy-done.14, ...), custom_call_target="tpu_custom_call", output_to_operand_aliasing={{}: (1, {})} | custom-call | flops 2415919104 | bytes 7077888 | tf_op jit(solution)/shard_map/pick/pallas_call | solution.py:42
  98.8 2.6 %collective-permute-done.2 = bf16[256,1152]{1,0:T(8,128)(2,1)S(1)} collective-permute-done((bf16[256,1152]{1,0:T(8,128)(2,1)S(1)}, bf16[256,1152]{1,0:T(8,128)(2,1)S(1)}, u32[]{:S(2)}, u32[]{:S(2)}) %collective-permute-start.2) | collective-permute-done | bytes 589856 | tf_op jit(solution)/shard_map/ppermute | solution.py:266
  101.9 1.6 collective-permute-start.3
  104.5 22.8 %collective-permute-done.3 = bf16[256,1152]{1,0:T(8,128)(2,1)S(1)} collective-permute-done((bf16[256,1152]{1,0:T(8,128)(2,1)S(1)}, bf16[256,1152]{1,0:T(8,128)(2,1)S(1)}, u32[]{:S(2)}, u32[]{:S(2)}) %collective-permute-start.3) | collective-permute-done | bytes 589856 | tf_op jit(solution)/shard_map/ppermute | solution.py:269
  127.3 1.4 collective-permute-start.28
  128.7 1.7 pad_maximum_fusion.tok_ref
  130.5 0.9 copy-done.11
  131.4 0.9 copy-done.12
  132.3 0.9 copy-done.13
  133.3 13.7 %pick.3.act_ref = bf16[1024,1152]{1,0:T(8,128)(2,1)} custom-call(s32[1024,1]{1,0:T(8,128)} %fusion.5.idx_ref, bf16[1024,1152]{1,0:T(8,128)(2,1)} %pick.2.acc_ref, bf16[384,1152]{1,0:T(8,128)(2,1)} %constant_dynamic-update-slice_fusion.2.refs_0_, bf16[384,1152]{1,0:T(8,128)(2,1)} %collective-permute-done.21.refs_1_, ...), custom_call_target="tpu_custom_call", output_to_operand_aliasing={{}: (1, {})} | custom-call | flops 7247757312 | bytes 11796480 | tf_op jit(solution)/shard_map/pick/pallas_call | solution.py:42
  147.0 25.8 %project.1 = (bf16[2304,1024]{1,0:T(8,128)(2,1)}, bf16[1152,512]{1,0:T(8,128)(2,1)}, bf16[512,1152]{1,0:T(8,128)(2,1)}) custom-call(s32[2]{0:T(128)} %pad_add_fusion.1.place_ref, bf16[1024,1152]{1,0:T(8,128)(2,1)} %pad_maximum_fusion.tok_ref, bf16[1024,1152]{1,0:T(8,128)(2,1)} %pick.3.act_ref, bf16[1152,3456]{1,0:T(8,128)(2,1)} %wada_ref.1, ...), custom_call_target="tpu_custom_call" | custom-call | tf_op jit(solution)/shard_map/project/pallas_call | solution.py:106
  172.7 8.1 %collective-permute-done.29.kb_ref.vb_ref = bf16[2304,1024]{1,0:T(8,128)(2,1)S(1)} collective-permute-done((bf16[2304,1024]{1,0:T(8,128)(2,1)}, bf16[2304,1024]{1,0:T(8,128)(2,1)S(1)}, u32[]{:S(2)}, u32[]{:S(2)}) %collective-permute-start.29) | collective-permute-done | bytes 4718624 | tf_op jit(solution)/shard_map/ppermute | solution.py:208
  180.9 2.2 copy-done.2
  183.0 25.3 %attend.1.att_ref = bf16[1152,512]{1,0:T(8,128)(2,1)} custom-call(bf16[1152,512]{1,0:T(8,128)(2,1)} %get-tuple-element.8.q_ref, bf16[2304,1024]{1,0:T(8,128)(2,1)} %get-tuple-element.9.ka_ref.va_ref, bf16[2304,1024]{1,0:T(8,128)(2,1)} %copy-done.2, bf16[2304,1024]{1,0:T(8,128)(2,1)} %get-tuple-element.9.ka_ref.va_ref, bf16[2304,1024]{1,0:T(8,128)(2,1)} %copy-done.2), custom_call_target="tpu_custom_call" | custom-call | tf_op jit(solution)/shard_map/attend/pallas_call | solution.py:169
  208.3 6.1 %finish.1 = bf16[512,1152]{1,0:T(8,128)(2,1)} custom-call(s32[2]{0:T(128)} %pad_add_fusion.1.place_ref, bf16[1152,512]{1,0:T(8,128)(2,1)} %attend.1.att_ref, bf16[1024,1152]{1,0:T(8,128)(2,1)} %pad_maximum_fusion.tok_ref, bf16[512,1152]{1,0:T(8,128)(2,1)} %get-tuple-element.10.gate_ref, bf16[1152,1152]{1,0:T(8,128)(2,1)} %w_ref.1), custom_call_target="tpu_custom_call" | custom-call | tf_op jit(solution)/shard_map/finish/pallas_call | solution.py:188
  214.5 1.3 fusion.18
  215.8 2.1 collective-permute-start.31
  217.9 3.3 %collective-permute-start.30 = (bf16[256,1152]{1,0:T(8,128)(2,1)S(1)}, bf16[256,1152]{1,0:T(8,128)(2,1)S(1)}, u32[]{:S(2)}, u32[]{:S(2)}) collective-permute-start(bf16[256,1152]{1,0:T(8,128)(2,1)S(1)} %get-tuple-element.19), channel_id=1, source_target_pairs={{0,0},{1,2},{3,3},{2,1},{4,4},{5,6},{7,7},{6,5},{8,8},{9,10},{11,1... | collective-permute-start | bytes 1769480 | tf_op jit(solution)/shard_map/ppermute | solution.py:298
  221.2 10.5 %collective-permute-done.31 = bf16[256,1152]{1,0:T(8,128)(2,1)S(1)} collective-permute-done((bf16[256,1152]{1,0:T(8,128)(2,1)S(1)}, bf16[256,1152]{1,0:T(8,128)(2,1)S(1)}, u32[]{:S(2)}, u32[]{:S(2)}) %collective-permute-start.31) | collective-permute-done | bytes 589856 | tf_op jit(solution)/shard_map/ppermute | solution.py:298
  231.7 13.7 %collective-permute-done.30 = bf16[256,1152]{1,0:T(8,128)(2,1)S(1)} collective-permute-done((bf16[256,1152]{1,0:T(8,128)(2,1)S(1)}, bf16[256,1152]{1,0:T(8,128)(2,1)S(1)}, u32[]{:S(2)}, u32[]{:S(2)}) %collective-permute-start.30) | collective-permute-done | bytes 589856 | tf_op jit(solution)/shard_map/ppermute | solution.py:298
  245.5 0.9 collective-permute-start.32
  246.4 1.6 collective-permute-done.32
  248.2 1.1 maximum_bitcast_fusion
  (98 shorter events, 8.9 us)
Async XLA Ops:
  0.0 1.5 copy-start
  0.0 10.8 %copy-start.3 = (bf16[1,512,1152]{2,1,0:T(8,128)(2,1)S(1)}, bf16[1,512,1152]{2,1,0:T(8,128)(2,1)}, u32[]{:S(2)}) copy-start(bf16[1,512,1152]{2,1,0:T(8,128)(2,1)} %param.9) | copy-start | bytes 3538948
  0.0 15.3 %copy-start.10 = (f32[3456]{0:T(1024)S(1)}, f32[3456]{0:T(1024)}, u32[]{:S(2)}) copy-start(f32[3456]{0:T(1024)} %param.15) | copy-start | bytes 41476
  4.6 6.3 %collective-permute-start.8 = (s32[512]{0:T(512)S(1)}, s32[512]{0:T(512)S(1)}, u32[]{:S(2)}, u32[]{:S(2)}) collective-permute-start(s32[512]{0:T(512)S(1)} %fusion.14), channel_id=1, source_target_pairs={{0,3},{1,2},{2,1},{3,0},{4,7},{5,6},{6,5},{7,4},{8,11},{9,10},{10,... | collective-permute-start | bytes 6152 | tf_op jit(solution)/shard_map/ppermute | solution.py:208
  4.9 7.3 %collective-permute-start.7 = (s32[512]{0:T(512)S(1)}, s32[512]{0:T(512)S(1)}, u32[]{:S(2)}, u32[]{:S(2)}) collective-permute-start(s32[512]{0:T(512)S(1)} %fusion.14), channel_id=1, source_target_pairs={{0,2},{1,3},{2,0},{3,1},{4,6},{5,7},{6,4},{7,5},{8,10},{9,11},{10,... | collective-permute-start | bytes 6152 | tf_op jit(solution)/shard_map/ppermute | solution.py:208
  8.1 4.1 %collective-permute-start.6 = (s32[512]{0:T(512)S(1)}, s32[512]{0:T(512)S(1)}, u32[]{:S(2)}, u32[]{:S(2)}) collective-permute-start(s32[512]{0:T(512)S(1)} %fusion.14), channel_id=1, source_target_pairs={{0,1},{1,0},{2,3},{3,2},{4,5},{5,4},{6,7},{7,6},{8,9},{9,8},{10,11... | collective-permute-start | bytes 6152 | tf_op jit(solution)/shard_map/ppermute | solution.py:208
  8.1 22.3 %collective-permute-start.18 = (bf16[128,1152]{1,0:T(8,128)(2,1)}, bf16[128,1152]{1,0:T(8,128)(2,1)S(1)}, u32[]{:S(2)}, u32[]{:S(2)}) collective-permute-start(bf16[128,1152]{1,0:T(8,128)(2,1)} %refs_0_.1), channel_id=1, source_target_pairs={{0,1},{1,0},{2,3},{3,2},{4,5},{5,4},{6,7},{7,6},{8,9},{9,8},{10,11... | collective-permute-start | bytes 884744 | tf_op jit(solution)/shard_map/ppermute | solution.py:208
  9.5 35.8 %collective-permute-start.13 = (bf16[128,1152]{1,0:T(8,128)(2,1)}, bf16[128,1152]{1,0:T(8,128)(2,1)S(1)}, u32[]{:S(2)}, u32[]{:S(2)}) collective-permute-start(bf16[128,1152]{1,0:T(8,128)(2,1)} %refs_0_.1), channel_id=1, source_target_pairs={{0,16},{4,20},{8,24},{12,28},{16,0},{20,4},{24,8},{28,12},{1,17},{... | collective-permute-start | bytes 884744 | tf_op jit(solution)/shard_map/ppermute | solution.py:208
  10.9 34.7 %collective-permute-start.11 = (bf16[128,1152]{1,0:T(8,128)(2,1)}, bf16[128,1152]{1,0:T(8,128)(2,1)}, u32[]{:S(2)}, u32[]{:S(2)}) collective-permute-start(bf16[128,1152]{1,0:T(8,128)(2,1)} %refs_0_.1), channel_id=1, source_target_pairs={{0,8},{4,12},{8,0},{12,4},{16,24},{20,28},{24,16},{28,20},{1,9},{5... | collective-permute-start | bytes 884744 | tf_op jit(solution)/shard_map/ppermute | solution.py:208
  12.2 31.9 %collective-permute-start.20 = (bf16[128,1152]{1,0:T(8,128)(2,1)}, bf16[128,1152]{1,0:T(8,128)(2,1)S(1)}, u32[]{:S(2)}, u32[]{:S(2)}) collective-permute-start(bf16[128,1152]{1,0:T(8,128)(2,1)} %refs_0_.1), channel_id=1, source_target_pairs={{0,3},{1,2},{2,1},{3,0},{4,7},{5,6},{6,5},{7,4},{8,11},{9,10},{10,... | collective-permute-start | bytes 884744 | tf_op jit(solution)/shard_map/ppermute | solution.py:208
  12.2 15.2 %collective-permute-start.9 = (s32[4,512]{1,0:T(4,128)S(1)}, s32[4,512]{1,0:T(4,128)S(1)}, u32[]{:S(2)}, u32[]{:S(2)}) collective-permute-start(s32[4,512]{1,0:T(4,128)S(1)} %pad_add_fusion), channel_id=1, source_target_pairs={{0,4},{4,0},{8,12},{12,8},{16,20},{20,16},{24,28},{28,24},{1,5},{5... | collective-permute-start | bytes 24584 | tf_op jit(solution)/shard_map/ppermute | solution.py:208
  27.4 15.2 %collective-permute-start.19 = (bf16[128,1152]{1,0:T(8,128)(2,1)}, bf16[128,1152]{1,0:T(8,128)(2,1)S(1)}, u32[]{:S(2)}, u32[]{:S(2)}) collective-permute-start(bf16[128,1152]{1,0:T(8,128)(2,1)} %refs_0_.1), channel_id=1, source_target_pairs={{0,2},{1,3},{2,0},{3,1},{4,6},{5,7},{6,4},{7,5},{8,10},{9,11},{10,... | collective-permute-start | bytes 884744 | tf_op jit(solution)/shard_map/ppermute | solution.py:208
  30.4 17.4 %collective-permute-start = (bf16[256,1152]{1,0:T(8,128)(2,1)S(1)}, bf16[256,1152]{1,0:T(8,128)(2,1)S(1)}, u32[]{:S(2)}, u32[]{:S(2)}) collective-permute-start(bf16[256,1152]{1,0:T(8,128)(2,1)S(1)} %dynamic-slice_bitcast_fusion), channel_id=1, source_target_pairs={{0,4},{4,0},{8,12},{12,8},{16,20},{20,16},{24,28},{28,24},{1,5},{5... | collective-permute-start | bytes 1769480 | tf_op jit(solution)/shard_map/ppermute | solution.py:208
  42.6 29.7 %collective-permute-start.10 = (bf16[128,1152]{1,0:T(8,128)(2,1)}, bf16[128,1152]{1,0:T(8,128)(2,1)S(1)}, u32[]{:S(2)}, u32[]{:S(2)}) collective-permute-start(bf16[128,1152]{1,0:T(8,128)(2,1)} %refs_0_.1), channel_id=1, source_target_pairs={{0,4},{4,0},{8,12},{12,8},{16,20},{20,16},{24,28},{28,24},{1,5},{5... | collective-permute-start | bytes 884744 | tf_op jit(solution)/shard_map/ppermute | solution.py:208
  44.8 27.3 %collective-permute-start.24 = (bf16[384,1152]{1,0:T(8,128)(2,1)}, bf16[384,1152]{1,0:T(8,128)(2,1)S(1)}, u32[]{:S(2)}, u32[]{:S(2)}) collective-permute-start(bf16[384,1152]{1,0:T(8,128)(2,1)} %constant_dynamic-update-slice_fusion.2.refs_0_), channel_id=1, source_target_pairs={{0,16},{4,20},{8,24},{12,28},{16,0},{20,4},{24,8},{28,12},{1,17},{... | collective-permute-start | bytes 2654216 | tf_op jit(solution)/shard_map/ppermute | solution.py:208
  45.3 32.2 %copy-start.8 = (bf16[128,1152]{1,0:T(8,128)(2,1)}, bf16[128,1152]{1,0:T(8,128)(2,1)S(1)}, u32[]{:S(2)}) copy-start(bf16[128,1152]{1,0:T(8,128)(2,1)S(1)} %collective-permute-done.13.refs_4_) | copy-start | bytes 884740
  45.3 29.7 %collective-permute-start.22 = (bf16[384,1152]{1,0:T(8,128)(2,1)}, bf16[384,1152]{1,0:T(8,128)(2,1)S(1)}, u32[]{:S(2)}, u32[]{:S(2)}) collective-permute-start(bf16[384,1152]{1,0:T(8,128)(2,1)} %constant_dynamic-update-slice_fusion.2.refs_0_), channel_id=1, source_target_pairs={{0,8},{4,12},{8,0},{12,4},{16,24},{20,28},{24,16},{28,20},{1,9},{5... | collective-permute-start | bytes 2654216 | tf_op jit(solution)/shard_map/ppermute | solution.py:208
  45.6 24.1 %collective-permute-start.15 = (bf16[64,1152]{1,0:T(8,128)(2,1)S(1)}, bf16[64,1152]{1,0:T(8,128)(2,1)S(1)}, u32[]{:S(2)}, u32[]{:S(2)}) collective-permute-start(bf16[64,1152]{1,0:T(8,128)(2,1)S(1)} %slice.28), channel_id=1, source_target_pairs={{0,8},{4,12},{8,0},{12,4},{16,24},{20,28},{24,16},{28,20},{1,9},{5... | collective-permute-start | bytes 442376 | tf_op jit(solution)/shard_map/ppermute | solution.py:208
  47.8 22.9 %collective-permute-start.16 = (bf16[64,1152]{1,0:T(8,128)(2,1)S(1)}, bf16[64,1152]{1,0:T(8,128)(2,1)S(1)}, u32[]{:S(2)}, u32[]{:S(2)}) collective-permute-start(bf16[64,1152]{1,0:T(8,128)(2,1)S(1)} %slice.29), channel_id=1, source_target_pairs={{0,16},{4,20},{8,24},{12,28},{16,0},{20,4},{24,8},{28,12},{1,17},{... | collective-permute-start | bytes 442376 | tf_op jit(solution)/shard_map/ppermute | solution.py:208
  69.6 3.5 %collective-permute-start.14 = (bf16[128,1152]{1,0:T(8,128)(2,1)S(1)}, bf16[128,1152]{1,0:T(8,128)(2,1)S(1)}, u32[]{:S(2)}, u32[]{:S(2)}) collective-permute-start(bf16[128,1152]{1,0:T(8,128)(2,1)S(1)} %collective-permute-done.13.refs_4_), channel_id=1, source_target_pairs={{0,4},{4,0},{8,12},{12,8},{16,20},{20,16},{24,28},{28,24},{1,5},{5... | collective-permute-start | bytes 884744 | tf_op jit(solution)/shard_map/ppermute | solution.py:208
  70.7 17.8 %collective-permute-start.4 = (bf16[256,1152]{1,0:T(8,128)(2,1)S(1)}, bf16[256,1152]{1,0:T(8,128)(2,1)S(1)}, u32[]{:S(2)}, u32[]{:S(2)}) collective-permute-start(bf16[256,1152]{1,0:T(8,128)(2,1)S(1)} %get-tuple-element.17), channel_id=1, source_target_pairs={{3,1},{0,2},{7,5},{4,6},{11,9},{8,10},{15,13},{12,14},{19,17},{16,... | collective-permute-start | bytes 1769480 | tf_op jit(solution)/shard_map/ppermute | solution.py:266
  72.1 19.4 %copy-start.9 = (bf16[128,1152]{1,0:T(8,128)(2,1)}, bf16[128,1152]{1,0:T(8,128)(2,1)S(1)}, u32[]{:S(2)}) copy-start(bf16[128,1152]{1,0:T(8,128)(2,1)S(1)} %constant_dynamic-update-slice_fusion.refs_6_) | copy-start | bytes 884740
  72.1 29.4 %copy-start.4 = (bf16[384,1152]{1,0:T(8,128)(2,1)}, bf16[384,1152]{1,0:T(8,128)(2,1)S(1)}, u32[]{:S(2)}) copy-start(bf16[384,1152]{1,0:T(8,128)(2,1)S(1)} %collective-permute-done.24.refs_4_) | copy-start | bytes 2654212
  72.1 5.5 %collective-permute-start.12 = (bf16[128,1152]{1,0:T(8,128)(2,1)}, bf16[128,1152]{1,0:T(8,128)(2,1)S(1)}, u32[]{:S(2)}, u32[]{:S(2)}) collective-permute-start(bf16[128,1152]{1,0:T(8,128)(2,1)} %collective-permute-done.11.refs_2_), channel_id=1, source_target_pairs={{0,4},{4,0},{8,12},{12,8},{16,20},{20,16},{24,28},{28,24},{1,5},{5... | collective-permute-start | bytes 884744 | tf_op jit(solution)/shard_map/ppermute | solution.py:208
  72.2 6.3 %collective-permute-start.17 = (bf16[128,1152]{1,0:T(8,128)(2,1)S(1)}, bf16[128,1152]{1,0:T(8,128)(2,1)S(1)}, u32[]{:S(2)}, u32[]{:S(2)}) collective-permute-start(bf16[128,1152]{1,0:T(8,128)(2,1)S(1)} %constant_dynamic-update-slice_fusion.refs_6_), channel_id=1, source_target_pairs={{0,4},{4,0},{8,12},{12,8},{16,20},{20,16},{24,28},{28,24},{1,5},{5... | collective-permute-start | bytes 884744 | tf_op jit(solution)/shard_map/ppermute | solution.py:208
  73.1 18.4 %copy-start.15 = (bf16[128,1152]{1,0:T(8,128)(2,1)}, bf16[128,1152]{1,0:T(8,128)(2,1)S(1)}, u32[]{:S(2)}) copy-start(bf16[128,1152]{1,0:T(8,128)(2,1)S(1)} %collective-permute-done.14.refs_5_) | copy-start | bytes 884740
  73.1 28.4 %collective-permute-start.2 = (bf16[256,1152]{1,0:T(8,128)(2,1)S(1)}, bf16[256,1152]{1,0:T(8,128)(2,1)S(1)}, u32[]{:S(2)}, u32[]{:S(2)}) collective-permute-start(bf16[256,1152]{1,0:T(8,128)(2,1)S(1)} %get-tuple-element.17), channel_id=1, source_target_pairs={{2,1},{1,2},{6,5},{5,6},{10,9},{9,10},{14,13},{13,14},{18,17},{17,... | collective-permute-start | bytes 1769480 | tf_op jit(solution)/shard_map/ppermute | solution.py:266
  75.0 13.5 %copy-start.5 = (bf16[384,1152]{1,0:T(8,128)(2,1)}, bf16[384,1152]{1,0:T(8,128)(2,1)S(1)}, u32[]{:S(2)}) copy-start(bf16[384,1152]{1,0:T(8,128)(2,1)S(1)} %collective-permute-done.22.refs_2_) | copy-start | bytes 2654212
  75.0 23.6 %collective-permute-start.26 = (bf16[192,1152]{1,0:T(8,128)(2,1)S(1)}, bf16[192,1152]{1,0:T(8,128)(2,1)S(1)}, u32[]{:S(2)}, u32[]{:S(2)}) collective-permute-start(bf16[192,1152]{1,0:T(8,128)(2,1)S(1)} %slice.30), channel_id=1, source_target_pairs={{0,8},{4,12},{8,0},{12,4},{16,24},{20,28},{24,16},{28,20},{1,9},{5... | collective-permute-start | bytes 1327112 | tf_op jit(solution)/shard_map/ppermute | solution.py:208
  77.6 13.9 %copy-start.16 = (bf16[128,1152]{1,0:T(8,128)(2,1)}, bf16[128,1152]{1,0:T(8,128)(2,1)S(1)}, u32[]{:S(2)}) copy-start(bf16[128,1152]{1,0:T(8,128)(2,1)S(1)} %collective-permute-done.12.refs_3_) | copy-start | bytes 884740
  77.6 52.8 %collective-permute-start.21 = (bf16[384,1152]{1,0:T(8,128)(2,1)}, bf16[384,1152]{1,0:T(8,128)(2,1)}, u32[]{:S(2)}, u32[]{:S(2)}) collective-permute-start(bf16[384,1152]{1,0:T(8,128)(2,1)} %constant_dynamic-update-slice_fusion.2.refs_0_), channel_id=1, source_target_pairs={{0,4},{4,0},{8,12},{12,8},{16,20},{20,16},{24,28},{28,24},{1,5},{5... | collective-permute-start | bytes 2654216 | tf_op jit(solution)/shard_map/ppermute | solution.py:208
  78.6 13.0 %copy-start.17 = (bf16[128,1152]{1,0:T(8,128)(2,1)}, bf16[128,1152]{1,0:T(8,128)(2,1)S(1)}, u32[]{:S(2)}) copy-start(bf16[128,1152]{1,0:T(8,128)(2,1)S(1)} %collective-permute-done.17.refs_7_) | copy-start | bytes 884740
  78.6 23.4 %collective-permute-start.27 = (bf16[192,1152]{1,0:T(8,128)(2,1)S(1)}, bf16[192,1152]{1,0:T(8,128)(2,1)S(1)}, u32[]{:S(2)}, u32[]{:S(2)}) collective-permute-start(bf16[192,1152]{1,0:T(8,128)(2,1)S(1)} %slice.31), channel_id=1, source_target_pairs={{0,16},{4,20},{8,24},{12,28},{16,0},{20,4},{24,8},{28,12},{1,17},{... | collective-permute-start | bytes 1327112 | tf_op jit(solution)/shard_map/ppermute | solution.py:208
  88.6 15.1 %collective-permute-start.5 = (bf16[256,1152]{1,0:T(8,128)(2,1)S(1)}, bf16[256,1152]{1,0:T(8,128)(2,1)S(1)}, u32[]{:S(2)}, u32[]{:S(2)}) collective-permute-start(bf16[256,1152]{1,0:T(8,128)(2,1)S(1)} %collective-permute-done.4), channel_id=1, source_target_pairs={{1,0},{2,3},{5,4},{6,7},{9,8},{10,11},{13,12},{14,15},{17,16},{18,... | collective-permute-start | bytes 1769480 | tf_op jit(solution)/shard_map/ppermute | solution.py:269
  91.5 12.1 %copy-start.6 = (bf16[384,1152]{1,0:T(8,128)(2,1)S(1)}, bf16[384,1152]{1,0:T(8,128)(2,1)}, u32[]{:S(2)}) copy-start(bf16[384,1152]{1,0:T(8,128)(2,1)} %copy-done.5) | copy-start | bytes 2654212
  98.7 30.0 %collective-permute-start.1 = (bf16[256,1152]{1,0:T(8,128)(2,1)S(1)}, bf16[256,1152]{1,0:T(8,128)(2,1)S(1)}, u32[]{:S(2)}, u32[]{:S(2)}) collective-permute-start(bf16[256,1152]{1,0:T(8,128)(2,1)S(1)} %get-tuple-element.16), channel_id=1, source_target_pairs={{0,1},{1,0},{2,3},{3,2},{4,5},{5,4},{6,7},{7,6},{8,9},{9,8},{10,11... | collective-permute-start | bytes 1769480 | tf_op jit(solution)/shard_map/ppermute | solution.py:208
  101.5 29.0 %collective-permute-start.25 = (bf16[384,1152]{1,0:T(8,128)(2,1)S(1)}, bf16[384,1152]{1,0:T(8,128)(2,1)S(1)}, u32[]{:S(2)}, u32[]{:S(2)}) collective-permute-start(bf16[384,1152]{1,0:T(8,128)(2,1)S(1)} %collective-permute-done.24.refs_4_), channel_id=1, source_target_pairs={{0,4},{4,0},{8,12},{12,8},{16,20},{20,16},{24,28},{28,24},{1,5},{5... | collective-permute-start | bytes 2654216 | tf_op jit(solution)/shard_map/ppermute | solution.py:208
  101.9 25.3 %collective-permute-start.3 = (bf16[256,1152]{1,0:T(8,128)(2,1)S(1)}, bf16[256,1152]{1,0:T(8,128)(2,1)S(1)}, u32[]{:S(2)}, u32[]{:S(2)}) collective-permute-start(bf16[256,1152]{1,0:T(8,128)(2,1)S(1)} %collective-permute-done.2), channel_id=1, source_target_pairs={{1,0},{2,3},{5,4},{6,7},{9,8},{10,11},{13,12},{14,15},{17,16},{18,... | collective-permute-start | bytes 1769480 | tf_op jit(solution)/shard_map/ppermute | solution.py:269
  103.6 26.8 %copy-start.7 = (bf16[384,1152]{1,0:T(8,128)(2,1)}, bf16[384,1152]{1,0:T(8,128)(2,1)S(1)}, u32[]{:S(2)}) copy-start(bf16[384,1152]{1,0:T(8,128)(2,1)S(1)} %constant_dynamic-update-slice_fusion.5.refs_6_) | copy-start | bytes 2654212
  103.7 26.8 %collective-permute-start.23 = (bf16[384,1152]{1,0:T(8,128)(2,1)S(1)}, bf16[384,1152]{1,0:T(8,128)(2,1)S(1)}, u32[]{:S(2)}, u32[]{:S(2)}) collective-permute-start(bf16[384,1152]{1,0:T(8,128)(2,1)S(1)} %copy-done.6), channel_id=1, source_target_pairs={{0,4},{4,0},{8,12},{12,8},{16,20},{20,16},{24,28},{28,24},{1,5},{5... | collective-permute-start | bytes 2654216 | tf_op jit(solution)/shard_map/ppermute | solution.py:208
  127.3 4.1 %collective-permute-start.28 = (bf16[384,1152]{1,0:T(8,128)(2,1)S(1)}, bf16[384,1152]{1,0:T(8,128)(2,1)S(1)}, u32[]{:S(2)}, u32[]{:S(2)}) collective-permute-start(bf16[384,1152]{1,0:T(8,128)(2,1)S(1)} %constant_dynamic-update-slice_fusion.5.refs_6_), channel_id=1, source_target_pairs={{0,4},{4,0},{8,12},{12,8},{16,20},{20,16},{24,28},{28,24},{1,5},{5... | collective-permute-start | bytes 2654216 | tf_op jit(solution)/shard_map/ppermute | solution.py:208
  131.4 0.9 copy-start.12
  172.7 8.1 %collective-permute-start.29 = (bf16[2304,1024]{1,0:T(8,128)(2,1)}, bf16[2304,1024]{1,0:T(8,128)(2,1)S(1)}, u32[]{:S(2)}, u32[]{:S(2)}) collective-permute-start(bf16[2304,1024]{1,0:T(8,128)(2,1)} %get-tuple-element.9.ka_ref.va_ref), channel_id=1, source_target_pairs={{0,4},{4,0},{8,12},{12,8},{16,20},{20,16},{24,28},{28,24},{1,5},{5... | collective-permute-start | bytes 14155784 | tf_op jit(solution)/shard_map/ppermute | solution.py:208
  180.9 2.2 copy-start.2
  215.8 15.9 %collective-permute-start.31 = (bf16[256,1152]{1,0:T(8,128)(2,1)S(1)}, bf16[256,1152]{1,0:T(8,128)(2,1)S(1)}, u32[]{:S(2)}, u32[]{:S(2)}) collective-permute-start(bf16[256,1152]{1,0:T(8,128)(2,1)S(1)} %get-tuple-element.18), channel_id=1, source_target_pairs={{0,1},{1,3},{3,2},{2,0},{4,5},{5,7},{7,6},{6,4},{8,9},{9,11},{11,1... | collective-permute-start | bytes 1769480 | tf_op jit(solution)/shard_map/ppermute | solution.py:298
  217.9 27.4 %collective-permute-start.30 = (bf16[256,1152]{1,0:T(8,128)(2,1)S(1)}, bf16[256,1152]{1,0:T(8,128)(2,1)S(1)}, u32[]{:S(2)}, u32[]{:S(2)}) collective-permute-start(bf16[256,1152]{1,0:T(8,128)(2,1)S(1)} %get-tuple-element.19), channel_id=1, source_target_pairs={{0,0},{1,2},{3,3},{2,1},{4,4},{5,6},{7,7},{6,5},{8,8},{9,10},{11,1... | collective-permute-start | bytes 1769480 | tf_op jit(solution)/shard_map/ppermute | solution.py:298
  245.5 2.6 %collective-permute-start.32 = (bf16[256,1152]{1,0:T(8,128)(2,1)S(1)}, bf16[256,1152]{1,0:T(8,128)(2,1)S(1)}, u32[]{:S(2)}, u32[]{:S(2)}) collective-permute-start(bf16[256,1152]{1,0:T(8,128)(2,1)S(1)} %get-tuple-element.11), channel_id=1, source_target_pairs={{0,4},{4,0},{8,12},{12,8},{16,20},{20,16},{24,28},{28,24},{1,5},{5... | collective-permute-start | bytes 1769480 | tf_op jit(solution)/shard_map/ppermute | solution.py:208
  248.1 1.2 copy-start.1
  (3 other events, 2.7 us)

commit v2 on v1

v2 whole, which is shorter than its diff:
```python
import functools
import math

import jax
import jax.numpy as jnp
from jax import lax
from jax.experimental import pallas as pl
from jax.experimental.pallas import tpu as pltpu
from jax.sharding import PartitionSpec as P

HEADS = 16
F32 = jnp.float32
BF16 = jnp.bfloat16
VMEM_LIMIT = 56 * 2**20


def contract(a, b, dims):
    return lax.dot_general(a, b, (dims, ((), ())), preferred_element_type=F32)


def pick_kernel(bases, count, idx_ref, acc_ref, *refs):
    pieces, (out_ref, rows_ref) = refs[:-2], refs[-2:]
    rows = pieces[0].shape[0]

    @pl.when(pl.program_id(0) == 0)
    def _():
        for n, piece in enumerate(pieces):
            rows_ref[n * rows : (n + 1) * rows, :] = piece[...]

    idx = idx_ref[...]
    lane = lax.broadcasted_iota(jnp.int32, (1, rows), 1)
    hot = jnp.concatenate(
        [jnp.where(idx == lane + base, 1.0, 0.0).astype(BF16) for base in bases], axis=1
    )
    picked = contract(hot, rows_ref[...], ((1,), (0,)))
    out_ref[...] = (picked + acc_ref[...].astype(F32)).astype(BF16)


def pick_rows(idx, acc, pieces, bases, block):
    count, width = acc.shape
    rows = pieces[0].shape[0]
    return pl.pallas_call(
        functools.partial(pick_kernel, bases, count),
        grid=(count // block,),
        in_specs=[
            pl.BlockSpec((block, 1), lambda i: (i, 0)),
            pl.BlockSpec((block, width), lambda i: (i, 0)),
        ]
        + [
            pl.BlockSpec((rows, width), lambda i: (0, 0), pipeline_mode=pl.Buffered(1))
            for _ in pieces
        ],
        out_specs=pl.BlockSpec((block, width), lambda i: (i, 0)),
        out_shape=jax.ShapeDtypeStruct((count, width), BF16),
        scratch_shapes=[pltpu.VMEM((len(pieces) * rows, width), BF16)],
        input_output_aliases={1: 0},
        compiler_params=pltpu.CompilerParams(vmem_limit_bytes=VMEM_LIMIT),
        cost_estimate=pl.CostEstimate(flops=1, bytes_accessed=1, transcendentals=0),
        name="pick",
    )(idx, acc, *pieces)


def stretch_kernel(
    steps, tok_ref, act_ref, ws_ref, wc_ref, bs_ref, bc_ref, w_ref, kv_ref, x_ref, norm_ref, silu_ref
):
    i = pl.program_id(0)
    cols = ws_ref.shape[1]

    @pl.when(i == 0)
    def _():
        values = tok_ref[...].astype(F32)
        moved = values - jnp.mean(values, axis=1, keepdims=True)
        spread = jnp.mean(moved * moved, axis=1, keepdims=True)
        norm_ref[...] = moved * lax.rsqrt(spread + 1e-06)
        silu_ref[...] = jax.nn.silu(act_ref[...].astype(F32)).astype(BF16)

    for step in range(steps):

        @pl.when(i == step)
        def _():
            act = silu_ref[...]
            shift = (contract(act, ws_ref[...], ((1,), (0,))) + bs_ref[...]).astype(BF16)
            scale = (contract(act, wc_ref[...], ((1,), (0,))) + bc_ref[...]).astype(BF16)
            span = slice(step * cols, (step + 1) * cols)
            x_ref[:, span] = (
                norm_ref[:, span] * (1.0 + scale.astype(F32)) + shift.astype(F32)
            ).astype(BF16)

    @pl.when(i >= steps)
    def _():
        kv_ref[...] = contract(w_ref[...], x_ref[...], ((0,), (1,))).astype(BF16)


def stretch(tok, picked, w_ada, b_ada, w_qkv, first, count):
    width = tok.shape[1]
    cols, rows = width // 3, width
    steps, kv_steps = width // cols, 2 * width // rows
    at = first // count

    def ada(i):
        return jnp.minimum(i, steps - 1)

    def kv(i):
        return jnp.maximum(i - steps, 0)

    return pl.pallas_call(
        functools.partial(stretch_kernel, steps),
        grid=(steps + kv_steps,),
        in_specs=[
            pl.BlockSpec((count, width), lambda i: (0, 0)),
            pl.BlockSpec((count, width), lambda i: (at, 0)),
            pl.BlockSpec((width, cols), lambda i: (0, ada(i))),
            pl.BlockSpec((width, cols), lambda i: (0, ada(i) + steps)),
            pl.BlockSpec((1, cols), lambda i: (0, ada(i))),
            pl.BlockSpec((1, cols), lambda i: (0, ada(i) + steps)),
            pl.BlockSpec((width, rows), lambda i: (0, kv(i) + width // rows)),
        ],
        out_specs=[
            pl.BlockSpec((rows, count), lambda i: (kv(i), 0)),
            pl.BlockSpec((count, width), lambda i: (0, 0)),
        ],
        out_shape=[
            jax.ShapeDtypeStruct((2 * width, count), BF16),
            jax.ShapeDtypeStruct((count, width), BF16),
        ],
        scratch_shapes=[pltpu.VMEM((count, width), F32), pltpu.VMEM((count, width), BF16)],
        compiler_params=pltpu.CompilerParams(vmem_limit_bytes=VMEM_LIMIT),
        cost_estimate=pl.CostEstimate(flops=1, bytes_accessed=1, transcendentals=0),
        name="stretch",
    )(tok, picked, w_ada, w_ada, b_ada, b_ada, w_qkv)


def query_kernel(query_scale, place_ref, x_ref, act_ref, wg_ref, bg_ref, w_ref, q_ref, gate_ref):
    act = jax.nn.silu(act_ref[...].astype(F32)).astype(BF16)
    gate_ref[...] = (contract(act, wg_ref[...], ((1,), (0,))) + bg_ref[...]).astype(BF16)
    q = contract(w_ref[...], x_ref[...], ((0,), (1,)))
    q_ref[...] = (q * query_scale).astype(BF16)


def query(place, x, picked, w_ada, b_ada, w_qkv):
    count, width = x.shape
    query_scale = math.log2(math.e) / math.sqrt(width // HEADS)
    cols = width // 3
    last = 2 * width // cols
    return pl.pallas_call(
        functools.partial(query_kernel, query_scale),
        grid_spec=pltpu.PrefetchScalarGridSpec(
            num_scalar_prefetch=1,
            grid=(width // cols,),
            in_specs=[
                pl.BlockSpec((count, width), lambda i, place: (0, 0)),
                pl.BlockSpec((count, width), lambda i, place: (place[0] // 2, 0)),
                pl.BlockSpec((width, cols), lambda i, place: (0, i + last)),
                pl.BlockSpec((1, cols), lambda i, place: (0, i + last)),
                pl.BlockSpec((width, cols), lambda i, place: (0, i)),
            ],
            out_specs=[
                pl.BlockSpec((cols, count), lambda i, place: (i, 0)),
                pl.BlockSpec((count, cols), lambda i, place: (0, i)),
            ],
        ),
        out_shape=[
            jax.ShapeDtypeStruct((width, count), BF16),
            jax.ShapeDtypeStruct((count, width), BF16),
        ],
        compiler_params=pltpu.CompilerParams(vmem_limit_bytes=VMEM_LIMIT),
        cost_estimate=pl.CostEstimate(
            flops=4 * count * width * width, bytes_accessed=4 * width * width, transcendentals=0
        ),
        name="query",
    )(place, x, picked, w_ada, b_ada, w_qkv)


def attend_kernel(head_dim, chunk, place_ref, q_ref, *refs):
    kv_refs, (o_ref, s_ref) = refs[:-2], refs[-2:]
    pair, queries = q_ref.shape
    row = lax.broadcasted_iota(jnp.int32, (pair, 1), 0)
    q = q_ref[...]
    zero = jnp.zeros_like(q)
    both = jnp.concatenate(
        [jnp.where(row < head_dim, q, zero), jnp.where(row < head_dim, zero, q)], axis=1
    )
    half = len(kv_refs) // 2
    parts = [
        (k_ref, v_ref, i)
        for k_ref, v_ref in zip(kv_refs[:half], kv_refs[half:])
        for i in range(0, k_ref.shape[1], chunk)
    ]
    top = None
    for n, (k_ref, _, i) in enumerate(parts):
        scores = contract(k_ref[:, i : i + chunk], both, ((0,), (0,)))
        s_ref[n * chunk : (n + 1) * chunk, :] = scores
        peak = jnp.max(scores, axis=0, keepdims=True)
        top = peak if top is None else jnp.maximum(top, peak)
    weighted = denominator = None
    for n, (_, v_ref, i) in enumerate(parts):
        expo = jnp.exp2(s_ref[n * chunk : (n + 1) * chunk, :] - top)
        total = jnp.sum(expo, axis=0, keepdims=True)
        part = contract(v_ref[:, i : i + chunk], expo.astype(BF16), ((1,), (0,)))
        weighted = part if weighted is None else weighted + part
        denominator = total if denominator is None else denominator + total
    result = weighted / denominator
    o_ref[...] = jnp.where(row < head_dim, result[:, :queries], result[:, queries:]).astype(BF16)


def attend(place, which, qt, kvs):
    width, queries = qt.shape[0], qt.shape[1] // 2
    keys = kvs[0].shape[1]
    head_dim = width // HEADS
    pair, pairs = 2 * head_dim, HEADS // 2
    chunk = math.gcd(keys, 512)
    k_spec = pl.BlockSpec((pair, keys), lambda p, place: (p, 0))
    v_spec = pl.BlockSpec((pair, keys), lambda p, place: (p + pairs, 0))
    total = len(kvs) * keys
    return pl.pallas_call(
        functools.partial(attend_kernel, head_dim, chunk),
        grid_spec=pltpu.PrefetchScalarGridSpec(
            num_scalar_prefetch=1,
            grid=(pairs,),
            in_specs=[pl.BlockSpec((pair, queries), lambda p, place: (p, place[which]))]
            + [k_spec] * len(kvs)
            + [v_spec] * len(kvs),
            out_specs=pl.BlockSpec((pair, queries), lambda p, place: (p, 0)),
            scratch_shapes=[pltpu.VMEM((total, 2 * queries), F32)],
        ),
        out_shape=jax.ShapeDtypeStruct((width, queries), BF16),
        compiler_params=pltpu.CompilerParams(vmem_limit_bytes=VMEM_LIMIT),
        cost_estimate=pl.CostEstimate(
            flops=16 * total * queries * width,
            bytes_accessed=4 * total * width,
            transcendentals=HEADS * total * queries,
        ),
        name="attend",
    )(place, qt, *kvs, *kvs)


def finish_kernel(place_ref, att_ref, tok_ref, gate_ref, w_ref, o_ref):
    projected = contract(att_ref[...], w_ref[...], ((0,), (0,)))
    o_ref[...] = (tok_ref[...].astype(F32) + gate_ref[...].astype(F32) * projected).astype(BF16)


def finish(place, which, attended, tok, gate, w_out):
    width, queries = attended.shape
    at = pl.BlockSpec((queries, width), lambda i, place: (place[which], 0))
    return pl.pallas_call(
        finish_kernel,
        grid_spec=pltpu.PrefetchScalarGridSpec(
            num_scalar_prefetch=1,
            grid=(1,),
            in_specs=[
                pl.BlockSpec((width, queries), lambda i, place: (0, 0)),
                at,
                at,
                pl.BlockSpec((width, width), lambda i, place: (0, 0)),
            ],
            out_specs=pl.BlockSpec((queries, width), lambda i, place: (0, 0)),
        ),
        out_shape=jax.ShapeDtypeStruct((queries, width), BF16),
        compiler_params=pltpu.CompilerParams(vmem_limit_bytes=VMEM_LIMIT),
        name="finish",
    )(place, attended, tok, gate, w_out)


def swap(x, axis, bits):
    return lax.ppermute(x, axis, [(i, i ^ bits) for i in range(lax.axis_size(axis))])


def after(x, *others):
    return lax.optimization_barrier((x, others))[0]


def to_chips(own):
    return {o: swap(own, "region", o) if o else own for o in range(0, lax.axis_size("region"), 2)}


def to_cores(blocks):
    both = blocks | {o ^ 1: swap(b, "region", 1) for o, b in blocks.items()}
    return [both[o] for o in range(len(both))]


def per_device(
    tokens, element_ids, element_slot, live_count, cond_table, w_ada, b_ada, w_qkv, w_out
):
    device_tokens = tokens[0]
    tok_rows, width = device_tokens.shape
    elem_rows = cond_table.shape[0]
    size, n = lax.axis_size("region"), lax.axis_size("ctx")
    h = n // 2
    block = tok_rows // 2
    r, c = lax.axis_index("region"), lax.axis_index("ctx")
    core, upper = r % 2, (c >= h).astype(jnp.int32)
    m = jnp.where(upper == 1, n - 1 - c, c)

    tables = [swap(cond_table, "ctx", d) for d in range(1, n)]
    near = to_chips(cond_table)
    mine = lax.dynamic_slice_in_dim(device_tokens, core * block, block)
    other = lax.dynamic_slice_in_dim(device_tokens, (1 - core) * block, block)
    got = swap(other, "region", 1)
    position = jnp.arange(tok_rows, dtype=jnp.int32)
    ids = jnp.where(position < live_count[0, 0], element_ids[0], -1)
    ids = [ids] + [swap(ids, "ctx", d) for d in range(1, n)]
    tables, near, mine, got, ids = lax.optimization_barrier((tables, near, mine, got, ids))

    even, odd = jnp.where(core == 0, mine, got), jnp.where(core == 0, got, mine)
    work, pass_on = jnp.where(upper == 0, even, odd), jnp.where(upper == 0, odd, even)
    far = to_chips(jnp.concatenate(tables, axis=0))
    arrived = [work] + [swap(work if d < h else pass_on, "ctx", d) for d in range(1, n)]

    ids = jnp.stack(ids)
    ids = jnp.where(core == upper, ids, swap(ids, "region", 1))
    ids = lax.dynamic_slice_in_dim(ids, core * block, block, axis=1)
    ids = ids.reshape(n * block, 1)
    slots = element_slot[jnp.maximum(ids, 0)]
    owner = slots // elem_rows
    relative = ((((owner // n) ^ r) * n) + ((owner % n) ^ c)) * elem_rows + slots % elem_rows
    relative = jnp.where(ids < 0, -1, relative)

    def pick(picked, pieces, d):
        bases = [(o * n + d) * elem_rows for o in range(size)]
        return pick_rows(relative, picked, pieces, bases, 2 * block)

    picked = jnp.zeros((n * block, width), BF16)
    picked = pick(picked, to_cores(near), 0)
    far, picked = lax.optimization_barrier((far, picked))
    far = to_cores(far)
    for lo in range(0, size, 8):
        bases = [(o * n + 1) * elem_rows for o in range(lo, lo + 8)]
        picked = pick_rows(relative, picked, far[lo : lo + 8], bases, 2 * block)

    base, flip = ((2 * m) ^ m) & ~1, m & 1
    place = jnp.stack([base, core ^ flip, 1 - core ^ flip]).astype(jnp.int32)
    bias = b_ada.reshape(1, -1)
    kvs, xs, toks = [], [], []
    for at in range(0, n, 2):
        tok = jnp.concatenate(arrived[at : at + 2], axis=0)
        kv, x = stretch(tok, picked, w_ada, bias, w_qkv, at * block, 2 * block)
        kvs += [kv, swap(kv, "region", 1)]
        xs.append(x)
        toks.append(tok)
    x, tok = xs[0], toks[0]
    for at in range(1, n // 2):
        here = base == 2 * at
        x, tok = jnp.where(here, xs[at], x), jnp.where(here, toks[at], tok)
    qt, gate = query(place, x, picked, w_ada, bias, w_qkv)

    home = []
    for which in (1, 2):
        attended = attend(place, which, qt, kvs)
        result = finish(place, which, attended, tok, gate, w_out)
        pairs = []
        for region in range(size):
            for k in range(h):
                to = 2 * k + (region % 2 if which == 1 else 1 - region % 2)
                pairs.append((region * n + k, (region & ~1) * n + to))
                pairs.append((region * n + n - 1 - k, (region | 1) * n + n - 1 - to))
        home.append(lax.ppermute(result, ("region", "ctx"), pairs))
    number = jnp.where(core == 1, n - 1 - c, c) % 2
    low, high = jnp.where(number == 0, home[0], home[1]), jnp.where(number == 0, home[1], home[0])
    return jnp.concatenate([low, high], axis=0)[None]


def solution(mesh):
    placed = (
        P("region", "ctx", None),
        P("region", "ctx"),
        P(),
        P("region", "ctx"),
        P(("region", "ctx"), None),
        P(),
        P(),
        P(),
        P(),
    )
    return jax.shard_map(
        per_device, mesh=mesh, in_specs=placed, out_specs=P("region", "ctx", None), check_vma=False
    )
```

time: 250 us -> 218 us (0.87); the launches traced: 249 us -> 214 us
  waiting for transfers between devices: 100 us -> 59.1 us
  Pallas kernels: 78.1 us -> 96.9 us
  local copies, waits for them, and re-layouts: 27.7 us -> 16.7 us
  starting transfers between devices: 35.6 us -> 30.8 us
  other arithmetic: 6.77 us -> 9.39 us
    ppermute x6 -> x2, waiting for transfers between devices: 58.7 us -> 12.1 us  [per_device(): home.append(lax.ppermute(result, ('region', 'ctx'), pairs))]
    pallas_call x2 -> x5, Pallas kernels: 51.1 us -> 67 us  [the longest x2 31.5 us: attend(): pl.pallas_call(functools.partial(attend_kernel, head_dim, chunk), grid_sp...]
    unnamed x43 -> x50, local copies, waits for them, and re-layouts: 18.5 us -> 4.83 us
    ppermute x6 -> x2, starting transfers between devices: 11.5 us -> 4.52 us  [per_device(): home.append(lax.ppermute(result, ('region', 'ctx'), pairs))]
    ppermute x27, waiting for transfers between devices: 41.3 us -> 47 us  [swap(): lax.ppermute(x, axis, [(i, i ^ bits) for i in range(lax.axis_size(axis))])]
    pallas_call x1 -> x2, Pallas kernels: 6.12 us -> 9.7 us  [finish(): pl.pallas_call(finish_kernel, grid_spec=pltpu.PrefetchScalarGridSpec(num_...]
    select_n x10 -> x5, other arithmetic: 2.95 us -> 5.97 us  [the longest x2 2.98 us: per_device(): x, tok = (jnp.where(here, xs[at], x), jnp.where(here, toks[at], tok))]
    gather x2, local copies, waits for them, and re-layouts: 3.7 us -> 6.37 us  [per_device(): slots = element_slot[jnp.maximum(ids, 0)]]
  transfers between devices with their start and end apart: 33 -> 29, of which waited for: 9 -> 8; matrix products, arithmetic and copies ran while one was open for 9% -> 9% of each run, Pallas kernels for 3% -> 17%
where the time goes in v2:
time: 218 us; the launch traced here: 214 us
  Pallas kernels  96.9 us (44%)
  waiting for transfers between devices  59.1 us (27%)
  starting transfers between devices  30.8 us (14%)
  local copies, waits for them, and re-layouts  16.7 us (8%)
  other arithmetic  9.39 us (4%)
    ppermute x27, waiting for transfers between devices, swap(): lax.ppermute(x, axis, [(i, i ^ bits) for i in range(lax.axis_size(axis))])  47 us
    pallas_call x2, Pallas kernels, attend(): pl.pallas_call(functools.partial(attend_kernel, head_dim, chunk), grid_sp...  31.5 us
    pallas_call x2, Pallas kernels, stretch(): pl.pallas_call(functools.partial(stretch_kernel, steps), grid=(steps + kv...  27.4 us
    ppermute x27, starting transfers between devices, swap(): lax.ppermute(x, axis, [(i, i ^ bits) for i in range(lax.axis_size(axis))])  26.2 us
    pallas_call x2, Pallas kernels, pick_rows(): pl.pallas_call(functools.partial(pick_kernel, bases, count), grid=(count...  20.2 us
    ppermute x2, waiting for transfers between devices, per_device(): home.append(lax.ppermute(result, ('region', 'ctx'), pairs))  12.1 us
    pallas_call x2, Pallas kernels, finish(): pl.pallas_call(finish_kernel, grid_spec=pltpu.PrefetchScalarGridSpec(num_...  9.7 us
    pallas_call x1, Pallas kernels, query(): pl.pallas_call(functools.partial(query_kernel, query_scale), grid_spec=pl...  8.09 us
  transfers between devices with their start and end apart: 29, of which 8 were waited for; matrix products, arithmetic and copies ran while one was open for 9% of the time, Pallas kernels for 17%

profile of v2, /device:TPU:17, one launch (start us, length us, event | category | flops | bytes accessed | tf_op | source)
XLA Modules:
  0.0 213.8 jit_solution(7228223151243102302)
XLA Ops:
  0.0 1.3 collective-permute-start
  1.4 1.4 dynamic-slice_bitcast_fusion
  2.7 1.3 collective-permute-start.6
  4.8 2.5 %collective-permute-start.8 = (s32[512]{0:T(512)S(1)}, s32[512]{0:T(512)S(1)}, u32[]{:S(2)}, u32[]{:S(2)}) collective-permute-start(s32[512]{0:T(512)S(1)} %fusion.13), channel_id=1, source_target_pairs={{0,2},{1,3},{2,0},{3,1},{4,6},{5,7},{6,4},{7,5},{8,10},{9,11},{10,... | collective-permute-start | bytes 6152 | tf_op jit(solution)/shard_map/ppermute | solution.py:265
  7.3 7.2 %collective-permute-done.7 = s32[512]{0:T(512)S(1)} collective-permute-done((s32[512]{0:T(512)S(1)}, s32[512]{0:T(512)S(1)}, u32[]{:S(2)}, u32[]{:S(2)}) %collective-permute-start.7) | collective-permute-done | bytes 2080 | tf_op jit(solution)/shard_map/ppermute | solution.py:265
  14.7 1.4 collective-permute-start.2
  16.0 0.9 collective-permute-done.9
  16.9 1.2 collective-permute-start.3
  18.2 1.3 collective-permute-start.4
  19.9 1.3 reshape.262.bs_ref.bc_ref.bg_ref
  21.2 7.1 %collective-permute-done.2 = bf16[128,1152]{1,0:T(8,128)(2,1)S(1)} collective-permute-done((bf16[128,1152]{1,0:T(8,128)(2,1)S(1)}, bf16[128,1152]{1,0:T(8,128)(2,1)S(1)}, u32[]{:S(2)}, u32[]{:S(2)}) %collective-permute-start.2) | collective-permute-done | bytes 294944 | tf_op jit(solution)/shard_map/ppermute | solution.py:265
  28.4 0.8 pad_add_fusion
  29.1 9.1 %collective-permute-start.12 = (s32[4,512]{1,0:T(4,128)S(1)}, s32[4,512]{1,0:T(4,128)S(1)}, u32[]{:S(2)}, u32[]{:S(2)}) collective-permute-start(s32[4,512]{1,0:T(4,128)S(1)} %pad_add_fusion), channel_id=1, source_target_pairs={{0,4},{4,0},{8,12},{12,8},{16,20},{20,16},{24,28},{28,24},{1,5},{5... | collective-permute-start | bytes 24584 | tf_op jit(solution)/shard_map/ppermute | solution.py:265
  38.8 0.7 collective-permute-start.13
  39.5 0.9 collective-permute-start.14
  40.4 1.2 collective-permute-start.15
  41.6 1.0 collective-permute-start.18
  42.6 0.7 copy-done.14
  43.9 1.0 broadcast_select_fusion.4
  44.9 0.7 copy-done.15
  45.7 0.9 copy.18
  46.6 6.2 %gather_fusion = s32[1024]{0:T(1024)S(1)} fusion(s32[4096]{0:T(1024)S(1)} %copy-done, s32[1024]{0:T(1024)S(1)} %broadcast_clamp_fusion), kind=kCustom, calls=%fused_computation | custom fusion | bytes 12288 | tf_op jit(solution)/shard_map/gather | solution.py:313
  52.9 7.3 %collective-permute-done.13.refs_2_ = bf16[384,1152]{1,0:T(8,128)(2,1)S(1)} collective-permute-done((bf16[384,1152]{1,0:T(8,128)(2,1)S(1)}, bf16[384,1152]{1,0:T(8,128)(2,1)S(1)}, u32[]{:S(2)}, u32[]{:S(2)}) %collective-permute-start.13) | collective-permute-done | bytes 884768 | tf_op jit(solution)/shard_map/ppermute | solution.py:265
  60.3 2.9 %fusion.5.idx_ref = s32[1024,1]{1,0:T(8,128)} fusion(s32[1024,1]{1,0:T(8,128)S(1)} %copy.12, pred[1,1024]{0,1:T(8,128)(4,1)} %copy.18, s32[]{:T(128)S(6)} %axis_index.25, s32[]{:T(128)S(6)} %axis_index.23), kind=kLoop, calls=%fused_computation.28 | loop fusion | flops 46080 | bytes 9224 | tf_op jit(solution)/shard_map/jit(_where)/select_n | solution.py:316
  63.1 1.6 broadcast_in_dim.17.acc_ref
  64.7 6.6 %pick.2.acc_ref = bf16[1024,1152]{1,0:T(8,128)(2,1)} custom-call(s32[1024,1]{1,0:T(8,128)} %fusion.5.idx_ref, bf16[1024,1152]{1,0:T(8,128)(2,1)} %broadcast_in_dim.17.acc_ref, bf16[128,1152]{1,0:T(8,128)(2,1)} %refs_0_, bf16[128,1152]{1,0:T(8,128)(2,1)} %copy-done.13, bf16[128,1152]{1,0:T(8,128)(2,1)} %copy-done.10, ...), custom_call_target="tpu_custom_call", output_to_operand_aliasing={{}: (1, {})} | custom-call | flops 1 | bytes 1 | tf_op jit(solution)/shard_map/pick/pallas_call | solution.py:42
  71.3 8.8 %collective-permute-done.15.refs_6_ = bf16[384,1152]{1,0:T(8,128)(2,1)} collective-permute-done((bf16[384,1152]{1,0:T(8,128)(2,1)S(1)}, bf16[384,1152]{1,0:T(8,128)(2,1)}, u32[]{:S(2)}, u32[]{:S(2)}) %collective-permute-start.15) | collective-permute-done | bytes 884768 | tf_op jit(solution)/shard_map/ppermute | solution.py:265
  80.2 0.9 collective-permute-start.20
  81.1 1.5 collective-permute-done.10
  83.1 14.0 %collective-permute-done.11 = bf16[256,1152]{1,0:T(8,128)(2,1)} collective-permute-done((bf16[256,1152]{1,0:T(8,128)(2,1)}, bf16[256,1152]{1,0:T(8,128)(2,1)}, u32[]{:S(2)}, u32[]{:S(2)}) %collective-permute-start.11) | collective-permute-done | bytes 589856 | tf_op jit(solution)/shard_map/ppermute | solution.py:265
  97.1 0.8 collective-permute-start.23
  97.9 1.1 constant_dynamic-update-slice_fusion.tok_ref
  99.1 1.8 broadcast_select_fusion
  101.0 0.9 copy-done.5
  102.4 0.9 copy-done.8
  103.4 13.6 %pick.3.act_ref = bf16[1024,1152]{1,0:T(8,128)(2,1)} custom-call(s32[1024,1]{1,0:T(8,128)} %fusion.5.idx_ref, bf16[1024,1152]{1,0:T(8,128)(2,1)} %pick.2.acc_ref, bf16[384,1152]{1,0:T(8,128)(2,1)} %copy-done.2, bf16[384,1152]{1,0:T(8,128)(2,1)} %copy-done.5, bf16[384,1152]{1,0:T(8,128)(2,1)} %copy-done.4, ...), custom_call_target="tpu_custom_call", output_to_operand_aliasing={{}: (1, {})} | custom-call | flops 1 | bytes 1 | tf_op jit(solution)/shard_map/pick/pallas_call | solution.py:42
  116.9 13.7 %stretch.2 = (bf16[2304,512]{1,0:T(8,128)(2,1)}, bf16[512,1152]{1,0:T(8,128)(2,1)}) custom-call(bf16[512,1152]{1,0:T(8,128)(2,1)} %copy-done.1, bf16[1024,1152]{1,0:T(8,128)(2,1)} %pick.3.act_ref, bf16[1152,3456]{1,0:T(8,128)(2,1)} %wg_ref.1, bf16[1152,3456]{1,0:T(8,128)(2,1)} %wg_ref.1, f32[1,3456]{1,0:T(1,128)} %reshape.262.bs_ref.bc_ref.bg_ref, ...), custom_call_target="tpu_custom_call" | custom-call | flops 1 | bytes 1 | tf_op jit(solution)/shard_map/stretch/pallas_call | solution.py:106
  130.6 13.7 %stretch.3 = (bf16[2304,512]{1,0:T(8,128)(2,1)}, bf16[512,1152]{1,0:T(8,128)(2,1)}) custom-call(bf16[512,1152]{1,0:T(8,128)(2,1)} %get-tuple-element.56.tok_ref, bf16[1024,1152]{1,0:T(8,128)(2,1)} %pick.3.act_ref, bf16[1152,3456]{1,0:T(8,128)(2,1)} %wg_ref.1, bf16[1152,3456]{1,0:T(8,128)(2,1)} %wg_ref.1, f32[1,3456]{1,0:T(1,128)} %reshape.262.bs_ref.bc_ref.bg_ref, ...), custom_call_target="tpu_custom_call" | custom-call | flops 1 | bytes 1 | tf_op jit(solution)/shard_map/stretch/pallas_call | solution.py:106
  145.4 1.1 broadcast_select_fusion.1.x_ref
  146.6 8.1 %query.1 = (bf16[1152,512]{1,0:T(8,128)(2,1)}, bf16[512,1152]{1,0:T(8,128)(2,1)}) custom-call(s32[3]{0:T(128)} %pad_add_fusion.1.place_ref, bf16[512,1152]{1,0:T(8,128)(2,1)} %broadcast_select_fusion.1.x_ref, bf16[1024,1152]{1,0:T(8,128)(2,1)} %pick.3.act_ref, bf16[1152,3456]{1,0:T(8,128)(2,1)} %wg_ref.1, f32[1,3456]{1,0:T(1,128)} %reshape.262.bs_ref.bc_ref.bg_ref, ...), custom_call_target="tpu_custom_call" | custom-call | flops 2717908992 | bytes 5308416 | tf_op jit(solution)/shard_map/query/pallas_call | solution.py:145
  154.7 15.8 %attend.3.att_ref = bf16[1152,256]{1,0:T(8,128)(2,1)} custom-call(s32[3]{0:T(128)} %pad_add_fusion.1.place_ref, bf16[1152,512]{1,0:T(8,128)(2,1)} %get-tuple-element.49.q_ref, bf16[2304,512]{1,0:T(8,128)(2,1)} %get-tuple-element.50.refs_0_.refs_4_, bf16[2304,512]{1,0:T(8,128)(2,1)} %collective-permute-done.25.refs_1_.refs_5_, ...), custom_call_target="tpu_custom_call" | custom-call | flops 9663676416 | bytes 9437184 | tf_op jit(solution)/shard_map/attend/pallas_call | solution.py:215
  170.4 4.9 %finish.3 = bf16[256,1152]{1,0:T(8,128)(2,1)} custom-call(s32[3]{0:T(128)} %pad_add_fusion.1.place_ref, bf16[1152,256]{1,0:T(8,128)(2,1)} %attend.3.att_ref, bf16[512,1152]{1,0:T(8,128)(2,1)} %get-tuple-element.55.tok_ref, bf16[512,1152]{1,0:T(8,128)(2,1)} %get-tuple-element.52.gate_ref, bf16[1152,1152]{1,0:T(8,128)(2,1)} %w_ref.9), custom_call_target="tpu_custom_call" | custom-call | tf_op jit(solution)/shard_map/finish/pallas_call | solution.py:245
  175.3 1.9 collective-permute-start.28
  177.2 15.8 %attend.2.att_ref = bf16[1152,256]{1,0:T(8,128)(2,1)} custom-call(s32[3]{0:T(128)} %pad_add_fusion.1.place_ref, bf16[1152,512]{1,0:T(8,128)(2,1)} %get-tuple-element.49.q_ref, bf16[2304,512]{1,0:T(8,128)(2,1)} %get-tuple-element.50.refs_0_.refs_4_, bf16[2304,512]{1,0:T(8,128)(2,1)} %collective-permute-done.25.refs_1_.refs_5_, ...), custom_call_target="tpu_custom_call" | custom-call | flops 9663676416 | bytes 9437184 | tf_op jit(solution)/shard_map/attend/pallas_call | solution.py:215
  193.0 4.8 %finish.2 = bf16[256,1152]{1,0:T(8,128)(2,1)} custom-call(s32[3]{0:T(128)} %pad_add_fusion.1.place_ref, bf16[1152,256]{1,0:T(8,128)(2,1)} %attend.2.att_ref, bf16[512,1152]{1,0:T(8,128)(2,1)} %get-tuple-element.55.tok_ref, bf16[512,1152]{1,0:T(8,128)(2,1)} %get-tuple-element.52.gate_ref, bf16[1152,1152]{1,0:T(8,128)(2,1)} %w_ref.9), custom_call_target="tpu_custom_call" | custom-call | tf_op jit(solution)/shard_map/finish/pallas_call | solution.py:245
  197.8 2.6 %collective-permute-start.27 = (bf16[256,1152]{1,0:T(8,128)(2,1)}, bf16[256,1152]{1,0:T(8,128)(2,1)S(1)}, u32[]{:S(2)}, u32[]{:S(2)}) collective-permute-start(bf16[256,1152]{1,0:T(8,128)(2,1)} %finish.2), channel_id=1, source_target_pairs={{0,0},{3,7},{1,2},{2,5},{4,1},{7,6},{5,3},{6,4},{8,8},{11,15},{9,1... | collective-permute-start | bytes 1769480 | tf_op jit(solution)/shard_map/ppermute | solution.py:356
  200.4 12.1 %collective-permute-done.27 = bf16[256,1152]{1,0:T(8,128)(2,1)S(1)} collective-permute-done((bf16[256,1152]{1,0:T(8,128)(2,1)}, bf16[256,1152]{1,0:T(8,128)(2,1)S(1)}, u32[]{:S(2)}, u32[]{:S(2)}) %collective-permute-start.27) | collective-permute-done | bytes 589856 | tf_op jit(solution)/shard_map/ppermute | solution.py:356
  212.7 1.1 maximum_bitcast_fusion
  (88 shorter events, 4.6 us)
Async XLA Ops:
  0.0 46.6 %copy-start = (s32[4096]{0:T(1024)S(1)}, s32[4096]{0:T(1024)}, u32[]{:S(2)}) copy-start(s32[4096]{0:T(1024)} %param.11) | copy-start | bytes 49156
  0.0 18.2 %collective-permute-start = (bf16[128,1152]{1,0:T(8,128)(2,1)}, bf16[128,1152]{1,0:T(8,128)(2,1)S(1)}, u32[]{:S(2)}, u32[]{:S(2)}) collective-permute-start(bf16[128,1152]{1,0:T(8,128)(2,1)} %refs_0_), channel_id=1, source_target_pairs={{0,1},{1,0},{2,3},{3,2},{4,5},{5,4},{6,7},{7,6},{8,9},{9,8},{10,11... | collective-permute-start | bytes 884744 | tf_op jit(solution)/shard_map/ppermute | solution.py:265
  1.3 18.2 %collective-permute-start.1 = (bf16[128,1152]{1,0:T(8,128)(2,1)}, bf16[128,1152]{1,0:T(8,128)(2,1)S(1)}, u32[]{:S(2)}, u32[]{:S(2)}) collective-permute-start(bf16[128,1152]{1,0:T(8,128)(2,1)} %refs_0_), channel_id=1, source_target_pairs={{0,2},{1,3},{2,0},{3,1},{4,6},{5,7},{6,4},{7,5},{8,10},{9,11},{10,... | collective-permute-start | bytes 884744 | tf_op jit(solution)/shard_map/ppermute | solution.py:265
  1.4 3.3 %copy-start.17 = (s32[1,512]{1,0:T(1,128)S(1)}, s32[1,512]{1,0:T(1,128)}, u32[]{:S(2)}) copy-start(s32[1,512]{1,0:T(1,128)} %param.10) | copy-start | bytes 6148
  1.4 13.3 %copy-start.9 = (bf16[128,1152]{1,0:T(8,128)(2,1)S(1)}, bf16[128,1152]{1,0:T(8,128)(2,1)}, u32[]{:S(2)}) copy-start(bf16[128,1152]{1,0:T(8,128)(2,1)} %refs_0_) | copy-start | bytes 884740
  2.7 25.6 %collective-permute-start.6 = (bf16[256,1152]{1,0:T(8,128)(2,1)S(1)}, bf16[256,1152]{1,0:T(8,128)(2,1)S(1)}, u32[]{:S(2)}, u32[]{:S(2)}) collective-permute-start(bf16[256,1152]{1,0:T(8,128)(2,1)S(1)} %get-tuple-element.59), channel_id=1, source_target_pairs={{0,4},{4,0},{8,12},{12,8},{16,20},{20,16},{24,28},{28,24},{1,5},{5... | collective-permute-start | bytes 1769480 | tf_op jit(solution)/shard_map/ppermute | solution.py:265
  4.7 13.4 %copy-start.16 = (s32[512]{0:T(512)}, s32[512]{0:T(512)S(1)}, u32[]{:S(2)}) copy-start(s32[512]{0:T(512)S(1)} %fusion.13) | copy-start | bytes 6148
  4.7 9.8 %collective-permute-start.7 = (s32[512]{0:T(512)S(1)}, s32[512]{0:T(512)S(1)}, u32[]{:S(2)}, u32[]{:S(2)}) collective-permute-start(s32[512]{0:T(512)S(1)} %fusion.13), channel_id=1, source_target_pairs={{0,1},{1,0},{2,3},{3,2},{4,5},{5,4},{6,7},{7,6},{8,9},{9,8},{10,11... | collective-permute-start | bytes 6152 | tf_op jit(solution)/shard_map/ppermute | solution.py:265
  4.8 9.9 %collective-permute-start.8 = (s32[512]{0:T(512)S(1)}, s32[512]{0:T(512)S(1)}, u32[]{:S(2)}, u32[]{:S(2)}) collective-permute-start(s32[512]{0:T(512)S(1)} %fusion.13), channel_id=1, source_target_pairs={{0,2},{1,3},{2,0},{3,1},{4,6},{5,7},{6,4},{7,5},{8,10},{9,11},{10,... | collective-permute-start | bytes 6152 | tf_op jit(solution)/shard_map/ppermute | solution.py:265
  14.5 3.7 %copy-start.18 = (s32[512]{0:T(512)}, s32[512]{0:T(512)S(1)}, u32[]{:S(2)}) copy-start(s32[512]{0:T(512)S(1)} %collective-permute-done.7) | copy-start | bytes 6148
  14.5 2.4 %collective-permute-start.9 = (s32[512]{0:T(512)S(1)}, s32[512]{0:T(512)S(1)}, u32[]{:S(2)}, u32[]{:S(2)}) collective-permute-start(s32[512]{0:T(512)S(1)} %fusion.13), channel_id=1, source_target_pairs={{0,3},{1,2},{2,1},{3,0},{4,7},{5,6},{6,5},{7,4},{8,11},{9,10},{10,... | collective-permute-start | bytes 6152 | tf_op jit(solution)/shard_map/ppermute | solution.py:265
  14.7 3.5 %copy-start.19 = (s32[512]{0:T(512)}, s32[512]{0:T(512)S(1)}, u32[]{:S(2)}) copy-start(s32[512]{0:T(512)S(1)} %collective-permute-done.8) | copy-start | bytes 6148
  14.7 13.6 %collective-permute-start.2 = (bf16[128,1152]{1,0:T(8,128)(2,1)S(1)}, bf16[128,1152]{1,0:T(8,128)(2,1)S(1)}, u32[]{:S(2)}, u32[]{:S(2)}) collective-permute-start(bf16[128,1152]{1,0:T(8,128)(2,1)S(1)} %copy-done.9), channel_id=1, source_target_pairs={{0,3},{1,2},{2,1},{3,0},{4,7},{5,6},{6,5},{7,4},{8,11},{9,10},{10,... | collective-permute-start | bytes 884744 | tf_op jit(solution)/shard_map/ppermute | solution.py:265
  16.9 1.2 copy-start.20
  16.9 11.4 %collective-permute-start.3 = (bf16[128,1152]{1,0:T(8,128)(2,1)S(1)}, bf16[128,1152]{1,0:T(8,128)(2,1)S(1)}, u32[]{:S(2)}, u32[]{:S(2)}) collective-permute-start(bf16[128,1152]{1,0:T(8,128)(2,1)S(1)} %copy-done.9), channel_id=1, source_target_pairs={{0,8},{4,12},{8,0},{12,4},{16,24},{20,28},{24,16},{28,20},{1,9},{5... | collective-permute-start | bytes 884744 | tf_op jit(solution)/shard_map/ppermute | solution.py:265
  18.2 10.2 %collective-permute-start.4 = (bf16[128,1152]{1,0:T(8,128)(2,1)S(1)}, bf16[128,1152]{1,0:T(8,128)(2,1)S(1)}, u32[]{:S(2)}, u32[]{:S(2)}) collective-permute-start(bf16[128,1152]{1,0:T(8,128)(2,1)S(1)} %copy-done.9), channel_id=1, source_target_pairs={{0,16},{4,20},{8,24},{12,28},{16,0},{20,4},{24,8},{28,12},{1,17},{... | collective-permute-start | bytes 884744 | tf_op jit(solution)/shard_map/ppermute | solution.py:265
  19.5 8.9 %collective-permute-start.5 = (bf16[128,1152]{1,0:T(8,128)(2,1)S(1)}, bf16[128,1152]{1,0:T(8,128)(2,1)}, u32[]{:S(2)}, u32[]{:S(2)}) collective-permute-start(bf16[128,1152]{1,0:T(8,128)(2,1)S(1)} %copy-done.9), channel_id=1, source_target_pairs={{0,24},{4,28},{8,16},{12,20},{16,8},{20,12},{24,0},{28,4},{1,25},{... | collective-permute-start | bytes 884744 | tf_op jit(solution)/shard_map/ppermute | solution.py:265
  28.3 14.2 %copy-start.10 = (bf16[128,1152]{1,0:T(8,128)(2,1)}, bf16[128,1152]{1,0:T(8,128)(2,1)S(1)}, u32[]{:S(2)}) copy-start(bf16[128,1152]{1,0:T(8,128)(2,1)S(1)} %collective-permute-done.3.refs_2_) | copy-start | bytes 884740
  28.3 10.0 %copy-start.11 = (bf16[128,1152]{1,0:T(8,128)(2,1)}, bf16[128,1152]{1,0:T(8,128)(2,1)S(1)}, u32[]{:S(2)}) copy-start(bf16[128,1152]{1,0:T(8,128)(2,1)S(1)} %collective-permute-done.4.refs_4_) | copy-start | bytes 884740
  29.1 11.3 %collective-permute-start.12 = (s32[4,512]{1,0:T(4,128)S(1)}, s32[4,512]{1,0:T(4,128)S(1)}, u32[]{:S(2)}, u32[]{:S(2)}) collective-permute-start(s32[4,512]{1,0:T(4,128)S(1)} %pad_add_fusion), channel_id=1, source_target_pairs={{0,4},{4,0},{8,12},{12,8},{16,20},{20,16},{24,28},{28,24},{1,5},{5... | collective-permute-start | bytes 24584 | tf_op jit(solution)/shard_map/ppermute | solution.py:265
  38.2 3.4 %collective-permute-start.16 = (bf16[128,1152]{1,0:T(8,128)(2,1)S(1)}, bf16[128,1152]{1,0:T(8,128)(2,1)S(1)}, u32[]{:S(2)}, u32[]{:S(2)}) collective-permute-start(bf16[128,1152]{1,0:T(8,128)(2,1)S(1)} %copy-done.9), channel_id=1, source_target_pairs={{0,4},{4,0},{8,12},{12,8},{16,20},{20,16},{24,28},{28,24},{1,5},{5... | collective-permute-start | bytes 884744 | tf_op jit(solution)/shard_map/ppermute | solution.py:265
  38.3 4.3 %collective-permute-start.17 = (bf16[128,1152]{1,0:T(8,128)(2,1)S(1)}, bf16[128,1152]{1,0:T(8,128)(2,1)S(1)}, u32[]{:S(2)}, u32[]{:S(2)}) collective-permute-start(bf16[128,1152]{1,0:T(8,128)(2,1)S(1)} %collective-permute-done.3.refs_2_), channel_id=1, source_target_pairs={{0,4},{4,0},{8,12},{12,8},{16,20},{20,16},{24,28},{28,24},{1,5},{5... | collective-permute-start | bytes 884744 | tf_op jit(solution)/shard_map/ppermute | solution.py:265
  38.7 2.9 %copy-start.12 = (bf16[128,1152]{1,0:T(8,128)(2,1)S(1)}, bf16[128,1152]{1,0:T(8,128)(2,1)}, u32[]{:S(2)}) copy-start(bf16[128,1152]{1,0:T(8,128)(2,1)} %copy-done.11) | copy-start | bytes 884740
  38.8 41.3 %copy-start.2 = (bf16[384,1152]{1,0:T(8,128)(2,1)}, bf16[384,1152]{1,0:T(8,128)(2,1)S(1)}, u32[]{:S(2)}) copy-start(bf16[384,1152]{1,0:T(8,128)(2,1)S(1)} %constant_dynamic-update-slice_fusion.2.refs_0_) | copy-start | bytes 2654212
  38.8 21.4 %collective-permute-start.13 = (bf16[384,1152]{1,0:T(8,128)(2,1)S(1)}, bf16[384,1152]{1,0:T(8,128)(2,1)S(1)}, u32[]{:S(2)}, u32[]{:S(2)}) collective-permute-start(bf16[384,1152]{1,0:T(8,128)(2,1)S(1)} %constant_dynamic-update-slice_fusion.2.refs_0_), channel_id=1, source_target_pairs={{0,8},{4,12},{8,0},{12,4},{16,24},{20,28},{24,16},{28,20},{1,9},{5... | collective-permute-start | bytes 2654216 | tf_op jit(solution)/shard_map/ppermute | solution.py:265
  39.5 31.8 %collective-permute-start.14 = (bf16[384,1152]{1,0:T(8,128)(2,1)S(1)}, bf16[384,1152]{1,0:T(8,128)(2,1)}, u32[]{:S(2)}, u32[]{:S(2)}) collective-permute-start(bf16[384,1152]{1,0:T(8,128)(2,1)S(1)} %constant_dynamic-update-slice_fusion.2.refs_0_), channel_id=1, source_target_pairs={{0,16},{4,20},{8,24},{12,28},{16,0},{20,4},{24,8},{28,12},{1,17},{... | collective-permute-start | bytes 2654216 | tf_op jit(solution)/shard_map/ppermute | solution.py:265
  40.4 39.7 %collective-permute-start.15 = (bf16[384,1152]{1,0:T(8,128)(2,1)S(1)}, bf16[384,1152]{1,0:T(8,128)(2,1)}, u32[]{:S(2)}, u32[]{:S(2)}) collective-permute-start(bf16[384,1152]{1,0:T(8,128)(2,1)S(1)} %constant_dynamic-update-slice_fusion.2.refs_0_), channel_id=1, source_target_pairs={{0,24},{4,28},{8,16},{12,20},{16,8},{20,12},{24,0},{28,4},{1,25},{... | collective-permute-start | bytes 2654216 | tf_op jit(solution)/shard_map/ppermute | solution.py:265
  41.6 1.0 copy-start.13
  41.6 3.3 %collective-permute-start.18 = (bf16[128,1152]{1,0:T(8,128)(2,1)S(1)}, bf16[128,1152]{1,0:T(8,128)(2,1)S(1)}, u32[]{:S(2)}, u32[]{:S(2)}) collective-permute-start(bf16[128,1152]{1,0:T(8,128)(2,1)S(1)} %copy-done.12), channel_id=1, source_target_pairs={{0,4},{4,0},{8,12},{12,8},{16,20},{20,16},{24,28},{28,24},{1,5},{5... | collective-permute-start | bytes 884744 | tf_op jit(solution)/shard_map/ppermute | solution.py:265
  43.3 2.3 %collective-permute-start.19 = (bf16[128,1152]{1,0:T(8,128)(2,1)}, bf16[128,1152]{1,0:T(8,128)(2,1)}, u32[]{:S(2)}, u32[]{:S(2)}) collective-permute-start(bf16[128,1152]{1,0:T(8,128)(2,1)} %collective-permute-done.5.refs_6_), channel_id=1, source_target_pairs={{0,4},{4,0},{8,12},{12,8},{16,20},{20,16},{24,28},{28,24},{1,5},{5... | collective-permute-start | bytes 884744 | tf_op jit(solution)/shard_map/ppermute | solution.py:265
  45.6 37.0 %collective-permute-start.10 = (bf16[256,1152]{1,0:T(8,128)(2,1)}, bf16[256,1152]{1,0:T(8,128)(2,1)S(1)}, u32[]{:S(2)}, u32[]{:S(2)}) collective-permute-start(bf16[256,1152]{1,0:T(8,128)(2,1)} %get-tuple-element.58), channel_id=1, source_target_pairs={{0,2},{1,3},{2,0},{3,1},{4,6},{5,7},{6,4},{7,5},{8,10},{9,11},{10,... | collective-permute-start | bytes 1769480 | tf_op jit(solution)/shard_map/ppermute | solution.py:265
  45.6 51.5 %collective-permute-start.11 = (bf16[256,1152]{1,0:T(8,128)(2,1)}, bf16[256,1152]{1,0:T(8,128)(2,1)}, u32[]{:S(2)}, u32[]{:S(2)}) collective-permute-start(bf16[256,1152]{1,0:T(8,128)(2,1)} %get-tuple-element.58), channel_id=1, source_target_pairs={{0,3},{1,2},{2,1},{3,0},{4,7},{5,6},{6,5},{7,4},{8,11},{9,10},{10,... | collective-permute-start | bytes 1769480 | tf_op jit(solution)/shard_map/ppermute | solution.py:265
  60.2 20.8 %copy-start.4 = (bf16[384,1152]{1,0:T(8,128)(2,1)}, bf16[384,1152]{1,0:T(8,128)(2,1)S(1)}, u32[]{:S(2)}) copy-start(bf16[384,1152]{1,0:T(8,128)(2,1)S(1)} %collective-permute-done.13.refs_2_) | copy-start | bytes 2654212
  60.2 38.8 %collective-permute-start.24 = (bf16[256,1152]{1,0:T(8,128)(2,1)S(1)}, bf16[256,1152]{1,0:T(8,128)(2,1)S(1)}, u32[]{:S(2)}, u32[]{:S(2)}) collective-permute-start(bf16[256,1152]{1,0:T(8,128)(2,1)S(1)} %get-tuple-element.57), channel_id=1, source_target_pairs={{0,1},{1,0},{2,3},{3,2},{4,5},{5,4},{6,7},{7,6},{8,9},{9,8},{10,11... | collective-permute-start | bytes 1769480 | tf_op jit(solution)/shard_map/ppermute | solution.py:265
  80.2 20.8 %collective-permute-start.20 = (bf16[384,1152]{1,0:T(8,128)(2,1)S(1)}, bf16[384,1152]{1,0:T(8,128)(2,1)S(1)}, u32[]{:S(2)}, u32[]{:S(2)}) collective-permute-start(bf16[384,1152]{1,0:T(8,128)(2,1)S(1)} %constant_dynamic-update-slice_fusion.2.refs_0_), channel_id=1, source_target_pairs={{0,4},{4,0},{8,12},{12,8},{16,20},{20,16},{24,28},{28,24},{1,5},{5... | collective-permute-start | bytes 2654216 | tf_op jit(solution)/shard_map/ppermute | solution.py:265
  81.0 19.9 %collective-permute-start.21 = (bf16[384,1152]{1,0:T(8,128)(2,1)S(1)}, bf16[384,1152]{1,0:T(8,128)(2,1)S(1)}, u32[]{:S(2)}, u32[]{:S(2)}) collective-permute-start(bf16[384,1152]{1,0:T(8,128)(2,1)S(1)} %collective-permute-done.13.refs_2_), channel_id=1, source_target_pairs={{0,4},{4,0},{8,12},{12,8},{16,20},{20,16},{24,28},{28,24},{1,5},{5... | collective-permute-start | bytes 2654216 | tf_op jit(solution)/shard_map/ppermute | solution.py:265
  82.6 18.3 %collective-permute-start.22 = (bf16[384,1152]{1,0:T(8,128)(2,1)}, bf16[384,1152]{1,0:T(8,128)(2,1)S(1)}, u32[]{:S(2)}, u32[]{:S(2)}) collective-permute-start(bf16[384,1152]{1,0:T(8,128)(2,1)} %collective-permute-done.14.refs_4_), channel_id=1, source_target_pairs={{0,4},{4,0},{8,12},{12,8},{16,20},{20,16},{24,28},{28,24},{1,5},{5... | collective-permute-start | bytes 2654216 | tf_op jit(solution)/shard_map/ppermute | solution.py:265
  97.1 3.9 %collective-permute-start.23 = (bf16[384,1152]{1,0:T(8,128)(2,1)}, bf16[384,1152]{1,0:T(8,128)(2,1)S(1)}, u32[]{:S(2)}, u32[]{:S(2)}) collective-permute-start(bf16[384,1152]{1,0:T(8,128)(2,1)} %collective-permute-done.15.refs_6_), channel_id=1, source_target_pairs={{0,4},{4,0},{8,12},{12,8},{16,20},{20,16},{24,28},{28,24},{1,5},{5... | collective-permute-start | bytes 2654216 | tf_op jit(solution)/shard_map/ppermute | solution.py:265
  99.1 1.9 copy-start.1
  100.9 1.0 copy-start.5
  100.9 1.2 copy-start.6
  101.0 1.4 copy-start.7
  130.6 13.7 %copy-start.21 = (bf16[2304,512]{1,0:T(8,128)(2,1)S(1)}, bf16[2304,512]{1,0:T(8,128)(2,1)}, u32[]{:S(2)}) copy-start(bf16[2304,512]{1,0:T(8,128)(2,1)} %get-tuple-element.51.refs_2_.refs_6_) | copy-start | bytes 7077892
  130.6 14.8 %copy-start.3 = (bf16[512,1152]{1,0:T(8,128)(2,1)S(1)}, bf16[512,1152]{1,0:T(8,128)(2,1)}, u32[]{:S(2)}) copy-start(bf16[512,1152]{1,0:T(8,128)(2,1)} %get-tuple-element.47) | copy-start | bytes 3538948
  144.3 10.3 %collective-permute-start.25 = (bf16[2304,512]{1,0:T(8,128)(2,1)}, bf16[2304,512]{1,0:T(8,128)(2,1)}, u32[]{:S(2)}, u32[]{:S(2)}) collective-permute-start(bf16[2304,512]{1,0:T(8,128)(2,1)} %get-tuple-element.50.refs_0_.refs_4_), channel_id=1, source_target_pairs={{0,4},{4,0},{8,12},{12,8},{16,20},{20,16},{24,28},{28,24},{1,5},{5... | collective-permute-start | bytes 7077896 | tf_op jit(solution)/shard_map/ppermute | solution.py:265
  144.4 10.3 %collective-permute-start.26 = (bf16[2304,512]{1,0:T(8,128)(2,1)S(1)}, bf16[2304,512]{1,0:T(8,128)(2,1)}, u32[]{:S(2)}, u32[]{:S(2)}) collective-permute-start(bf16[2304,512]{1,0:T(8,128)(2,1)S(1)} %copy-done.21), channel_id=1, source_target_pairs={{0,4},{4,0},{8,12},{12,8},{16,20},{20,16},{24,28},{28,24},{1,5},{5... | collective-permute-start | bytes 7077896 | tf_op jit(solution)/shard_map/ppermute | solution.py:265
  175.3 25.2 %collective-permute-start.28 = (bf16[256,1152]{1,0:T(8,128)(2,1)}, bf16[256,1152]{1,0:T(8,128)(2,1)S(1)}, u32[]{:S(2)}, u32[]{:S(2)}) collective-permute-start(bf16[256,1152]{1,0:T(8,128)(2,1)} %finish.3), channel_id=1, source_target_pairs={{0,1},{3,6},{1,3},{2,4},{4,0},{7,7},{5,2},{6,5},{8,9},{11,14},{9,1... | collective-permute-start | bytes 1769480 | tf_op jit(solution)/shard_map/ppermute | solution.py:356
  197.8 14.8 %collective-permute-start.27 = (bf16[256,1152]{1,0:T(8,128)(2,1)}, bf16[256,1152]{1,0:T(8,128)(2,1)S(1)}, u32[]{:S(2)}, u32[]{:S(2)}) collective-permute-start(bf16[256,1152]{1,0:T(8,128)(2,1)} %finish.2), channel_id=1, source_target_pairs={{0,0},{3,7},{1,2},{2,5},{4,1},{7,6},{5,3},{6,4},{8,8},{11,15},{9,1... | collective-permute-start | bytes 1769480 | tf_op jit(solution)/shard_map/ppermute | solution.py:356
  (3 other events, 2.4 us)

commit v3 on v2

v3 whole, which is shorter than its diff:
```python
import functools
import math

import jax
import jax.numpy as jnp
from jax import lax
from jax.experimental import pallas as pl
from jax.experimental.pallas import tpu as pltpu
from jax.sharding import PartitionSpec as P

HEADS = 16
F32 = jnp.float32
BF16 = jnp.bfloat16
MIB = 2**20


def contract(a, b, dims):
    return lax.dot_general(a, b, (dims, ((), ())), preferred_element_type=F32)


VMEM = pl.BlockSpec(memory_space=pltpu.VMEM)
HBM = pl.BlockSpec(memory_space=pltpu.HBM)


def pick_kernel(bases, block, idx_ref, *refs):
    pieces, (out_ref, rows_ref) = refs[:-2], refs[-2:]
    acc_ref = None
    if len(pieces) > len(bases):
        acc_ref, pieces = pieces[0], pieces[1:]
    rows = pieces[0].shape[0]
    for n, piece in enumerate(pieces):
        rows_ref[n * rows : (n + 1) * rows, :] = piece[...]
    lane = lax.broadcasted_iota(jnp.int32, (1, rows), 1)
    for lo in range(0, out_ref.shape[0], block):
        span = slice(lo, lo + block)
        idx = idx_ref[span, :]
        hot = jnp.concatenate(
            [jnp.where(idx == lane + base, 1.0, 0.0).astype(BF16) for base in bases], axis=1
        )
        picked = contract(hot, rows_ref[...], ((1,), (0,)))
        if acc_ref is not None:
            picked = picked + acc_ref[span, :].astype(F32)
        out_ref[span, :] = picked.astype(BF16)


def pick_rows(idx, acc, pieces, bases, block):
    rows, width = pieces[0].shape
    return pl.pallas_call(
        functools.partial(pick_kernel, bases, block),
        in_specs=[VMEM] * (1 + len(acc) + len(pieces)),
        out_specs=VMEM,
        out_shape=jax.ShapeDtypeStruct((idx.shape[0], width), BF16),
        scratch_shapes=[pltpu.VMEM((len(pieces) * rows, width), BF16)],
        input_output_aliases={1: 0} if acc else {},
        compiler_params=pltpu.CompilerParams(vmem_limit_bytes=16 * MIB),
        cost_estimate=pl.CostEstimate(flops=1, bytes_accessed=1, transcendentals=0),
        name="pick",
    )(idx, *acc, *pieces)


def stretch_kernel(steps, act_ref, wa_ref, ba_ref, tok_ref, wq_ref, kv_ref, x_ref, *scratch):
    tok_buf, wq_buf, silu_ref, mods_ref, sems = scratch
    count, width = x_ref.shape
    cols = wa_ref.shape[1]
    i = pl.program_id(0)
    tok_copy = pltpu.make_async_copy(tok_ref, tok_buf, sems.at[0])
    wq_copies = [
        pltpu.make_async_copy(
            wq_ref.at[:, k * width : (k + 1) * width], wq_buf.at[k - 1], sems.at[k]
        )
        for k in (1, 2)
    ]
    blocks = [slice(lo, lo + 256) for lo in range(0, count, 256)]

    @pl.when(i == 0)
    def _():
        tok_copy.start()
        for copy in wq_copies:
            copy.start()
        for span in blocks:
            silu_ref[span, :] = jax.nn.silu(act_ref[span, :].astype(F32)).astype(BF16)

    for k in range(steps):

        @pl.when(i == k)
        def _():
            mods = contract(silu_ref[...], wa_ref[...], ((1,), (0,))) + ba_ref[...]
            mods_ref[:, k * cols : (k + 1) * cols] = mods.astype(BF16)

    @pl.when(i == steps - 1)
    def _():
        tok_copy.wait()
        for span in blocks:
            values = tok_buf[span, :].astype(F32)
            moved = values - jnp.mean(values, axis=1, keepdims=True)
            spread = jnp.mean(moved * moved, axis=1, keepdims=True)
            normed = moved * lax.rsqrt(spread + 1e-06)
            shift, scale = mods_ref[span, :width], mods_ref[span, width:]
            x_ref[span, :] = (normed * (1.0 + scale.astype(F32)) + shift.astype(F32)).astype(BF16)

    for k, copy in enumerate(wq_copies):

        @pl.when(i == steps + k)
        def _():
            copy.wait()
            kv_ref[...] = contract(wq_buf[k], x_ref[...], ((0,), (1,))).astype(BF16)


def stretch(tok, picked, w_ada, b_ada, w_qkv):
    count, width = tok.shape
    steps = 3
    cols = 2 * width // steps

    def ada(i):
        return jnp.minimum(i, steps - 1)

    return pl.pallas_call(
        functools.partial(stretch_kernel, steps),
        grid=(steps + 2,),
        in_specs=[
            pl.BlockSpec((count, width), lambda i: (0, 0), pipeline_mode=pl.Buffered(1)),
            pl.BlockSpec((width, cols), lambda i: (0, ada(i))),
            pl.BlockSpec((1, cols), lambda i: (0, ada(i))),
            HBM,
            HBM,
        ],
        out_specs=[
            pl.BlockSpec((width, count), lambda i: (jnp.maximum(i - steps, 0), 0)),
            pl.BlockSpec((count, width), lambda i: (0, 0), pipeline_mode=pl.Buffered(1)),
        ],
        out_shape=[
            jax.ShapeDtypeStruct((2 * width, count), BF16),
            jax.ShapeDtypeStruct((count, width), BF16),
        ],
        scratch_shapes=[
            pltpu.VMEM((count, width), BF16),
            pltpu.VMEM((2, width, width), BF16),
            pltpu.VMEM((count, width), BF16),
            pltpu.VMEM((count, 2 * width), BF16),
            pltpu.SemaphoreType.DMA((3,)),
        ],
        compiler_params=pltpu.CompilerParams(vmem_limit_bytes=58 * MIB),
        cost_estimate=pl.CostEstimate(flops=1, bytes_accessed=1, transcendentals=0),
        name="stretch",
    )(picked, w_ada, b_ada, tok, w_qkv)


def query_kernel(query_scale, place_ref, act_ref, x_ref, ba_ref, wa_ref, wq_ref, *refs):
    q_ref, gate_ref, wa_buf, wq_buf, sems = refs
    count, width = gate_ref.shape
    copies = [
        pltpu.make_async_copy(wq_ref.at[:, :width], wq_buf, sems.at[0]),
        pltpu.make_async_copy(wa_ref.at[:, 2 * width :], wa_buf, sems.at[1]),
    ]
    for copy in copies:
        copy.start()
    mine = pl.ds(pl.multiple_of(place_ref[0] * count, count), count)
    act = jax.nn.silu(act_ref[mine, :].astype(F32)).astype(BF16)
    copies[0].wait()
    q_ref[...] = (contract(wq_buf[...], x_ref[mine, :], ((0,), (1,))) * query_scale).astype(BF16)
    copies[1].wait()
    gate = contract(act, wa_buf[...], ((1,), (0,))) + ba_ref[:, 2 * width :]
    gate_ref[...] = gate.astype(BF16)


def query(place, x, picked, w_ada, b_ada, w_qkv, count):
    width = x.shape[1]
    query_scale = math.log2(math.e) / math.sqrt(width // HEADS)
    return pl.pallas_call(
        functools.partial(query_kernel, query_scale),
        in_specs=[pl.BlockSpec(memory_space=pltpu.SMEM), VMEM, VMEM, VMEM, HBM, HBM],
        out_specs=[VMEM, VMEM],
        out_shape=[
            jax.ShapeDtypeStruct((width, count), BF16),
            jax.ShapeDtypeStruct((count, width), BF16),
        ],
        scratch_shapes=[
            pltpu.VMEM((width, width), BF16),
            pltpu.VMEM((width, width), BF16),
            pltpu.SemaphoreType.DMA((2,)),
        ],
        compiler_params=pltpu.CompilerParams(vmem_limit_bytes=58 * MIB),
        cost_estimate=pl.CostEstimate(flops=1, bytes_accessed=1, transcendentals=0),
        name="query",
    )(place, picked, x, b_ada, w_ada, w_qkv)


def attend_kernel(head_dim, chunk, place_ref, q_ref, *refs):
    kv_refs, (o_ref, s_ref) = refs[:-2], refs[-2:]
    pair, queries = q_ref.shape
    row = lax.broadcasted_iota(jnp.int32, (pair, 1), 0)
    q = q_ref[...]
    zero = jnp.zeros_like(q)
    both = jnp.concatenate(
        [jnp.where(row < head_dim, q, zero), jnp.where(row < head_dim, zero, q)], axis=1
    )
    half = len(kv_refs) // 2
    parts = [
        (k_ref, v_ref, i)
        for k_ref, v_ref in zip(kv_refs[:half], kv_refs[half:])
        for i in range(0, k_ref.shape[1], chunk)
    ]
    top = None
    for n, (k_ref, _, i) in enumerate(parts):
        scores = contract(k_ref[:, i : i + chunk], both, ((0,), (0,)))
        s_ref[n * chunk : (n + 1) * chunk, :] = scores
        peak = jnp.max(scores, axis=0, keepdims=True)
        top = peak if top is None else jnp.maximum(top, peak)
    weighted = denominator = None
    for n, (_, v_ref, i) in enumerate(parts):
        expo = jnp.exp2(s_ref[n * chunk : (n + 1) * chunk, :] - top)
        total = jnp.sum(expo, axis=0, keepdims=True)
        part = contract(v_ref[:, i : i + chunk], expo.astype(BF16), ((1,), (0,)))
        weighted = part if weighted is None else weighted + part
        denominator = total if denominator is None else denominator + total
    result = weighted / denominator
    o_ref[...] = jnp.where(row < head_dim, result[:, :queries], result[:, queries:]).astype(BF16)


def attend(place, which, qt, kvs):
    width, queries = qt.shape[0], qt.shape[1] // 2
    keys = kvs[0].shape[1]
    head_dim = width // HEADS
    pair, pairs = 2 * head_dim, HEADS // 2
    chunk = math.gcd(keys, 512)
    k_spec = pl.BlockSpec((pair, keys), lambda p, place: (p, 0))
    v_spec = pl.BlockSpec((pair, keys), lambda p, place: (p + pairs, 0))
    total = len(kvs) * keys
    return pl.pallas_call(
        functools.partial(attend_kernel, head_dim, chunk),
        grid_spec=pltpu.PrefetchScalarGridSpec(
            num_scalar_prefetch=1,
            grid=(pairs,),
            in_specs=[pl.BlockSpec((pair, queries), lambda p, place: (p, place[which]))]
            + [k_spec] * len(kvs)
            + [v_spec] * len(kvs),
            out_specs=pl.BlockSpec((pair, queries), lambda p, place: (p, 0)),
            scratch_shapes=[pltpu.VMEM((total, 2 * queries), F32)],
        ),
        out_shape=jax.ShapeDtypeStruct((width, queries), BF16),
        compiler_params=pltpu.CompilerParams(vmem_limit_bytes=16 * MIB),
        cost_estimate=pl.CostEstimate(
            flops=16 * total * queries * width,
            bytes_accessed=4 * total * width,
            transcendentals=HEADS * total * queries,
        ),
        name="attend",
    )(place, qt, *kvs, *kvs)


def finish_kernel(place_ref, att_ref, tok_ref, gate_ref, w_ref, o_ref):
    projected = contract(att_ref[...], w_ref[...], ((0,), (0,)))
    o_ref[...] = (tok_ref[...].astype(F32) + gate_ref[...].astype(F32) * projected).astype(BF16)


def finish(place, which, attended, tok, gate, w_out):
    width, queries = attended.shape
    at = pl.BlockSpec((queries, width), lambda i, place: (place[which], 0))
    tok_at = pl.BlockSpec((queries, width), lambda i, place: (2 * place[0] + place[which], 0))
    return pl.pallas_call(
        finish_kernel,
        grid_spec=pltpu.PrefetchScalarGridSpec(
            num_scalar_prefetch=1,
            grid=(1,),
            in_specs=[
                pl.BlockSpec((width, queries), lambda i, place: (0, 0)),
                tok_at,
                at,
                pl.BlockSpec((width, width), lambda i, place: (0, 0)),
            ],
            out_specs=pl.BlockSpec((queries, width), lambda i, place: (0, 0)),
        ),
        out_shape=jax.ShapeDtypeStruct((queries, width), BF16),
        compiler_params=pltpu.CompilerParams(vmem_limit_bytes=12 * MIB),
        name="finish",
    )(place, attended, tok, gate, w_out)


def swap(x, axis, bits):
    return lax.ppermute(x, axis, [(i, i ^ bits) for i in range(lax.axis_size(axis))])


def after(x, *others):
    return lax.optimization_barrier((x, others))[0]


def to_chips(own):
    return {o: swap(own, "region", o) if o else own for o in range(0, lax.axis_size("region"), 2)}


def to_cores(blocks):
    both = blocks | {o ^ 1: swap(b, "region", 1) for o, b in blocks.items()}
    return [both[o] for o in range(len(both))]


def per_device(
    tokens, element_ids, element_slot, live_count, cond_table, w_ada, b_ada, w_qkv, w_out
):
    device_tokens = tokens[0]
    tok_rows, width = device_tokens.shape
    elem_rows = cond_table.shape[0]
    size, n = lax.axis_size("region"), lax.axis_size("ctx")
    h = n // 2
    block = tok_rows // 2
    r, c = lax.axis_index("region"), lax.axis_index("ctx")
    core, upper = r % 2, (c >= h).astype(jnp.int32)
    m = jnp.where(upper == 1, n - 1 - c, c)

    tables = [swap(cond_table, "ctx", d) for d in range(1, n)]
    near = to_chips(after(cond_table, tables[0]))
    mine = lax.dynamic_slice_in_dim(device_tokens, core * block, block)
    other = lax.dynamic_slice_in_dim(device_tokens, (1 - core) * block, block)
    got = swap(other, "region", 1)
    position = jnp.arange(tok_rows, dtype=jnp.int32)
    ids = jnp.where(position < live_count[0, 0], element_ids[0], -1)
    ids = after(ids, tables[0])
    ids = lax.all_to_all(
        jnp.broadcast_to(ids, (n, tok_rows)), "ctx", split_axis=0, concat_axis=0, tiled=True
    )
    tables, near, mine, got = lax.optimization_barrier((tables, near, mine, got))

    far = to_chips(jnp.concatenate(tables, axis=0))
    even, odd = jnp.where(core == 0, mine, got), jnp.where(core == 0, got, mine)
    work, pass_on = jnp.where(upper == 0, even, odd), jnp.where(upper == 0, odd, even)
    same = (jnp.arange(n) >= h).astype(jnp.int32) == upper
    sent = jnp.where(same[:, None, None], work[None], pass_on[None])
    tok = lax.all_to_all(sent, "ctx", split_axis=0, concat_axis=0, tiled=True)
    tok = tok.reshape(n * block, width)

    ids = jnp.where(core == upper, ids, swap(ids, "region", 1))
    ids = lax.dynamic_slice_in_dim(ids, core * block, block, axis=1).reshape(n * block, 1)
    slots = element_slot[jnp.maximum(ids, 0)]
    owner = slots // elem_rows
    relative = ((((owner // n) ^ r) * n) + ((owner % n) ^ c)) * elem_rows + slots % elem_rows
    relative = jnp.where(ids < 0, -1, relative)

    def pick(picked, chips, d):
        order = list(chips) + [o ^ 1 for o in chips]
        pieces = list(chips.values()) + [swap(b, "region", 1) for b in chips.values()]
        bases = [(o * n + d) * elem_rows for o in order]
        return pick_rows(relative, picked, pieces, bases, 2 * block)

    picked = pick([], near, 0)
    far, picked = lax.optimization_barrier((far, picked))
    first = {o: far[o] for o in far if o < size // 2}
    second = {o: far[o] for o in far if o >= size // 2}
    picked = pick([picked], first, 1)
    picked = pick([picked], second, 1)
    tok = after(tok, picked)

    base = jnp.where(upper == 1, n - 2 - 2 * m, 2 * m)
    place = jnp.stack([base // 2, core ^ upper, 1 - core ^ upper]).astype(jnp.int32)
    bias = b_ada.reshape(1, -1)
    kv, x = stretch(tok, picked, w_ada, bias, w_qkv)
    kvs = [kv, swap(kv, "region", 1)]
    qt, gate = query(place, x, picked, w_ada, bias, w_qkv, 2 * block)

    home = []
    for which in (1, 2):
        attended = attend(place, which, qt, kvs)
        if home:
            attended = after(attended, home[0])
        result = finish(place, which, attended, tok, gate, w_out)
        pairs = []
        for region in range(size):
            for k in range(h):
                to = 2 * k + (region % 2 if which == 1 else 1 - region % 2)
                pairs.append((region * n + k, (region & ~1) * n + to))
                pairs.append((region * n + n - 1 - k, (region | 1) * n + n - 1 - to))
        home.append(lax.ppermute(result, ("region", "ctx"), pairs))
    number = jnp.where(core == 1, n - 1 - c, c) % 2
    low, high = jnp.where(number == 0, home[0], home[1]), jnp.where(number == 0, home[1], home[0])
    return jnp.concatenate([low, high], axis=0)[None]


def solution(mesh):
    placed = (
        P("region", "ctx", None),
        P("region", "ctx"),
        P(),
        P("region", "ctx"),
        P(("region", "ctx"), None),
        P(),
        P(),
        P(),
        P(),
    )
    return jax.shard_map(
        per_device, mesh=mesh, in_specs=placed, out_specs=P("region", "ctx", None), check_vma=False
    )
```

time: 218 us -> 189 us (0.87)
  the two profiles are of different devices: /device:TPU:17 before, /device:TPU:1 now
where the time goes in v3:
time: 189 us; the launch traced here: 188 us
  Pallas kernels  79.3 us (42%)
  waiting for transfers between devices  46.7 us (25%)
  starting transfers between devices  36.7 us (19%)
  local copies, waits for them, and re-layouts  18.5 us (10%)
  other arithmetic  6.04 us (3%)
    ppermute x20, waiting for transfers between devices, swap(): lax.ppermute(x, axis, [(i, i ^ bits) for i in range(lax.axis_size(axis))])  30.5 us
    pallas_call x2, Pallas kernels, attend(): pl.pallas_call(functools.partial(attend_kernel, head_dim, chunk), grid_sp...  29.4 us
    ppermute x20, starting transfers between devices, swap(): lax.ppermute(x, axis, [(i, i ^ bits) for i in range(lax.axis_size(axis))])  20.5 us
    pallas_call x1, Pallas kernels, stretch(): pl.pallas_call(functools.partial(stretch_kernel, steps), grid=(steps + 2,...  20.4 us
    ppermute x2, waiting for transfers between devices, per_device(): home.append(lax.ppermute(result, ('region', 'ctx'), pairs))  16.2 us
    pallas_call x3, Pallas kernels, pick_rows(): pl.pallas_call(functools.partial(pick_kernel, bases, block), in_specs=[VM...  14.4 us
    pallas_call x1, Pallas kernels, query(): pl.pallas_call(functools.partial(query_kernel, query_scale), in_specs=[pl...  9.69 us
    unnamed x46, local copies, waits for them, and re-layouts  8.6 us
  transfers between devices with their start and end apart: 24, of which 8 were waited for; matrix products, arithmetic and copies ran while one was open for 8% of the time, Pallas kernels for 21%

profile of v3, /device:TPU:1, one launch (start us, length us, event | category | flops | bytes accessed | tf_op | source)
XLA Modules:
  0.0 188.3 jit_solution(9219144076268998638)
XLA Ops:
  0.0 3.1 %collective-permute-start.2 = (bf16[128,1152]{1,0:T(8,128)(2,1)}, bf16[128,1152]{1,0:T(8,128)(2,1)S(1)}, u32[]{:S(2)}, u32[]{:S(2)}) collective-permute-start(bf16[128,1152]{1,0:T(8,128)(2,1)} %refs_0_), channel_id=1, source_target_pairs={{0,2},{1,3},{2,0},{3,1},{4,6},{5,7},{6,4},{7,5},{8,10},{9,11},{10,... | collective-permute-start | bytes 884744 | tf_op jit(solution)/shard_map/ppermute | solution.py:280
  3.1 1.3 collective-permute-start
  4.4 1.3 dynamic-slice_bitcast_fusion
  5.8 1.3 collective-permute-start.7
  7.7 7.8 %collective-permute-done = bf16[128,1152]{1,0:T(8,128)(2,1)S(1)} collective-permute-done((bf16[128,1152]{1,0:T(8,128)(2,1)}, bf16[128,1152]{1,0:T(8,128)(2,1)S(1)}, u32[]{:S(2)}, u32[]{:S(2)}) %collective-permute-start) | collective-permute-done | bytes 294944 | tf_op jit(solution)/shard_map/ppermute | solution.py:280
  15.5 2.2 %collective-permute-start.6 = (bf16[128,1152]{1,0:T(8,128)(2,1)S(1)}, bf16[128,1152]{1,0:T(8,128)(2,1)S(1)}, u32[]{:S(2)}, u32[]{:S(2)}) collective-permute-start(bf16[128,1152]{1,0:T(8,128)(2,1)S(1)} %copy-done.4), channel_id=1, source_target_pairs={{0,24},{4,28},{8,16},{12,20},{16,8},{20,12},{24,0},{28,4},{1,25},{... | collective-permute-start | bytes 884744 | tf_op jit(solution)/shard_map/ppermute | solution.py:280
  18.2 0.6 fusion.14
  18.7 0.7 fusion.13
  19.4 0.6 broadcast_in_dim.43
  20.0 5.7 %all-to-all-start = ((s32[4,1,512]{2,1,0:T(1,128)}), s32[4,1,512]{2,1,0:T(1,128)}, u32[]{:S(2)}, u32[]{:S(2)}) async-start(s32[4,1,512]{2,1,0:T(1,128)} %broadcast_in_dim.43), calls=%async_computation | async-start | bytes 16384 | tf_op jit(solution)/shard_map/all_to_all | solution.py:317
  25.8 5.1 %collective-permute-done.5.refs_2_ = bf16[128,1152]{1,0:T(8,128)(2,1)S(1)} collective-permute-done((bf16[128,1152]{1,0:T(8,128)(2,1)S(1)}, bf16[128,1152]{1,0:T(8,128)(2,1)S(1)}, u32[]{:S(2)}, u32[]{:S(2)}) %collective-permute-start.5) | collective-permute-done | bytes 294944 | tf_op jit(solution)/shard_map/ppermute | solution.py:280
  31.1 1.7 broadcast_select_fusion
  32.8 4.5 %all-to-all-start.1 = ((bf16[4,256,1152]{2,1,0:T(8,128)(2,1)}), bf16[4,256,1152]{2,1,0:T(8,128)(2,1)}, u32[]{:S(2)}, u32[]{:S(2)}) async-start(bf16[4,256,1152]{2,1,0:T(8,128)(2,1)} %broadcast_select_fusion), calls=%async_computation.1 | async-start | bytes 4718592 | tf_op jit(solution)/shard_map/all_to_all | solution.py:327
  37.4 1.0 constant_dynamic-update-slice_fusion.refs_1_
  38.4 1.5 collective-permute-start.10
  39.9 1.5 collective-permute-start.9
  41.5 0.7 copy.27
  42.2 5.8 %collective-permute-start.1 = (s32[4,512]{1,0:T(4,128)S(1)}, s32[4,512]{1,0:T(4,128)S(1)}, u32[]{:S(2)}, u32[]{:S(2)}) collective-permute-start(s32[4,512]{1,0:T(4,128)S(1)} %bitcast.26), channel_id=1, source_target_pairs={{0,4},{4,0},{8,12},{12,8},{16,20},{20,16},{24,28},{28,24},{1,5},{5... | collective-permute-start | bytes 24584 | tf_op jit(solution)/shard_map/ppermute | solution.py:280
  47.9 0.8 collective-permute-done.1
  49.7 6.2 %gather_fusion = s32[1024]{0:T(1024)S(1)} fusion(s32[4096]{0:T(1024)S(1)} %copy-done, s32[1024]{0:T(1024)S(1)} %broadcast_clamp_fusion), kind=kCustom, calls=%fused_computation | custom fusion | bytes 12288 | tf_op jit(solution)/shard_map/gather | solution.py:332
  56.7 1.0 fusion.5.idx_ref
  58.2 1.0 copy-done.6
  59.1 1.0 copy-done.8
  60.1 1.0 copy-done.10
  61.1 1.0 copy-done.12
  62.0 1.0 copy-done.14
  63.0 3.0 %pick.3.refs_0_ = bf16[1024,1152]{1,0:T(8,128)(2,1)S(1)} custom-call(s32[1024,1]{1,0:T(8,128)S(1)} %fusion.5.idx_ref, bf16[128,1152]{1,0:T(8,128)(2,1)S(1)} %copy-done.4, bf16[128,1152]{1,0:T(8,128)(2,1)S(1)} %copy-done.10, bf16[128,1152]{1,0:T(8,128)(2,1)S(1)} %copy-done.8, bf16[128,1152]{1,0:T(8,128)(2,1)S(1)} %copy-done.6, ...), custom_call_target="tpu_custom_call" | custom-call | flops 1 | bytes 1 | tf_op jit(solution)/shard_map/pick/pallas_call | solution.py:48
  66.0 14.1 %collective-permute-done.9.refs_1_ = bf16[384,1152]{1,0:T(8,128)(2,1)} collective-permute-done((bf16[384,1152]{1,0:T(8,128)(2,1)S(1)}, bf16[384,1152]{1,0:T(8,128)(2,1)}, u32[]{:S(2)}, u32[]{:S(2)}) %collective-permute-start.9) | collective-permute-done | bytes 884768 | tf_op jit(solution)/shard_map/ppermute | solution.py:280
  80.0 1.2 collective-permute-start.15
  81.2 0.5 collective-permute-start.17
  81.7 0.6 reshape.277.ba_ref
  82.3 2.2 %collective-permute-done.15.refs_3_ = bf16[384,1152]{1,0:T(8,128)(2,1)S(1)} collective-permute-done((bf16[384,1152]{1,0:T(8,128)(2,1)S(1)}, bf16[384,1152]{1,0:T(8,128)(2,1)S(1)}, u32[]{:S(2)}, u32[]{:S(2)}) %collective-permute-start.15) | collective-permute-done | bytes 884768 | tf_op jit(solution)/shard_map/ppermute | solution.py:280
  84.7 5.6 %pick.4.refs_0_ = bf16[1024,1152]{1,0:T(8,128)(2,1)S(1)} custom-call(s32[1024,1]{1,0:T(8,128)S(1)} %fusion.5.idx_ref, bf16[1024,1152]{1,0:T(8,128)(2,1)S(1)} %pick.3.refs_0_, bf16[384,1152]{1,0:T(8,128)(2,1)S(1)} %constant_dynamic-update-slice_fusion.refs_1_, bf16[384,1152]{1,0:T(8,128)(2,1)} %collective-permute-done.8.refs_2_, ...), custom_call_target="tpu_custom_call", output_to_operand_aliasing={{}: (1, {})} | custom-call | flops 1 | bytes 1 | tf_op jit(solution)/shard_map/pick/pallas_call | solution.py:48
  90.3 5.9 %pick.5.act_ref = bf16[1024,1152]{1,0:T(8,128)(2,1)S(1)} custom-call(s32[1024,1]{1,0:T(8,128)S(1)} %fusion.5.idx_ref, bf16[1024,1152]{1,0:T(8,128)(2,1)S(1)} %pick.4.refs_0_, bf16[384,1152]{1,0:T(8,128)(2,1)} %collective-permute-done.9.refs_1_, bf16[384,1152]{1,0:T(8,128)(2,1)} %collective-permute-done.10.refs_2_, ...), custom_call_target="tpu_custom_call", output_to_operand_aliasing={{}: (1, {})} | custom-call | flops 1 | bytes 1 | tf_op jit(solution)/shard_map/pick/pallas_call | solution.py:48
  96.2 1.4 copy-done.1
  97.7 20.4 %stretch.1 = (bf16[2304,1024]{1,0:T(8,128)(2,1)}, bf16[1024,1152]{1,0:T(8,128)(2,1)}) custom-call(bf16[1024,1152]{1,0:T(8,128)(2,1)} %copy-done.1, bf16[1152,3456]{1,0:T(8,128)(2,1)} %wa_ref.3, f32[1,3456]{1,0:T(1,128)} %reshape.277.ba_ref, bf16[1024,1152]{1,0:T(8,128)(2,1)} %bitcast.8.tok_ref, bf16[1152,3456]{1,0:T(8,128)(2,1)} %wq_ref.3), custom_call_target="tpu_custom_call" | custom-call | flops 1 | bytes 1 | tf_op jit(solution)/shard_map/stretch/pallas_call | solution.py:117
  118.1 0.4 collective-permute-start.19
  118.5 0.6 pad_add_fusion.place_ref
  119.1 9.7 %query.1 = (bf16[1152,512]{1,0:T(8,128)(2,1)}, bf16[512,1152]{1,0:T(8,128)(2,1)}) custom-call(s32[3]{0:T(128)} %pad_add_fusion.place_ref, bf16[1024,1152]{1,0:T(8,128)(2,1)} %copy-done.1, bf16[1024,1152]{1,0:T(8,128)(2,1)} %get-tuple-element.44.x_ref, f32[1,3456]{1,0:T(1,128)} %reshape.277.ba_ref, bf16[1152,3456]{1,0:T(8,128)(2,1)} %wa_ref.3, ...), custom_call_target="tpu_custom_call" | custom-call | flops 1 | bytes 1 | tf_op jit(solution)/shard_map/query/pallas_call | solution.py:169
  128.9 1.3 copy-done.17
  130.1 14.9 %attend.2.att_ref = bf16[1152,256]{1,0:T(8,128)(2,1)S(1)} custom-call(s32[3]{0:T(128)S(1)} %copy-done.15, bf16[1152,512]{1,0:T(8,128)(2,1)S(1)} %copy-done.17, bf16[2304,1024]{1,0:T(8,128)(2,1)S(1)} %copy-done.16, bf16[2304,1024]{1,0:T(8,128)(2,1)} %collective-permute-done.19.refs_1_.refs_3_, bf16[2304,1024]{1,0:T(8,128)(2,1)S(1)} %copy-done.16, ...), custom_call_target="tpu_custom_call" | custom-call | flops 9663676416 | bytes 9437184 | tf_op jit(solution)/shard_map/attend/pallas_call | solution.py:229
  145.0 2.7 %finish.2 = bf16[256,1152]{1,0:T(8,128)(2,1)S(1)} custom-call(s32[3]{0:T(128)S(1)} %copy-done.15, bf16[1152,256]{1,0:T(8,128)(2,1)S(1)} %attend.2.att_ref, bf16[1024,1152]{1,0:T(8,128)(2,1)} %bitcast.8.tok_ref, bf16[512,1152]{1,0:T(8,128)(2,1)S(1)} %copy-done.3, bf16[1152,1152]{1,0:T(8,128)(2,1)S(1)} %copy-done.2), custom_call_target="tpu_custom_call" | custom-call | tf_op jit(solution)/shard_map/finish/pallas_call | solution.py:260
  147.7 4.0 %collective-permute-start.20 = (bf16[256,1152]{1,0:T(8,128)(2,1)S(1)}, bf16[256,1152]{1,0:T(8,128)(2,1)S(1)}, u32[]{:S(2)}, u32[]{:S(2)}) collective-permute-start(bf16[256,1152]{1,0:T(8,128)(2,1)S(1)} %finish.2), channel_id=1, source_target_pairs={{0,0},{3,7},{1,2},{2,5},{4,1},{7,6},{5,3},{6,4},{8,8},{11,15},{9,1... | collective-permute-start | bytes 1769480 | tf_op jit(solution)/shard_map/ppermute | solution.py:370
  151.7 14.6 %attend.3.att_ref = bf16[1152,256]{1,0:T(8,128)(2,1)S(1)} custom-call(s32[3]{0:T(128)S(1)} %copy-done.15, bf16[1152,512]{1,0:T(8,128)(2,1)S(1)} %copy-done.17, bf16[2304,1024]{1,0:T(8,128)(2,1)S(1)} %copy-done.16, bf16[2304,1024]{1,0:T(8,128)(2,1)} %collective-permute-done.19.refs_1_.refs_3_, bf16[2304,1024]{1,0:T(8,128)(2,1)S(1)} %copy-done.16, ...), custom_call_target="tpu_custom_call" | custom-call | flops 9663676416 | bytes 9437184 | tf_op jit(solution)/shard_map/attend/pallas_call | solution.py:229
  166.3 2.7 %finish.3 = bf16[256,1152]{1,0:T(8,128)(2,1)S(1)} custom-call(s32[3]{0:T(128)S(1)} %copy-done.15, bf16[1152,256]{1,0:T(8,128)(2,1)S(1)} %attend.3.att_ref, bf16[1024,1152]{1,0:T(8,128)(2,1)} %bitcast.8.tok_ref, bf16[512,1152]{1,0:T(8,128)(2,1)S(1)} %copy-done.3, bf16[1152,1152]{1,0:T(8,128)(2,1)S(1)} %copy-done.2), custom_call_target="tpu_custom_call" | custom-call | tf_op jit(solution)/shard_map/finish/pallas_call | solution.py:260
  168.9 1.9 %collective-permute-start.21 = (bf16[256,1152]{1,0:T(8,128)(2,1)S(1)}, bf16[256,1152]{1,0:T(8,128)(2,1)S(1)}, u32[]{:S(2)}, u32[]{:S(2)}) collective-permute-start(bf16[256,1152]{1,0:T(8,128)(2,1)S(1)} %finish.3), channel_id=1, source_target_pairs={{0,1},{3,6},{1,3},{2,4},{4,0},{7,7},{5,2},{6,5},{8,9},{11,14},{9,1... | collective-permute-start | bytes 1769480 | tf_op jit(solution)/shard_map/ppermute | solution.py:370
  170.9 16.2 %collective-permute-done.21 = bf16[256,1152]{1,0:T(8,128)(2,1)S(1)} collective-permute-done((bf16[256,1152]{1,0:T(8,128)(2,1)S(1)}, bf16[256,1152]{1,0:T(8,128)(2,1)S(1)}, u32[]{:S(2)}, u32[]{:S(2)}) %collective-permute-start.21) | collective-permute-done | bytes 589856 | tf_op jit(solution)/shard_map/ppermute | solution.py:370
  187.2 1.1 maximum_bitcast_fusion
  (72 shorter events, 3.3 us)
Async XLA Ops:
  0.0 49.7 %copy-start = (s32[4096]{0:T(1024)S(1)}, s32[4096]{0:T(1024)}, u32[]{:S(2)}) copy-start(s32[4096]{0:T(1024)} %param.11) | copy-start | bytes 49156
  0.0 7.1 %copy-start.4 = (bf16[128,1152]{1,0:T(8,128)(2,1)S(1)}, bf16[128,1152]{1,0:T(8,128)(2,1)}, u32[]{:S(2)}) copy-start(bf16[128,1152]{1,0:T(8,128)(2,1)} %refs_0_) | copy-start | bytes 884740
  0.0 17.9 %collective-permute-start.2 = (bf16[128,1152]{1,0:T(8,128)(2,1)}, bf16[128,1152]{1,0:T(8,128)(2,1)S(1)}, u32[]{:S(2)}, u32[]{:S(2)}) collective-permute-start(bf16[128,1152]{1,0:T(8,128)(2,1)} %refs_0_), channel_id=1, source_target_pairs={{0,2},{1,3},{2,0},{3,1},{4,6},{5,7},{6,4},{7,5},{8,10},{9,11},{10,... | collective-permute-start | bytes 884744 | tf_op jit(solution)/shard_map/ppermute | solution.py:280
  3.1 12.4 %collective-permute-start = (bf16[128,1152]{1,0:T(8,128)(2,1)}, bf16[128,1152]{1,0:T(8,128)(2,1)S(1)}, u32[]{:S(2)}, u32[]{:S(2)}) collective-permute-start(bf16[128,1152]{1,0:T(8,128)(2,1)} %refs_0_), channel_id=1, source_target_pairs={{0,1},{1,0},{2,3},{3,2},{4,5},{5,4},{6,7},{7,6},{8,9},{9,8},{10,11... | collective-permute-start | bytes 884744 | tf_op jit(solution)/shard_map/ppermute | solution.py:280
  5.8 25.1 %collective-permute-start.7 = (bf16[256,1152]{1,0:T(8,128)(2,1)S(1)}, bf16[256,1152]{1,0:T(8,128)(2,1)S(1)}, u32[]{:S(2)}, u32[]{:S(2)}) collective-permute-start(bf16[256,1152]{1,0:T(8,128)(2,1)S(1)} %get-tuple-element.53), channel_id=1, source_target_pairs={{0,4},{4,0},{8,12},{12,8},{16,20},{20,16},{24,28},{28,24},{1,5},{5... | collective-permute-start | bytes 1769480 | tf_op jit(solution)/shard_map/ppermute | solution.py:280
  7.1 18.7 %collective-permute-start.3 = (bf16[128,1152]{1,0:T(8,128)(2,1)S(1)}, bf16[128,1152]{1,0:T(8,128)(2,1)}, u32[]{:S(2)}, u32[]{:S(2)}) collective-permute-start(bf16[128,1152]{1,0:T(8,128)(2,1)S(1)} %copy-done.4), channel_id=1, source_target_pairs={{0,3},{1,2},{2,1},{3,0},{4,7},{5,6},{6,5},{7,4},{8,11},{9,10},{10,... | collective-permute-start | bytes 884744 | tf_op jit(solution)/shard_map/ppermute | solution.py:280
  15.5 10.3 %collective-permute-start.6 = (bf16[128,1152]{1,0:T(8,128)(2,1)S(1)}, bf16[128,1152]{1,0:T(8,128)(2,1)S(1)}, u32[]{:S(2)}, u32[]{:S(2)}) collective-permute-start(bf16[128,1152]{1,0:T(8,128)(2,1)S(1)} %copy-done.4), channel_id=1, source_target_pairs={{0,24},{4,28},{8,16},{12,20},{16,8},{20,12},{24,0},{28,4},{1,25},{... | collective-permute-start | bytes 884744 | tf_op jit(solution)/shard_map/ppermute | solution.py:280
  17.7 13.2 %collective-permute-start.5 = (bf16[128,1152]{1,0:T(8,128)(2,1)S(1)}, bf16[128,1152]{1,0:T(8,128)(2,1)S(1)}, u32[]{:S(2)}, u32[]{:S(2)}) collective-permute-start(bf16[128,1152]{1,0:T(8,128)(2,1)S(1)} %copy-done.4), channel_id=1, source_target_pairs={{0,16},{4,20},{8,24},{12,28},{16,0},{20,4},{24,8},{28,12},{1,17},{... | collective-permute-start | bytes 884744 | tf_op jit(solution)/shard_map/ppermute | solution.py:280
  17.9 13.0 %collective-permute-start.4 = (bf16[128,1152]{1,0:T(8,128)(2,1)S(1)}, bf16[128,1152]{1,0:T(8,128)(2,1)S(1)}, u32[]{:S(2)}, u32[]{:S(2)}) collective-permute-start(bf16[128,1152]{1,0:T(8,128)(2,1)S(1)} %copy-done.4), channel_id=1, source_target_pairs={{0,8},{4,12},{8,0},{12,4},{16,24},{20,28},{24,16},{28,20},{1,9},{5... | collective-permute-start | bytes 884744 | tf_op jit(solution)/shard_map/ppermute | solution.py:280
  20.0 12.8 %all-to-all-start = ((s32[4,1,512]{2,1,0:T(1,128)}), s32[4,1,512]{2,1,0:T(1,128)}, u32[]{:S(2)}, u32[]{:S(2)}) async-start(s32[4,1,512]{2,1,0:T(1,128)} %broadcast_in_dim.43), calls=%async_computation | async-start | bytes 16384 | tf_op jit(solution)/shard_map/all_to_all | solution.py:317
  25.8 5.3 %copy-start.19 = (pred[4]{0:T(512)(128)(4,1)S(1)}, pred[4]{0:T(512)(128)(4,1)}, u32[]{:S(2)}) copy-start(pred[4]{0:T(512)(128)(4,1)} %fusion.14) | copy-start | bytes 16
  25.8 30.7 %copy-start.5 = (bf16[128,1152]{1,0:T(8,128)(2,1)}, bf16[128,1152]{1,0:T(8,128)(2,1)S(1)}, u32[]{:S(2)}) copy-start(bf16[128,1152]{1,0:T(8,128)(2,1)S(1)} %collective-permute-done.6.refs_3_) | copy-start | bytes 884740
  30.9 25.2 %copy-start.7 = (bf16[128,1152]{1,0:T(8,128)(2,1)}, bf16[128,1152]{1,0:T(8,128)(2,1)S(1)}, u32[]{:S(2)}) copy-start(bf16[128,1152]{1,0:T(8,128)(2,1)S(1)} %collective-permute-done.5.refs_2_) | copy-start | bytes 884740
  30.9 18.3 %copy-start.9 = (bf16[128,1152]{1,0:T(8,128)(2,1)}, bf16[128,1152]{1,0:T(8,128)(2,1)S(1)}, u32[]{:S(2)}) copy-start(bf16[128,1152]{1,0:T(8,128)(2,1)S(1)} %collective-permute-done.4.refs_1_) | copy-start | bytes 884740
  32.8 64.8 %all-to-all-start.1 = ((bf16[4,256,1152]{2,1,0:T(8,128)(2,1)}), bf16[4,256,1152]{2,1,0:T(8,128)(2,1)}, u32[]{:S(2)}, u32[]{:S(2)}) async-start(bf16[4,256,1152]{2,1,0:T(8,128)(2,1)} %broadcast_select_fusion), calls=%async_computation.1 | async-start | bytes 4718592 | tf_op jit(solution)/shard_map/all_to_all | solution.py:327
  38.4 27.5 %collective-permute-start.10 = (bf16[384,1152]{1,0:T(8,128)(2,1)S(1)}, bf16[384,1152]{1,0:T(8,128)(2,1)}, u32[]{:S(2)}, u32[]{:S(2)}) collective-permute-start(bf16[384,1152]{1,0:T(8,128)(2,1)S(1)} %constant_dynamic-update-slice_fusion.refs_1_), channel_id=1, source_target_pairs={{0,24},{4,28},{8,16},{12,20},{16,8},{20,12},{24,0},{28,4},{1,25},{... | collective-permute-start | bytes 2654216 | tf_op jit(solution)/shard_map/ppermute | solution.py:280
  39.9 40.1 %collective-permute-start.9 = (bf16[384,1152]{1,0:T(8,128)(2,1)S(1)}, bf16[384,1152]{1,0:T(8,128)(2,1)}, u32[]{:S(2)}, u32[]{:S(2)}) collective-permute-start(bf16[384,1152]{1,0:T(8,128)(2,1)S(1)} %constant_dynamic-update-slice_fusion.refs_1_), channel_id=1, source_target_pairs={{0,16},{4,20},{8,24},{12,28},{16,0},{20,4},{24,8},{28,12},{1,17},{... | collective-permute-start | bytes 2654216 | tf_op jit(solution)/shard_map/ppermute | solution.py:280
  41.4 38.6 %collective-permute-start.8 = (bf16[384,1152]{1,0:T(8,128)(2,1)S(1)}, bf16[384,1152]{1,0:T(8,128)(2,1)}, u32[]{:S(2)}, u32[]{:S(2)}) collective-permute-start(bf16[384,1152]{1,0:T(8,128)(2,1)S(1)} %constant_dynamic-update-slice_fusion.refs_1_), channel_id=1, source_target_pairs={{0,8},{4,12},{8,0},{12,4},{16,24},{20,28},{24,16},{28,20},{1,9},{5... | collective-permute-start | bytes 2654216 | tf_op jit(solution)/shard_map/ppermute | solution.py:280
  42.2 6.6 %collective-permute-start.1 = (s32[4,512]{1,0:T(4,128)S(1)}, s32[4,512]{1,0:T(4,128)S(1)}, u32[]{:S(2)}, u32[]{:S(2)}) collective-permute-start(s32[4,512]{1,0:T(4,128)S(1)} %bitcast.26), channel_id=1, source_target_pairs={{0,4},{4,0},{8,12},{12,8},{16,20},{20,16},{24,28},{28,24},{1,5},{5... | collective-permute-start | bytes 24584 | tf_op jit(solution)/shard_map/ppermute | solution.py:280
  48.8 7.3 %collective-permute-start.11 = (bf16[128,1152]{1,0:T(8,128)(2,1)S(1)}, bf16[128,1152]{1,0:T(8,128)(2,1)S(1)}, u32[]{:S(2)}, u32[]{:S(2)}) collective-permute-start(bf16[128,1152]{1,0:T(8,128)(2,1)S(1)} %copy-done.4), channel_id=1, source_target_pairs={{0,4},{4,0},{8,12},{12,8},{16,20},{20,16},{24,28},{28,24},{1,5},{5... | collective-permute-start | bytes 884744 | tf_op jit(solution)/shard_map/ppermute | solution.py:280
  49.2 7.3 %collective-permute-start.12 = (bf16[128,1152]{1,0:T(8,128)(2,1)S(1)}, bf16[128,1152]{1,0:T(8,128)(2,1)S(1)}, u32[]{:S(2)}, u32[]{:S(2)}) collective-permute-start(bf16[128,1152]{1,0:T(8,128)(2,1)S(1)} %collective-permute-done.4.refs_1_), channel_id=1, source_target_pairs={{0,4},{4,0},{8,12},{12,8},{16,20},{20,16},{24,28},{28,24},{1,5},{5... | collective-permute-start | bytes 884744 | tf_op jit(solution)/shard_map/ppermute | solution.py:280
  56.1 1.7 copy-start.11
  56.1 1.7 collective-permute-start.13
  56.5 1.3 copy-start.13
  56.5 1.7 collective-permute-start.14
  56.7 24.9 %copy-start.18 = (f32[3456]{0:T(1024)S(1)}, f32[3456]{0:T(1024)}, u32[]{:S(2)}) copy-start(f32[3456]{0:T(1024)} %param.15) | copy-start | bytes 41476
  58.2 1.0 copy-start.6
  59.1 1.0 copy-start.8
  60.1 1.0 copy-start.10
  61.1 1.0 copy-start.12
  62.0 1.0 copy-start.14
  80.0 4.4 %collective-permute-start.15 = (bf16[384,1152]{1,0:T(8,128)(2,1)S(1)}, bf16[384,1152]{1,0:T(8,128)(2,1)S(1)}, u32[]{:S(2)}, u32[]{:S(2)}) collective-permute-start(bf16[384,1152]{1,0:T(8,128)(2,1)S(1)} %constant_dynamic-update-slice_fusion.refs_1_), channel_id=1, source_target_pairs={{0,4},{4,0},{8,12},{12,8},{16,20},{20,16},{24,28},{28,24},{1,5},{5... | collective-permute-start | bytes 2654216 | tf_op jit(solution)/shard_map/ppermute | solution.py:280
  81.2 3.5 %collective-permute-start.16 = (bf16[384,1152]{1,0:T(8,128)(2,1)}, bf16[384,1152]{1,0:T(8,128)(2,1)S(1)}, u32[]{:S(2)}, u32[]{:S(2)}) collective-permute-start(bf16[384,1152]{1,0:T(8,128)(2,1)} %collective-permute-done.8.refs_2_), channel_id=1, source_target_pairs={{0,4},{4,0},{8,12},{12,8},{16,20},{20,16},{24,28},{28,24},{1,5},{5... | collective-permute-start | bytes 2654216 | tf_op jit(solution)/shard_map/ppermute | solution.py:280
  81.2 9.1 %collective-permute-start.17 = (bf16[384,1152]{1,0:T(8,128)(2,1)}, bf16[384,1152]{1,0:T(8,128)(2,1)S(1)}, u32[]{:S(2)}, u32[]{:S(2)}) collective-permute-start(bf16[384,1152]{1,0:T(8,128)(2,1)} %collective-permute-done.9.refs_1_), channel_id=1, source_target_pairs={{0,4},{4,0},{8,12},{12,8},{16,20},{20,16},{24,28},{28,24},{1,5},{5... | collective-permute-start | bytes 2654216 | tf_op jit(solution)/shard_map/ppermute | solution.py:280
  81.7 8.6 %collective-permute-start.18 = (bf16[384,1152]{1,0:T(8,128)(2,1)}, bf16[384,1152]{1,0:T(8,128)(2,1)S(1)}, u32[]{:S(2)}, u32[]{:S(2)}) collective-permute-start(bf16[384,1152]{1,0:T(8,128)(2,1)} %collective-permute-done.10.refs_2_), channel_id=1, source_target_pairs={{0,4},{4,0},{8,12},{12,8},{16,20},{20,16},{24,28},{28,24},{1,5},{5... | collective-permute-start | bytes 2654216 | tf_op jit(solution)/shard_map/ppermute | solution.py:280
  96.2 1.4 copy-start.1
  118.1 10.8 %collective-permute-start.19 = (bf16[2304,1024]{1,0:T(8,128)(2,1)}, bf16[2304,1024]{1,0:T(8,128)(2,1)}, u32[]{:S(2)}, u32[]{:S(2)}) collective-permute-start(bf16[2304,1024]{1,0:T(8,128)(2,1)} %get-tuple-element.46.refs_0_.refs_2_), channel_id=1, source_target_pairs={{0,4},{4,0},{8,12},{12,8},{16,20},{20,16},{24,28},{28,24},{1,5},{5... | collective-permute-start | bytes 14155784 | tf_op jit(solution)/shard_map/ppermute | solution.py:280
  119.1 9.7 %copy-start.15 = (s32[3]{0:T(128)S(1)}, s32[3]{0:T(128)}, u32[]{:S(2)}) copy-start(s32[3]{0:T(128)} %pad_add_fusion.place_ref) | copy-start | bytes 40
  119.1 9.7 %copy-start.16 = (bf16[2304,1024]{1,0:T(8,128)(2,1)S(1)}, bf16[2304,1024]{1,0:T(8,128)(2,1)}, u32[]{:S(2)}) copy-start(bf16[2304,1024]{1,0:T(8,128)(2,1)} %get-tuple-element.46.refs_0_.refs_2_) | copy-start | bytes 14155780
  128.8 1.3 copy-start.17
  130.1 14.9 %copy-start.2 = (bf16[1152,1152]{1,0:T(8,128)(2,1)S(1)}, bf16[1152,1152]{1,0:T(8,128)(2,1)}, u32[]{:S(2)}) copy-start(bf16[1152,1152]{1,0:T(8,128)(2,1)} %w_ref.3) | copy-start | bytes 7962628
  130.1 14.9 %copy-start.3 = (bf16[512,1152]{1,0:T(8,128)(2,1)S(1)}, bf16[512,1152]{1,0:T(8,128)(2,1)}, u32[]{:S(2)}) copy-start(bf16[512,1152]{1,0:T(8,128)(2,1)} %get-tuple-element.47.gate_ref) | copy-start | bytes 3538948
  147.7 18.6 %collective-permute-start.20 = (bf16[256,1152]{1,0:T(8,128)(2,1)S(1)}, bf16[256,1152]{1,0:T(8,128)(2,1)S(1)}, u32[]{:S(2)}, u32[]{:S(2)}) collective-permute-start(bf16[256,1152]{1,0:T(8,128)(2,1)S(1)} %finish.2), channel_id=1, source_target_pairs={{0,0},{3,7},{1,2},{2,5},{4,1},{7,6},{5,3},{6,4},{8,8},{11,15},{9,1... | collective-permute-start | bytes 1769480 | tf_op jit(solution)/shard_map/ppermute | solution.py:370
  168.9 18.1 %collective-permute-start.21 = (bf16[256,1152]{1,0:T(8,128)(2,1)S(1)}, bf16[256,1152]{1,0:T(8,128)(2,1)S(1)}, u32[]{:S(2)}, u32[]{:S(2)}) collective-permute-start(bf16[256,1152]{1,0:T(8,128)(2,1)S(1)} %finish.3), channel_id=1, source_target_pairs={{0,1},{3,6},{1,3},{2,4},{4,0},{7,7},{5,2},{6,5},{8,9},{11,14},{9,1... | collective-permute-start | bytes 1769480 | tf_op jit(solution)/shard_map/ppermute | solution.py:370

commit v4 on v3

--- a/solution.py
+++ b/solution.py
@@ -148,16 +148,19 @@
 def query_kernel(query_scale, place_ref, act_ref, x_ref, ba_ref, wa_ref, wq_ref, *refs):
     q_ref, gate_ref, wa_buf, wq_buf, sems = refs
     count, width = gate_ref.shape
+    half = count // 2
     copies = [
         pltpu.make_async_copy(wq_ref.at[:, :width], wq_buf, sems.at[0]),
         pltpu.make_async_copy(wa_ref.at[:, 2 * width :], wa_buf, sems.at[1]),
     ]
     for copy in copies:
         copy.start()
-    mine = pl.ds(pl.multiple_of(place_ref[0] * count, count), count)
-    act = jax.nn.silu(act_ref[mine, :].astype(F32)).astype(BF16)
+    rows = [pl.ds(pl.multiple_of(place_ref[k] * half, half), half) for k in range(2)]
+    x = jnp.concatenate([x_ref[span, :] for span in rows], axis=0)
+    act = jnp.concatenate([act_ref[span, :] for span in rows], axis=0)
+    act = jax.nn.silu(act.astype(F32)).astype(BF16)
     copies[0].wait()
-    q_ref[...] = (contract(wq_buf[...], x_ref[mine, :], ((0,), (1,))) * query_scale).astype(BF16)
+    q_ref[...] = (contract(wq_buf[...], x, ((0,), (1,))) * query_scale).astype(BF16)
     copies[1].wait()
     gate = contract(act, wa_buf[...], ((1,), (0,))) + ba_ref[:, 2 * width :]
     gate_ref[...] = gate.astype(BF16)
@@ -185,7 +188,7 @@
     )(place, picked, x, b_ada, w_ada, w_qkv)
 
 
-def attend_kernel(head_dim, chunk, place_ref, q_ref, *refs):
+def attend_kernel(head_dim, chunk, q_ref, *refs):
     kv_refs, (o_ref, s_ref) = refs[:-2], refs[-2:]
     pair, queries = q_ref.shape
     row = lax.broadcasted_iota(jnp.int32, (pair, 1), 0)
@@ -217,27 +220,24 @@
     o_ref[...] = jnp.where(row < head_dim, result[:, :queries], result[:, queries:]).astype(BF16)
 
 
-def attend(place, which, qt, kvs):
+def attend(which, qt, kvs):
     width, queries = qt.shape[0], qt.shape[1] // 2
     keys = kvs[0].shape[1]
     head_dim = width // HEADS
     pair, pairs = 2 * head_dim, HEADS // 2
     chunk = math.gcd(keys, 512)
-    k_spec = pl.BlockSpec((pair, keys), lambda p, place: (p, 0))
-    v_spec = pl.BlockSpec((pair, keys), lambda p, place: (p + pairs, 0))
+    k_spec = pl.BlockSpec((pair, keys), lambda p: (p, 0))
+    v_spec = pl.BlockSpec((pair, keys), lambda p: (p + pairs, 0))
     total = len(kvs) * keys
     return pl.pallas_call(
         functools.partial(attend_kernel, head_dim, chunk),
-        grid_spec=pltpu.PrefetchScalarGridSpec(
-            num_scalar_prefetch=1,
-            grid=(pairs,),
-            in_specs=[pl.BlockSpec((pair, queries), lambda p, place: (p, place[which]))]
-            + [k_spec] * len(kvs)
-            + [v_spec] * len(kvs),
-            out_specs=pl.BlockSpec((pair, queries), lambda p, place: (p, 0)),
-            scratch_shapes=[pltpu.VMEM((total, 2 * queries), F32)],
-        ),
+        grid=(pairs,),
+        in_specs=[pl.BlockSpec((pair, queries), lambda p: (p, which))]
+        + [k_spec] * len(kvs)
+        + [v_spec] * len(kvs),
+        out_specs=pl.BlockSpec((pair, queries), lambda p: (p, 0)),
         out_shape=jax.ShapeDtypeStruct((width, queries), BF16),
+        scratch_shapes=[pltpu.VMEM((total, 2 * queries), F32)],
         compiler_params=pltpu.CompilerParams(vmem_limit_bytes=16 * MIB),
         cost_estimate=pl.CostEstimate(
             flops=16 * total * queries * width,
@@ -245,7 +245,7 @@
             transcendentals=HEADS * total * queries,
         ),
         name="attend",
-    )(place, qt, *kvs, *kvs)
+    )(qt, *kvs, *kvs)
 
 
 def finish_kernel(place_ref, att_ref, tok_ref, gate_ref, w_ref, o_ref):
@@ -255,8 +255,8 @@
 
 def finish(place, which, attended, tok, gate, w_out):
     width, queries = attended.shape
-    at = pl.BlockSpec((queries, width), lambda i, place: (place[which], 0))
-    tok_at = pl.BlockSpec((queries, width), lambda i, place: (2 * place[0] + place[which], 0))
+    at = pl.BlockSpec((queries, width), lambda i, place: (which, 0))
+    tok_at = pl.BlockSpec((queries, width), lambda i, place: (place[which], 0))
     return pl.pallas_call(
         finish_kernel,
         grid_spec=pltpu.PrefetchScalarGridSpec(
@@ -304,26 +304,25 @@
     block = tok_rows // 2
     r, c = lax.axis_index("region"), lax.axis_index("ctx")
     core, upper = r % 2, (c >= h).astype(jnp.int32)
-    m = jnp.where(upper == 1, n - 1 - c, c)
 
     tables = [swap(cond_table, "ctx", d) for d in range(1, n)]
-    near = to_chips(after(cond_table, tables[0]))
     mine = lax.dynamic_slice_in_dim(device_tokens, core * block, block)
     other = lax.dynamic_slice_in_dim(device_tokens, (1 - core) * block, block)
     got = swap(other, "region", 1)
+    own, all_ids = after((cond_table, element_ids[0]), got)
+    near = to_chips(own)
     position = jnp.arange(tok_rows, dtype=jnp.int32)
-    ids = jnp.where(position < live_count[0, 0], element_ids[0], -1)
-    ids = after(ids, tables[0])
+    ids = jnp.where(position < live_count[0, 0], all_ids, -1)
     ids = lax.all_to_all(
         jnp.broadcast_to(ids, (n, tok_rows)), "ctx", split_axis=0, concat_axis=0, tiled=True
     )
-    tables, near, mine, got = lax.optimization_barrier((tables, near, mine, got))
-
-    far = to_chips(jnp.concatenate(tables, axis=0))
     even, odd = jnp.where(core == 0, mine, got), jnp.where(core == 0, got, mine)
     work, pass_on = jnp.where(upper == 0, even, odd), jnp.where(upper == 0, odd, even)
     same = (jnp.arange(n) >= h).astype(jnp.int32) == upper
     sent = jnp.where(same[:, None, None], work[None], pass_on[None])
+    tables, near, sent, ids = lax.optimization_barrier((tables, near, sent, ids))
+
+    far = to_chips(jnp.concatenate(tables, axis=0))
     tok = lax.all_to_all(sent, "ctx", split_axis=0, concat_axis=0, tiled=True)
     tok = tok.reshape(n * block, width)
 
@@ -348,28 +347,31 @@
     picked = pick([picked], second, 1)
     tok = after(tok, picked)
 
-    base = jnp.where(upper == 1, n - 2 - 2 * m, 2 * m)
-    place = jnp.stack([base // 2, core ^ upper, 1 - core ^ upper]).astype(jnp.int32)
+    place = jnp.stack([n - 1 - c, c]).astype(jnp.int32)
     bias = b_ada.reshape(1, -1)
     kv, x = stretch(tok, picked, w_ada, bias, w_qkv)
     kvs = [kv, swap(kv, "region", 1)]
     qt, gate = query(place, x, picked, w_ada, bias, w_qkv, 2 * block)
 
-    home = []
-    for which in (1, 2):
-        attended = attend(place, which, qt, kvs)
-        if home:
-            attended = after(attended, home[0])
-        result = finish(place, which, attended, tok, gate, w_out)
-        pairs = []
-        for region in range(size):
-            for k in range(h):
-                to = 2 * k + (region % 2 if which == 1 else 1 - region % 2)
-                pairs.append((region * n + k, (region & ~1) * n + to))
-                pairs.append((region * n + n - 1 - k, (region | 1) * n + n - 1 - to))
-        home.append(lax.ppermute(result, ("region", "ctx"), pairs))
-    number = jnp.where(core == 1, n - 1 - c, c) % 2
-    low, high = jnp.where(number == 0, home[0], home[1]), jnp.where(number == 0, home[1], home[0])
+    there = finish(place, 0, attend(0, qt, kvs), tok, gate, w_out)
+    low, high = (
+        lax.ppermute(
+            there,
+            ("region", "ctx"),
+            [
+                ((pair + k) * n + chip, (pair + chip // h) * n + n - 1 - chip)
+                for pair in range(0, size, 2)
+                for chip in range(n)
+            ],
+        )
+        for k in range(2)
+    )
+    attended = attend(1, qt, kvs)
+    here = finish(place, 1, attended, tok, gate, w_out)
+    here, low, high = lax.optimization_barrier((here, low, high))
+    other = swap(here, "region", 1)
+    own_low, own_high = jnp.where(core == 0, here, other), jnp.where(core == 0, other, here)
+    low, high = jnp.where(core == upper, own_low, low), jnp.where(core == upper, own_high, high)
     return jnp.concatenate([low, high], axis=0)[None]
 
 

time: 189 us -> 178 us (0.942)
  the two profiles are of different devices: /device:TPU:1 before, /device:TPU:17 now
where the time goes in v4:
time: 178 us; the launch traced here: 177 us
  Pallas kernels  78 us (44%)
  waiting for transfers between devices  45 us (25%)
  starting transfers between devices  29.5 us (17%)
  local copies, waits for them, and re-layouts  16.7 us (9%)
  other arithmetic  6.85 us (4%)
    pallas_call x2, Pallas kernels, attend(): pl.pallas_call(functools.partial(attend_kernel, head_dim, chunk), grid=(p...  28.2 us
    ppermute x21, waiting for transfers between devices, swap(): lax.ppermute(x, axis, [(i, i ^ bits) for i in range(lax.axis_size(axis))])  24.4 us
    pallas_call x1, Pallas kernels, stretch(): pl.pallas_call(functools.partial(stretch_kernel, steps), grid=(steps + 2,...  20.4 us
    ppermute x21, starting transfers between devices, swap(): lax.ppermute(x, axis, [(i, i ^ bits) for i in range(lax.axis_size(axis))])  16.7 us
    pallas_call x3, Pallas kernels, pick_rows(): pl.pallas_call(functools.partial(pick_kernel, bases, block), in_specs=[VM...  14.5 us
    all_to_all x1, waiting for transfers between devices, per_device(): lax.all_to_all(jnp.broadcast_to(ids, (n, tok_rows)), 'ctx', split_axis=0,...  13 us
    pallas_call x1, Pallas kernels, query(): pl.pallas_call(functools.partial(query_kernel, query_scale), in_specs=[pl...  9.69 us
    unnamed x46, local copies, waits for them, and re-layouts  7.9 us
  transfers between devices with their start and end apart: 25, of which 8 were waited for; matrix products, arithmetic and copies ran while one was open for 8% of the time, Pallas kernels for 23%

profile of v4, /device:TPU:17, one launch (start us, length us, event | category | flops | bytes accessed | tf_op | source)
XLA Modules:
  0.0 177.0 jit_solution(3060135552992711566)
XLA Ops:
  0.0 1.2 dynamic-slice_bitcast_fusion
  1.2 0.7 collective-permute-start.3
  1.9 1.4 collective-permute-start
  3.3 1.3 collective-permute-start.2
  5.2 2.2 %collective-permute-start.6 = (bf16[128,1152]{1,0:T(8,128)(2,1)}, bf16[128,1152]{1,0:T(8,128)(2,1)S(1)}, u32[]{:S(2)}, u32[]{:S(2)}) collective-permute-start(bf16[128,1152]{1,0:T(8,128)(2,1)} %refs_0_), channel_id=1, source_target_pairs={{0,24},{4,28},{8,16},{12,20},{16,8},{20,12},{24,0},{28,4},{1,25},{... | collective-permute-start | bytes 884744 | tf_op jit(solution)/shard_map/ppermute | solution.py:280
  7.7 0.7 fusion.13
  8.4 0.6 broadcast_in_dim.46
  9.0 5.5 %all-to-all-start = ((s32[4,1,512]{2,1,0:T(1,128)}), s32[4,1,512]{2,1,0:T(1,128)S(1)}, u32[]{:S(2)}, u32[]{:S(2)}) async-start(s32[4,1,512]{2,1,0:T(1,128)} %broadcast_in_dim.46), calls=%async_computation | async-start | bytes 16384 | tf_op jit(solution)/shard_map/all_to_all | solution.py:316
  14.5 1.3 broadcast_select_fusion.2
  16.2 1.9 %broadcast_select_fusion = bf16[4,256,1152]{2,1,0:T(8,128)(2,1)} fusion(pred[4]{0:T(512)(128)(4,1)S(1)} %fusion.14, bf16[256,1152]{1,0:T(8,128)(2,1)S(1)} %get-tuple-element.54, bf16[256,1152]{1,0:T(8,128)(2,1)S(1)} %get-tuple-element.53), kind=kLoop, calls=%fused_computation.1 | loop fusion | flops 1179648 | bytes 3538948 | tf_op jit(solution)/shard_map/jit(_where)/select_n | solution.py:322
  18.1 13.0 %all-to-all-done = s32[4,1,512]{2,1,0:T(1,128)S(1)} async-done(((s32[4,1,512]{2,1,0:T(1,128)}), s32[4,1,512]{2,1,0:T(1,128)S(1)}, u32[]{:S(2)}, u32[]{:S(2)}) %all-to-all-start) | async-done | bytes 8224 | tf_op jit(solution)/shard_map/all_to_all | solution.py:316
  31.2 4.5 %all-to-all-start.1 = ((bf16[4,256,1152]{2,1,0:T(8,128)(2,1)}), bf16[4,256,1152]{2,1,0:T(8,128)(2,1)}, u32[]{:S(2)}, u32[]{:S(2)}) async-start(bf16[4,256,1152]{2,1,0:T(8,128)(2,1)} %broadcast_select_fusion), calls=%async_computation.1 | async-start | bytes 4718592 | tf_op jit(solution)/shard_map/all_to_all | solution.py:326
  35.8 2.2 %collective-permute-start.10 = (bf16[384,1152]{1,0:T(8,128)(2,1)S(1)}, bf16[384,1152]{1,0:T(8,128)(2,1)}, u32[]{:S(2)}, u32[]{:S(2)}) collective-permute-start(bf16[384,1152]{1,0:T(8,128)(2,1)S(1)} %constant_dynamic-update-slice_fusion.refs_1_), channel_id=1, source_target_pairs={{0,24},{4,28},{8,16},{12,20},{16,8},{20,12},{24,0},{28,4},{1,25},{... | collective-permute-start | bytes 2654216 | tf_op jit(solution)/shard_map/ppermute | solution.py:280
  38.5 1.9 %collective-permute-start.7 = (s32[4,512]{1,0:T(4,128)S(1)}, s32[4,512]{1,0:T(4,128)S(1)}, u32[]{:S(2)}, u32[]{:S(2)}) collective-permute-start(s32[4,512]{1,0:T(4,128)S(1)} %bitcast.34), channel_id=1, source_target_pairs={{0,4},{4,0},{8,12},{12,8},{16,20},{20,16},{24,28},{28,24},{1,5},{5... | collective-permute-start | bytes 24584 | tf_op jit(solution)/shard_map/ppermute | solution.py:280
  40.4 0.8 collective-permute-done.7
  42.0 6.2 %gather_fusion = s32[1024]{0:T(1024)S(1)} fusion(s32[4096]{0:T(1024)S(1)} %copy-done, s32[1024]{0:T(1024)S(1)} %broadcast_clamp_fusion), kind=kCustom, calls=%fused_computation | custom fusion | bytes 12288 | tf_op jit(solution)/shard_map/gather | solution.py:331
  48.6 0.4 collective-permute-start.14
  49.0 1.0 fusion.5.idx_ref
  50.1 0.4 collective-permute-done.14.refs_7_
  50.5 1.0 copy-done.6
  51.4 1.0 copy-done.8
  52.4 1.0 copy-done.10
  53.3 1.0 copy-done.12
  54.3 1.0 copy-done.14
  55.3 3.0 %pick.3.refs_0_ = bf16[1024,1152]{1,0:T(8,128)(2,1)S(1)} custom-call(s32[1024,1]{1,0:T(8,128)S(1)} %fusion.5.idx_ref, bf16[128,1152]{1,0:T(8,128)(2,1)S(1)} %copy-done.4, bf16[128,1152]{1,0:T(8,128)(2,1)S(1)} %copy-done.10, bf16[128,1152]{1,0:T(8,128)(2,1)S(1)} %copy-done.8, bf16[128,1152]{1,0:T(8,128)(2,1)S(1)} %copy-done.6, ...), custom_call_target="tpu_custom_call" | custom-call | flops 1 | bytes 1 | tf_op jit(solution)/shard_map/pick/pallas_call | solution.py:48
  58.2 19.2 %collective-permute-done.9.refs_1_ = bf16[384,1152]{1,0:T(8,128)(2,1)} collective-permute-done((bf16[384,1152]{1,0:T(8,128)(2,1)S(1)}, bf16[384,1152]{1,0:T(8,128)(2,1)}, u32[]{:S(2)}, u32[]{:S(2)}) %collective-permute-start.9) | collective-permute-done | bytes 884768 | tf_op jit(solution)/shard_map/ppermute | solution.py:280
  77.4 0.6 collective-permute-start.15
  78.0 0.5 collective-permute-start.17
  78.5 0.6 reshape.277.ba_ref
  79.1 2.2 %collective-permute-done.15.refs_3_ = bf16[384,1152]{1,0:T(8,128)(2,1)S(1)} collective-permute-done((bf16[384,1152]{1,0:T(8,128)(2,1)S(1)}, bf16[384,1152]{1,0:T(8,128)(2,1)S(1)}, u32[]{:S(2)}, u32[]{:S(2)}) %collective-permute-start.15) | collective-permute-done | bytes 884768 | tf_op jit(solution)/shard_map/ppermute | solution.py:280
  81.5 5.6 %pick.4.refs_0_ = bf16[1024,1152]{1,0:T(8,128)(2,1)S(1)} custom-call(s32[1024,1]{1,0:T(8,128)S(1)} %fusion.5.idx_ref, bf16[1024,1152]{1,0:T(8,128)(2,1)S(1)} %pick.3.refs_0_, bf16[384,1152]{1,0:T(8,128)(2,1)S(1)} %constant_dynamic-update-slice_fusion.refs_1_, bf16[384,1152]{1,0:T(8,128)(2,1)} %collective-permute-done.8.refs_2_, ...), custom_call_target="tpu_custom_call", output_to_operand_aliasing={{}: (1, {})} | custom-call | flops 1 | bytes 1 | tf_op jit(solution)/shard_map/pick/pallas_call | solution.py:48
  87.2 5.9 %pick.5.act_ref = bf16[1024,1152]{1,0:T(8,128)(2,1)S(1)} custom-call(s32[1024,1]{1,0:T(8,128)S(1)} %fusion.5.idx_ref, bf16[1024,1152]{1,0:T(8,128)(2,1)S(1)} %pick.4.refs_0_, bf16[384,1152]{1,0:T(8,128)(2,1)} %collective-permute-done.9.refs_1_, bf16[384,1152]{1,0:T(8,128)(2,1)} %collective-permute-done.10.refs_2_, ...), custom_call_target="tpu_custom_call", output_to_operand_aliasing={{}: (1, {})} | custom-call | flops 1 | bytes 1 | tf_op jit(solution)/shard_map/pick/pallas_call | solution.py:48
  93.1 1.4 copy-done.1
  94.5 20.4 %stretch.1 = (bf16[2304,1024]{1,0:T(8,128)(2,1)}, bf16[1024,1152]{1,0:T(8,128)(2,1)}) custom-call(bf16[1024,1152]{1,0:T(8,128)(2,1)} %copy-done.1, bf16[1152,3456]{1,0:T(8,128)(2,1)} %wa_ref.3, f32[1,3456]{1,0:T(1,128)} %reshape.277.ba_ref, bf16[1024,1152]{1,0:T(8,128)(2,1)} %bitcast.7.tok_ref, bf16[1152,3456]{1,0:T(8,128)(2,1)} %wq_ref.3), custom_call_target="tpu_custom_call" | custom-call | flops 1 | bytes 1 | tf_op jit(solution)/shard_map/stretch/pallas_call | solution.py:117
  114.9 0.4 collective-permute-start.19
  115.3 0.6 pad_add_fusion.place_ref
  115.9 9.7 %query.1 = (bf16[1152,512]{1,0:T(8,128)(2,1)}, bf16[512,1152]{1,0:T(8,128)(2,1)}) custom-call(s32[2]{0:T(128)} %pad_add_fusion.place_ref, bf16[1024,1152]{1,0:T(8,128)(2,1)} %copy-done.1, bf16[1024,1152]{1,0:T(8,128)(2,1)} %get-tuple-element.46.x_ref, f32[1,3456]{1,0:T(1,128)} %reshape.277.ba_ref, bf16[1152,3456]{1,0:T(8,128)(2,1)} %wa_ref.3, ...), custom_call_target="tpu_custom_call" | custom-call | flops 1 | bytes 1 | tf_op jit(solution)/shard_map/query/pallas_call | solution.py:172
  125.7 1.3 copy-done.17
  126.9 14.1 %attend.3.att_ref = bf16[1152,256]{1,0:T(8,128)(2,1)S(1)} custom-call(bf16[1152,512]{1,0:T(8,128)(2,1)S(1)} %copy-done.17, bf16[2304,1024]{1,0:T(8,128)(2,1)S(1)} %copy-done.16, bf16[2304,1024]{1,0:T(8,128)(2,1)} %collective-permute-done.19.refs_1_.refs_3_, bf16[2304,1024]{1,0:T(8,128)(2,1)S(1)} %copy-done.16, ...), custom_call_target="tpu_custom_call" | custom-call | flops 9663676416 | bytes 9437184 | tf_op jit(solution)/shard_map/attend/pallas_call | solution.py:232
  141.1 2.7 %finish.3 = bf16[256,1152]{1,0:T(8,128)(2,1)S(1)} custom-call(s32[2]{0:T(128)S(1)} %copy-done.15, bf16[1152,256]{1,0:T(8,128)(2,1)S(1)} %attend.3.att_ref, bf16[1024,1152]{1,0:T(8,128)(2,1)} %bitcast.7.tok_ref, bf16[512,1152]{1,0:T(8,128)(2,1)S(1)} %copy-done.3, bf16[1152,1152]{1,0:T(8,128)(2,1)S(1)} %copy-done.2), custom_call_target="tpu_custom_call" | custom-call | tf_op jit(solution)/shard_map/finish/pallas_call | solution.py:260
  143.8 2.0 %collective-permute-start.21 = (bf16[256,1152]{1,0:T(8,128)(2,1)S(1)}, bf16[256,1152]{1,0:T(8,128)(2,1)S(1)}, u32[]{:S(2)}, u32[]{:S(2)}) collective-permute-start(bf16[256,1152]{1,0:T(8,128)(2,1)S(1)} %finish.3), channel_id=1, source_target_pairs={{4,3},{5,2},{6,5},{7,4},{12,11},{13,10},{14,13},{15,12},{20,19},{2... | collective-permute-start | bytes 1769480 | tf_op jit(solution)/shard_map/ppermute | solution.py:358
  145.8 0.7 collective-permute-start.20
  146.5 14.0 %attend.2.att_ref = bf16[1152,256]{1,0:T(8,128)(2,1)S(1)} custom-call(bf16[1152,512]{1,0:T(8,128)(2,1)S(1)} %copy-done.18, bf16[2304,1024]{1,0:T(8,128)(2,1)S(1)} %copy-done.16, bf16[2304,1024]{1,0:T(8,128)(2,1)} %collective-permute-done.19.refs_1_.refs_3_, bf16[2304,1024]{1,0:T(8,128)(2,1)S(1)} %copy-done.16, ...), custom_call_target="tpu_custom_call" | custom-call | flops 9663676416 | bytes 9437184 | tf_op jit(solution)/shard_map/attend/pallas_call | solution.py:232
  160.5 2.7 %finish.2 = bf16[256,1152]{1,0:T(8,128)(2,1)S(1)} custom-call(s32[2]{0:T(128)S(1)} %copy-done.15, bf16[1152,256]{1,0:T(8,128)(2,1)S(1)} %attend.2.att_ref, bf16[1024,1152]{1,0:T(8,128)(2,1)} %bitcast.7.tok_ref, bf16[512,1152]{1,0:T(8,128)(2,1)S(1)} %copy-done.3, bf16[1152,1152]{1,0:T(8,128)(2,1)S(1)} %copy-done.2), custom_call_target="tpu_custom_call" | custom-call | tf_op jit(solution)/shard_map/finish/pallas_call | solution.py:260
  163.2 7.5 %collective-permute-done.21 = bf16[256,1152]{1,0:T(8,128)(2,1)S(1)} collective-permute-done((bf16[256,1152]{1,0:T(8,128)(2,1)S(1)}, bf16[256,1152]{1,0:T(8,128)(2,1)S(1)}, u32[]{:S(2)}, u32[]{:S(2)}) %collective-permute-start.21) | collective-permute-done | bytes 589856 | tf_op jit(solution)/shard_map/ppermute | solution.py:358
  170.7 3.3 %collective-permute-start.22 = (bf16[256,1152]{1,0:T(8,128)(2,1)S(1)}, bf16[256,1152]{1,0:T(8,128)(2,1)S(1)}, u32[]{:S(2)}, u32[]{:S(2)}) collective-permute-start(bf16[256,1152]{1,0:T(8,128)(2,1)S(1)} %finish.2), channel_id=1, source_target_pairs={{0,4},{4,0},{8,12},{12,8},{16,20},{20,16},{24,28},{28,24},{1,5},{5... | collective-permute-start | bytes 1769480 | tf_op jit(solution)/shard_map/ppermute | solution.py:280
  174.1 1.6 collective-permute-done.22
  175.9 1.1 maximum_bitcast_fusion
  (74 shorter events, 2.8 us)
Async XLA Ops:
  0.0 42.0 %copy-start = (s32[4096]{0:T(1024)S(1)}, s32[4096]{0:T(1024)}, u32[]{:S(2)}) copy-start(s32[4096]{0:T(1024)} %param.11) | copy-start | bytes 49156
  0.0 15.9 %copy-start.4 = (bf16[128,1152]{1,0:T(8,128)(2,1)S(1)}, bf16[128,1152]{1,0:T(8,128)(2,1)}, u32[]{:S(2)}) copy-start(bf16[128,1152]{1,0:T(8,128)(2,1)} %refs_0_) | copy-start | bytes 884740
  1.2 4.1 %collective-permute-start.3 = (bf16[256,1152]{1,0:T(8,128)(2,1)S(1)}, bf16[256,1152]{1,0:T(8,128)(2,1)S(1)}, u32[]{:S(2)}, u32[]{:S(2)}) collective-permute-start(bf16[256,1152]{1,0:T(8,128)(2,1)S(1)} %dynamic-slice_bitcast_fusion), channel_id=1, source_target_pairs={{0,4},{4,0},{8,12},{12,8},{16,20},{20,16},{24,28},{28,24},{1,5},{5... | collective-permute-start | bytes 1769480 | tf_op jit(solution)/shard_map/ppermute | solution.py:280
  1.9 14.0 %collective-permute-start.1 = (bf16[128,1152]{1,0:T(8,128)(2,1)}, bf16[128,1152]{1,0:T(8,128)(2,1)S(1)}, u32[]{:S(2)}, u32[]{:S(2)}) collective-permute-start(bf16[128,1152]{1,0:T(8,128)(2,1)} %refs_0_), channel_id=1, source_target_pairs={{0,2},{1,3},{2,0},{3,1},{4,6},{5,7},{6,4},{7,5},{8,10},{9,11},{10,... | collective-permute-start | bytes 884744 | tf_op jit(solution)/shard_map/ppermute | solution.py:280
  1.9 29.2 %collective-permute-start = (bf16[128,1152]{1,0:T(8,128)(2,1)}, bf16[128,1152]{1,0:T(8,128)(2,1)S(1)}, u32[]{:S(2)}, u32[]{:S(2)}) collective-permute-start(bf16[128,1152]{1,0:T(8,128)(2,1)} %refs_0_), channel_id=1, source_target_pairs={{0,1},{1,0},{2,3},{3,2},{4,5},{5,4},{6,7},{7,6},{8,9},{9,8},{10,11... | collective-permute-start | bytes 884744 | tf_op jit(solution)/shard_map/ppermute | solution.py:280
  3.3 27.8 %collective-permute-start.2 = (bf16[128,1152]{1,0:T(8,128)(2,1)}, bf16[128,1152]{1,0:T(8,128)(2,1)S(1)}, u32[]{:S(2)}, u32[]{:S(2)}) collective-permute-start(bf16[128,1152]{1,0:T(8,128)(2,1)} %refs_0_), channel_id=1, source_target_pairs={{0,3},{1,2},{2,1},{3,0},{4,7},{5,6},{6,5},{7,4},{8,11},{9,10},{10,... | collective-permute-start | bytes 884744 | tf_op jit(solution)/shard_map/ppermute | solution.py:280
  5.2 25.9 %collective-permute-start.6 = (bf16[128,1152]{1,0:T(8,128)(2,1)}, bf16[128,1152]{1,0:T(8,128)(2,1)S(1)}, u32[]{:S(2)}, u32[]{:S(2)}) collective-permute-start(bf16[128,1152]{1,0:T(8,128)(2,1)} %refs_0_), channel_id=1, source_target_pairs={{0,24},{4,28},{8,16},{12,20},{16,8},{20,12},{24,0},{28,4},{1,25},{... | collective-permute-start | bytes 884744 | tf_op jit(solution)/shard_map/ppermute | solution.py:280
  7.5 23.7 %collective-permute-start.5 = (bf16[128,1152]{1,0:T(8,128)(2,1)}, bf16[128,1152]{1,0:T(8,128)(2,1)S(1)}, u32[]{:S(2)}, u32[]{:S(2)}) collective-permute-start(bf16[128,1152]{1,0:T(8,128)(2,1)} %refs_0_), channel_id=1, source_target_pairs={{0,16},{4,20},{8,24},{12,28},{16,0},{20,4},{24,8},{28,12},{1,17},{... | collective-permute-start | bytes 884744 | tf_op jit(solution)/shard_map/ppermute | solution.py:280
  9.0 22.1 %all-to-all-start = ((s32[4,1,512]{2,1,0:T(1,128)}), s32[4,1,512]{2,1,0:T(1,128)S(1)}, u32[]{:S(2)}, u32[]{:S(2)}) async-start(s32[4,1,512]{2,1,0:T(1,128)} %broadcast_in_dim.46), calls=%async_computation | async-start | bytes 16384 | tf_op jit(solution)/shard_map/all_to_all | solution.py:316
  15.9 15.3 %collective-permute-start.4 = (bf16[128,1152]{1,0:T(8,128)(2,1)S(1)}, bf16[128,1152]{1,0:T(8,128)(2,1)S(1)}, u32[]{:S(2)}, u32[]{:S(2)}) collective-permute-start(bf16[128,1152]{1,0:T(8,128)(2,1)S(1)} %copy-done.4), channel_id=1, source_target_pairs={{0,8},{4,12},{8,0},{12,4},{16,24},{20,28},{24,16},{28,20},{1,9},{5... | collective-permute-start | bytes 884744 | tf_op jit(solution)/shard_map/ppermute | solution.py:280
  31.1 17.5 %copy-start.5 = (bf16[128,1152]{1,0:T(8,128)(2,1)}, bf16[128,1152]{1,0:T(8,128)(2,1)S(1)}, u32[]{:S(2)}) copy-start(bf16[128,1152]{1,0:T(8,128)(2,1)S(1)} %collective-permute-done.6.refs_3_) | copy-start | bytes 884740
  31.1 17.2 %copy-start.7 = (bf16[128,1152]{1,0:T(8,128)(2,1)}, bf16[128,1152]{1,0:T(8,128)(2,1)S(1)}, u32[]{:S(2)}) copy-start(bf16[128,1152]{1,0:T(8,128)(2,1)S(1)} %collective-permute-done.5.refs_2_) | copy-start | bytes 884740
  31.2 10.1 %copy-start.9 = (bf16[128,1152]{1,0:T(8,128)(2,1)}, bf16[128,1152]{1,0:T(8,128)(2,1)S(1)}, u32[]{:S(2)}) copy-start(bf16[128,1152]{1,0:T(8,128)(2,1)S(1)} %collective-permute-done.4.refs_1_) | copy-start | bytes 884740
  31.2 63.3 %all-to-all-start.1 = ((bf16[4,256,1152]{2,1,0:T(8,128)(2,1)}), bf16[4,256,1152]{2,1,0:T(8,128)(2,1)}, u32[]{:S(2)}, u32[]{:S(2)}) async-start(bf16[4,256,1152]{2,1,0:T(8,128)(2,1)} %broadcast_select_fusion), calls=%async_computation.1 | async-start | bytes 4718592 | tf_op jit(solution)/shard_map/all_to_all | solution.py:326
  35.8 22.4 %collective-permute-start.10 = (bf16[384,1152]{1,0:T(8,128)(2,1)S(1)}, bf16[384,1152]{1,0:T(8,128)(2,1)}, u32[]{:S(2)}, u32[]{:S(2)}) collective-permute-start(bf16[384,1152]{1,0:T(8,128)(2,1)S(1)} %constant_dynamic-update-slice_fusion.refs_1_), channel_id=1, source_target_pairs={{0,24},{4,28},{8,16},{12,20},{16,8},{20,12},{24,0},{28,4},{1,25},{... | collective-permute-start | bytes 2654216 | tf_op jit(solution)/shard_map/ppermute | solution.py:280
  38.0 39.4 %collective-permute-start.9 = (bf16[384,1152]{1,0:T(8,128)(2,1)S(1)}, bf16[384,1152]{1,0:T(8,128)(2,1)}, u32[]{:S(2)}, u32[]{:S(2)}) collective-permute-start(bf16[384,1152]{1,0:T(8,128)(2,1)S(1)} %constant_dynamic-update-slice_fusion.refs_1_), channel_id=1, source_target_pairs={{0,16},{4,20},{8,24},{12,28},{16,0},{20,4},{24,8},{28,12},{1,17},{... | collective-permute-start | bytes 2654216 | tf_op jit(solution)/shard_map/ppermute | solution.py:280
  38.3 39.1 %collective-permute-start.8 = (bf16[384,1152]{1,0:T(8,128)(2,1)S(1)}, bf16[384,1152]{1,0:T(8,128)(2,1)}, u32[]{:S(2)}, u32[]{:S(2)}) collective-permute-start(bf16[384,1152]{1,0:T(8,128)(2,1)S(1)} %constant_dynamic-update-slice_fusion.refs_1_), channel_id=1, source_target_pairs={{0,8},{4,12},{8,0},{12,4},{16,24},{20,28},{24,16},{28,20},{1,9},{5... | collective-permute-start | bytes 2654216 | tf_op jit(solution)/shard_map/ppermute | solution.py:280
  38.5 2.7 %collective-permute-start.7 = (s32[4,512]{1,0:T(4,128)S(1)}, s32[4,512]{1,0:T(4,128)S(1)}, u32[]{:S(2)}, u32[]{:S(2)}) collective-permute-start(s32[4,512]{1,0:T(4,128)S(1)} %bitcast.34), channel_id=1, source_target_pairs={{0,4},{4,0},{8,12},{12,8},{16,20},{20,16},{24,28},{28,24},{1,5},{5... | collective-permute-start | bytes 24584 | tf_op jit(solution)/shard_map/ppermute | solution.py:280
  40.4 7.9 %collective-permute-start.11 = (bf16[128,1152]{1,0:T(8,128)(2,1)S(1)}, bf16[128,1152]{1,0:T(8,128)(2,1)S(1)}, u32[]{:S(2)}, u32[]{:S(2)}) collective-permute-start(bf16[128,1152]{1,0:T(8,128)(2,1)S(1)} %copy-done.4), channel_id=1, source_target_pairs={{0,4},{4,0},{8,12},{12,8},{16,20},{20,16},{24,28},{28,24},{1,5},{5... | collective-permute-start | bytes 884744 | tf_op jit(solution)/shard_map/ppermute | solution.py:280
  41.3 7.4 %collective-permute-start.12 = (bf16[128,1152]{1,0:T(8,128)(2,1)S(1)}, bf16[128,1152]{1,0:T(8,128)(2,1)S(1)}, u32[]{:S(2)}, u32[]{:S(2)}) collective-permute-start(bf16[128,1152]{1,0:T(8,128)(2,1)S(1)} %collective-permute-done.4.refs_1_), channel_id=1, source_target_pairs={{0,4},{4,0},{8,12},{12,8},{16,20},{20,16},{24,28},{28,24},{1,5},{5... | collective-permute-start | bytes 884744 | tf_op jit(solution)/shard_map/ppermute | solution.py:280
  48.4 1.7 copy-start.11
  48.4 1.7 collective-permute-start.13
  48.6 1.5 copy-start.13
  48.6 1.8 %collective-permute-start.14 = (bf16[128,1152]{1,0:T(8,128)(2,1)S(1)}, bf16[128,1152]{1,0:T(8,128)(2,1)S(1)}, u32[]{:S(2)}, u32[]{:S(2)}) collective-permute-start(bf16[128,1152]{1,0:T(8,128)(2,1)S(1)} %collective-permute-done.6.refs_3_), channel_id=1, source_target_pairs={{0,4},{4,0},{8,12},{12,8},{16,20},{20,16},{24,28},{28,24},{1,5},{5... | collective-permute-start | bytes 884744 | tf_op jit(solution)/shard_map/ppermute | solution.py:280
  49.0 29.5 %copy-start.19 = (f32[3456]{0:T(1024)S(1)}, f32[3456]{0:T(1024)}, u32[]{:S(2)}) copy-start(f32[3456]{0:T(1024)} %param.15) | copy-start | bytes 41476
  50.5 1.0 copy-start.6
  51.4 1.0 copy-start.8
  52.4 1.0 copy-start.10
  53.3 1.0 copy-start.12
  54.3 1.0 copy-start.14
  77.4 3.9 %collective-permute-start.15 = (bf16[384,1152]{1,0:T(8,128)(2,1)S(1)}, bf16[384,1152]{1,0:T(8,128)(2,1)S(1)}, u32[]{:S(2)}, u32[]{:S(2)}) collective-permute-start(bf16[384,1152]{1,0:T(8,128)(2,1)S(1)} %constant_dynamic-update-slice_fusion.refs_1_), channel_id=1, source_target_pairs={{0,4},{4,0},{8,12},{12,8},{16,20},{20,16},{24,28},{28,24},{1,5},{5... | collective-permute-start | bytes 2654216 | tf_op jit(solution)/shard_map/ppermute | solution.py:280
  78.0 3.5 %collective-permute-start.16 = (bf16[384,1152]{1,0:T(8,128)(2,1)}, bf16[384,1152]{1,0:T(8,128)(2,1)S(1)}, u32[]{:S(2)}, u32[]{:S(2)}) collective-permute-start(bf16[384,1152]{1,0:T(8,128)(2,1)} %collective-permute-done.8.refs_2_), channel_id=1, source_target_pairs={{0,4},{4,0},{8,12},{12,8},{16,20},{20,16},{24,28},{28,24},{1,5},{5... | collective-permute-start | bytes 2654216 | tf_op jit(solution)/shard_map/ppermute | solution.py:280
  78.0 9.1 %collective-permute-start.17 = (bf16[384,1152]{1,0:T(8,128)(2,1)}, bf16[384,1152]{1,0:T(8,128)(2,1)S(1)}, u32[]{:S(2)}, u32[]{:S(2)}) collective-permute-start(bf16[384,1152]{1,0:T(8,128)(2,1)} %collective-permute-done.9.refs_1_), channel_id=1, source_target_pairs={{0,4},{4,0},{8,12},{12,8},{16,20},{20,16},{24,28},{28,24},{1,5},{5... | collective-permute-start | bytes 2654216 | tf_op jit(solution)/shard_map/ppermute | solution.py:280
  78.5 8.7 %collective-permute-start.18 = (bf16[384,1152]{1,0:T(8,128)(2,1)}, bf16[384,1152]{1,0:T(8,128)(2,1)S(1)}, u32[]{:S(2)}, u32[]{:S(2)}) collective-permute-start(bf16[384,1152]{1,0:T(8,128)(2,1)} %collective-permute-done.10.refs_2_), channel_id=1, source_target_pairs={{0,4},{4,0},{8,12},{12,8},{16,20},{20,16},{24,28},{28,24},{1,5},{5... | collective-permute-start | bytes 2654216 | tf_op jit(solution)/shard_map/ppermute | solution.py:280
  93.0 1.4 copy-start.1
  114.9 10.7 %collective-permute-start.19 = (bf16[2304,1024]{1,0:T(8,128)(2,1)}, bf16[2304,1024]{1,0:T(8,128)(2,1)}, u32[]{:S(2)}, u32[]{:S(2)}) collective-permute-start(bf16[2304,1024]{1,0:T(8,128)(2,1)} %get-tuple-element.48.refs_0_.refs_2_), channel_id=1, source_target_pairs={{0,4},{4,0},{8,12},{12,8},{16,20},{20,16},{24,28},{28,24},{1,5},{5... | collective-permute-start | bytes 14155784 | tf_op jit(solution)/shard_map/ppermute | solution.py:280
  115.9 9.7 %copy-start.16 = (bf16[2304,1024]{1,0:T(8,128)(2,1)S(1)}, bf16[2304,1024]{1,0:T(8,128)(2,1)}, u32[]{:S(2)}) copy-start(bf16[2304,1024]{1,0:T(8,128)(2,1)} %get-tuple-element.48.refs_0_.refs_2_) | copy-start | bytes 14155780
  125.6 1.3 copy-start.17
  126.9 14.2 %copy-start.2 = (bf16[1152,1152]{1,0:T(8,128)(2,1)S(1)}, bf16[1152,1152]{1,0:T(8,128)(2,1)}, u32[]{:S(2)}) copy-start(bf16[1152,1152]{1,0:T(8,128)(2,1)} %w_ref.3) | copy-start | bytes 7962628
  126.9 14.2 %copy-start.3 = (bf16[512,1152]{1,0:T(8,128)(2,1)S(1)}, bf16[512,1152]{1,0:T(8,128)(2,1)}, u32[]{:S(2)}) copy-start(bf16[512,1152]{1,0:T(8,128)(2,1)} %get-tuple-element.49.gate_ref) | copy-start | bytes 3538948
  126.9 14.2 %copy-start.15 = (s32[2]{0:T(128)S(1)}, s32[2]{0:T(128)}, u32[]{:S(2)}) copy-start(s32[2]{0:T(128)} %pad_add_fusion.place_ref) | copy-start | bytes 28
  141.1 5.4 %copy-start.18 = (bf16[1152,512]{1,0:T(8,128)(2,1)S(1)}, bf16[1152,512]{1,0:T(8,128)(2,1)}, u32[]{:S(2)}) copy-start(bf16[1152,512]{1,0:T(8,128)(2,1)} %get-tuple-element.47.q_ref) | copy-start | bytes 3538948
  143.8 27.0 %collective-permute-start.21 = (bf16[256,1152]{1,0:T(8,128)(2,1)S(1)}, bf16[256,1152]{1,0:T(8,128)(2,1)S(1)}, u32[]{:S(2)}, u32[]{:S(2)}) collective-permute-start(bf16[256,1152]{1,0:T(8,128)(2,1)S(1)} %finish.3), channel_id=1, source_target_pairs={{4,3},{5,2},{6,5},{7,4},{12,11},{13,10},{14,13},{15,12},{20,19},{2... | collective-permute-start | bytes 1769480 | tf_op jit(solution)/shard_map/ppermute | solution.py:358
  145.8 24.9 %collective-permute-start.20 = (bf16[256,1152]{1,0:T(8,128)(2,1)S(1)}, bf16[256,1152]{1,0:T(8,128)(2,1)S(1)}, u32[]{:S(2)}, u32[]{:S(2)}) collective-permute-start(bf16[256,1152]{1,0:T(8,128)(2,1)S(1)} %finish.3), channel_id=1, source_target_pairs={{0,3},{1,2},{2,5},{3,4},{8,11},{9,10},{10,13},{11,12},{16,19},{17,... | collective-permute-start | bytes 1769480 | tf_op jit(solution)/shard_map/ppermute | solution.py:358
  170.7 5.0 %collective-permute-start.22 = (bf16[256,1152]{1,0:T(8,128)(2,1)S(1)}, bf16[256,1152]{1,0:T(8,128)(2,1)S(1)}, u32[]{:S(2)}, u32[]{:S(2)}) collective-permute-start(bf16[256,1152]{1,0:T(8,128)(2,1)S(1)} %finish.2), channel_id=1, source_target_pairs={{0,4},{4,0},{8,12},{12,8},{16,20},{20,16},{24,28},{28,24},{1,5},{5... | collective-permute-start | bytes 1769480 | tf_op jit(solution)/shard_map/ppermute | solution.py:280

commit v5 on v4

--- a/solution.py
+++ b/solution.py
@@ -74,18 +74,22 @@
 
     @pl.when(i == 0)
     def _():
+        for span in blocks:
+            silu_ref[span, :] = jax.nn.silu(act_ref[span, :].astype(F32)).astype(BF16)
+
+    @pl.when(i < steps)
+    def _():
+        mods = contract(silu_ref[...], wa_ref[...], ((1,), (0,))) + ba_ref[...]
+        mods_ref[i] = mods.astype(BF16)
+
+    @pl.when(i == 0)
+    def _():
         tok_copy.start()
+
+    @pl.when(i == 1)
+    def _():
         for copy in wq_copies:
             copy.start()
-        for span in blocks:
-            silu_ref[span, :] = jax.nn.silu(act_ref[span, :].astype(F32)).astype(BF16)
-
-    for k in range(steps):
-
-        @pl.when(i == k)
-        def _():
-            mods = contract(silu_ref[...], wa_ref[...], ((1,), (0,))) + ba_ref[...]
-            mods_ref[:, k * cols : (k + 1) * cols] = mods.astype(BF16)
 
     @pl.when(i == steps - 1)
     def _():
@@ -95,7 +99,9 @@
             moved = values - jnp.mean(values, axis=1, keepdims=True)
             spread = jnp.mean(moved * moved, axis=1, keepdims=True)
             normed = moved * lax.rsqrt(spread + 1e-06)
-            shift, scale = mods_ref[span, :width], mods_ref[span, width:]
+            first = width - cols
+            shift = jnp.concatenate([mods_ref[0, span, :], mods_ref[1, span, :first]], axis=1)
+            scale = jnp.concatenate([mods_ref[1, span, first:], mods_ref[2, span, :]], axis=1)
             x_ref[span, :] = (normed * (1.0 + scale.astype(F32)) + shift.astype(F32)).astype(BF16)
 
     for k, copy in enumerate(wq_copies):
@@ -103,7 +109,10 @@
         @pl.when(i == steps + k)
         def _():
             copy.wait()
-            kv_ref[...] = contract(wq_buf[k], x_ref[...], ((0,), (1,))).astype(BF16)
+
+    @pl.when(i >= steps)
+    def _():
+        kv_ref[...] = contract(wq_buf[i - steps], x_ref[...], ((0,), (1,))).astype(BF16)
 
 
 def stretch(tok, picked, w_ada, b_ada, w_qkv):
@@ -136,7 +145,7 @@
             pltpu.VMEM((count, width), BF16),
             pltpu.VMEM((2, width, width), BF16),
             pltpu.VMEM((count, width), BF16),
-            pltpu.VMEM((count, 2 * width), BF16),
+            pltpu.VMEM((steps, count, cols), BF16),
             pltpu.SemaphoreType.DMA((3,)),
         ],
         compiler_params=pltpu.CompilerParams(vmem_limit_bytes=58 * MIB),
@@ -190,55 +199,67 @@
 
 def attend_kernel(head_dim, chunk, q_ref, *refs):
     kv_refs, (o_ref, s_ref) = refs[:-2], refs[-2:]
-    pair, queries = q_ref.shape
+    pair, queries = 2 * head_dim, q_ref.shape[1]
     row = lax.broadcasted_iota(jnp.int32, (pair, 1), 0)
-    q = q_ref[...]
-    zero = jnp.zeros_like(q)
-    both = jnp.concatenate(
-        [jnp.where(row < head_dim, q, zero), jnp.where(row < head_dim, zero, q)], axis=1
-    )
     half = len(kv_refs) // 2
     parts = [
         (k_ref, v_ref, i)
         for k_ref, v_ref in zip(kv_refs[:half], kv_refs[half:])
         for i in range(0, k_ref.shape[1], chunk)
     ]
-    top = None
-    for n, (k_ref, _, i) in enumerate(parts):
-        scores = contract(k_ref[:, i : i + chunk], both, ((0,), (0,)))
-        s_ref[n * chunk : (n + 1) * chunk, :] = scores
+    groups = [slice(lo, lo + pair) for lo in range(0, q_ref.shape[0], pair)]
+    both, top = {}, {}
+
+    def score(g, n):
+        if n == 0:
+            q = q_ref[groups[g], :]
+            zero = jnp.zeros_like(q)
+            sides = [jnp.where(row < head_dim, q, zero), jnp.where(row < head_dim, zero, q)]
+            both[g] = jnp.concatenate(sides, axis=1)
+        k_ref, _, i = parts[n]
+        scores = contract(k_ref[groups[g], i : i + chunk], both[g], ((0,), (0,)))
+        s_ref[g % 2, n * chunk : (n + 1) * chunk, :] = scores
         peak = jnp.max(scores, axis=0, keepdims=True)
-        top = peak if top is None else jnp.maximum(top, peak)
-    weighted = denominator = None
-    for n, (_, v_ref, i) in enumerate(parts):
-        expo = jnp.exp2(s_ref[n * chunk : (n + 1) * chunk, :] - top)
-        total = jnp.sum(expo, axis=0, keepdims=True)
-        part = contract(v_ref[:, i : i + chunk], expo.astype(BF16), ((1,), (0,)))
-        weighted = part if weighted is None else weighted + part
-        denominator = total if denominator is None else denominator + total
-    result = weighted / denominator
-    o_ref[...] = jnp.where(row < head_dim, result[:, :queries], result[:, queries:]).astype(BF16)
+        top[g] = jnp.maximum(top[g], peak) if n else peak
+
+    for n in range(len(parts)):
+        score(0, n)
+    for g, rows in enumerate(groups):
+        weighted = denominator = None
+        for n, (_, v_ref, i) in enumerate(parts):
+            if g + 1 < len(groups):
+                score(g + 1, n)
+            expo = jnp.exp2(s_ref[g % 2, n * chunk : (n + 1) * chunk, :] - top[g])
+            total = jnp.sum(expo, axis=0, keepdims=True)
+            part = contract(v_ref[rows, i : i + chunk], expo.astype(BF16), ((1,), (0,)))
+            weighted = weighted + part if n else part
+            denominator = denominator + total if n else total
+        result = weighted / denominator
+        o_ref[rows, :] = jnp.where(row < head_dim, result[:, :queries], result[:, queries:]).astype(
+            BF16
+        )
 
 
 def attend(which, qt, kvs):
     width, queries = qt.shape[0], qt.shape[1] // 2
     keys = kvs[0].shape[1]
     head_dim = width // HEADS
-    pair, pairs = 2 * head_dim, HEADS // 2
-    chunk = math.gcd(keys, 512)
-    k_spec = pl.BlockSpec((pair, keys), lambda p: (p, 0))
-    v_spec = pl.BlockSpec((pair, keys), lambda p: (p + pairs, 0))
+    steps = HEADS // 4
+    rows = width // steps
+    chunk = math.gcd(keys, 1024)
+    k_spec = pl.BlockSpec((rows, keys), lambda p: (p, 0))
+    v_spec = pl.BlockSpec((rows, keys), lambda p: (p + steps, 0))
     total = len(kvs) * keys
     return pl.pallas_call(
         functools.partial(attend_kernel, head_dim, chunk),
-        grid=(pairs,),
-        in_specs=[pl.BlockSpec((pair, queries), lambda p: (p, which))]
+        grid=(steps,),
+        in_specs=[pl.BlockSpec((rows, queries), lambda p: (p, which))]
         + [k_spec] * len(kvs)
         + [v_spec] * len(kvs),
-        out_specs=pl.BlockSpec((pair, queries), lambda p: (p, 0)),
+        out_specs=pl.BlockSpec((rows, queries), lambda p: (p, 0)),
         out_shape=jax.ShapeDtypeStruct((width, queries), BF16),
-        scratch_shapes=[pltpu.VMEM((total, 2 * queries), F32)],
-        compiler_params=pltpu.CompilerParams(vmem_limit_bytes=16 * MIB),
+        scratch_shapes=[pltpu.VMEM((2, total, 2 * queries), F32)],
+        compiler_params=pltpu.CompilerParams(vmem_limit_bytes=8 * MIB + 32 * total * queries),
         cost_estimate=pl.CostEstimate(
             flops=16 * total * queries * width,
             bytes_accessed=4 * total * width,
@@ -333,18 +354,17 @@
     relative = ((((owner // n) ^ r) * n) + ((owner % n) ^ c)) * elem_rows + slots % elem_rows
     relative = jnp.where(ids < 0, -1, relative)
 
-    def pick(picked, chips, d):
-        order = list(chips) + [o ^ 1 for o in chips]
-        pieces = list(chips.values()) + [swap(b, "region", 1) for b in chips.values()]
-        bases = [(o * n + d) * elem_rows for o in order]
-        return pick_rows(relative, picked, pieces, bases, 2 * block)
-
-    picked = pick([], near, 0)
+    def pick(picked, blocks, d):
+        bases = [(o * n + d) * elem_rows for o in blocks]
+        return pick_rows(relative, picked, list(blocks.values()), bases, 2 * block)
+
+    def other_core(chips):
+        return {o ^ 1: swap(b, "region", 1) for o, b in chips.items()}
+
+    picked = pick([], near | other_core(near), 0)
     far, picked = lax.optimization_barrier((far, picked))
-    first = {o: far[o] for o in far if o < size // 2}
-    second = {o: far[o] for o in far if o >= size // 2}
-    picked = pick([picked], first, 1)
-    picked = pick([picked], second, 1)
+    picked = pick([picked], far, 1)
+    picked = pick([picked], other_core(far), 1)
     tok = after(tok, picked)
 
     place = jnp.stack([n - 1 - c, c]).astype(jnp.int32)
@@ -354,24 +374,12 @@
     qt, gate = query(place, x, picked, w_ada, bias, w_qkv, 2 * block)
 
     there = finish(place, 0, attend(0, qt, kvs), tok, gate, w_out)
-    low, high = (
-        lax.ppermute(
-            there,
-            ("region", "ctx"),
-            [
-                ((pair + k) * n + chip, (pair + chip // h) * n + n - 1 - chip)
-                for pair in range(0, size, 2)
-                for chip in range(n)
-            ],
-        )
-        for k in range(2)
-    )
-    attended = attend(1, qt, kvs)
-    here = finish(place, 1, attended, tok, gate, w_out)
-    here, low, high = lax.optimization_barrier((here, low, high))
-    other = swap(here, "region", 1)
-    own_low, own_high = jnp.where(core == 0, here, other), jnp.where(core == 0, other, here)
-    low, high = jnp.where(core == upper, own_low, low), jnp.where(core == upper, own_high, high)
+    back = swap(there, "ctx", n - 1)
+    here = finish(place, 1, attend(1, qt, kvs), tok, gate, w_out)
+    here, back = lax.optimization_barrier((here, back))
+    mine, given = jnp.where(core == upper, here, back), jnp.where(core == upper, back, here)
+    other = swap(given, "region", 1)
+    low, high = jnp.where(core == 0, mine, other), jnp.where(core == 0, other, mine)
     return jnp.concatenate([low, high], axis=0)[None]
 
 

time: 178 us -> 171 us (0.961)
  Pallas kernels: 78 us -> 72.9 us
  starting transfers between devices: 29.5 us -> 24.5 us
  waiting for transfers between devices: 45 us -> 48.2 us
    ppermute x21 -> x22, waiting for transfers between devices: 24.4 us -> 35.2 us  [swap(): lax.ppermute(x, axis, [(i, i ^ bits) for i in range(lax.axis_size(axis))])]
    ppermute x2 -> x0, waiting for transfers between devices: 7.55 us -> none  [per_device(): lax.ppermute(there, ('region', 'ctx'), [((pair + k) * n + chip, (pair + c...]
    pallas_call x2, Pallas kernels: 28.2 us -> 23.6 us  [attend(): pl.pallas_call(functools.partial(attend_kernel, head_dim, chunk), grid=(s...]
    ppermute x2 -> x0, starting transfers between devices: 2.72 us -> none  [per_device(): lax.ppermute(there, ('region', 'ctx'), [((pair + k) * n + chip, (pair + c...]
    ppermute x21 -> x22, starting transfers between devices: 16.7 us -> 14.5 us  [swap(): lax.ppermute(x, axis, [(i, i ^ bits) for i in range(lax.axis_size(axis))])]
    unnamed x46 -> x44, local copies, waits for them, and re-layouts: 7.9 us -> 7.91 us
  transfers between devices with their start and end apart: 25 -> 24, of which waited for: 8 -> 6; matrix products, arithmetic and copies ran while one was open for 8% -> 8% of each run, Pallas kernels for 23% -> 22%
where the time goes in v5:
time: 171 us; the launch traced here: 170 us
  Pallas kernels  72.9 us (43%)
  waiting for transfers between devices  48.2 us (28%)
  starting transfers between devices  24.5 us (14%)
  local copies, waits for them, and re-layouts  16.7 us (10%)
  other arithmetic  6.83 us (4%)
    ppermute x22, waiting for transfers between devices, swap(): lax.ppermute(x, axis, [(i, i ^ bits) for i in range(lax.axis_size(axis))])  35.2 us
    pallas_call x2, Pallas kernels, attend(): pl.pallas_call(functools.partial(attend_kernel, head_dim, chunk), grid=(s...  23.6 us
    pallas_call x1, Pallas kernels, stretch(): pl.pallas_call(functools.partial(stretch_kernel, steps), grid=(steps + 2,...  20.7 us
    ppermute x22, starting transfers between devices, swap(): lax.ppermute(x, axis, [(i, i ^ bits) for i in range(lax.axis_size(axis))])  14.5 us
    pallas_call x3, Pallas kernels, pick_rows(): pl.pallas_call(functools.partial(pick_kernel, bases, block), in_specs=[VM...  13.5 us
    all_to_all x1, waiting for transfers between devices, per_device(): lax.all_to_all(jnp.broadcast_to(ids, (n, tok_rows)), 'ctx', split_axis=0,...  13 us
    pallas_call x1, Pallas kernels, query(): pl.pallas_call(functools.partial(query_kernel, query_scale), in_specs=[pl...  9.67 us
    unnamed x44, local copies, waits for them, and re-layouts  7.91 us
  transfers between devices with their start and end apart: 24, of which 6 were waited for; matrix products, arithmetic and copies ran while one was open for 8% of the time, Pallas kernels for 22%

profile of v5, /device:TPU:17, one launch (start us, length us, event | category | flops | bytes accessed | tf_op | source)
XLA Modules:
  0.0 170.2 jit_solution(8659932554485728730)
XLA Ops:
  0.0 1.2 dynamic-slice_bitcast_fusion
  1.2 0.7 collective-permute-start.3
  1.9 1.4 collective-permute-start
  3.3 1.3 collective-permute-start.2
  5.2 2.2 %collective-permute-start.6 = (bf16[128,1152]{1,0:T(8,128)(2,1)}, bf16[128,1152]{1,0:T(8,128)(2,1)S(1)}, u32[]{:S(2)}, u32[]{:S(2)}) collective-permute-start(bf16[128,1152]{1,0:T(8,128)(2,1)} %refs_0_), channel_id=1, source_target_pairs={{0,24},{4,28},{8,16},{12,20},{16,8},{20,12},{24,0},{28,4},{1,25},{... | collective-permute-start | bytes 884744 | tf_op jit(solution)/shard_map/ppermute | solution.py:301
  7.7 0.7 fusion.13
  8.4 0.6 broadcast_in_dim.46
  9.0 5.5 %all-to-all-start = ((s32[4,1,512]{2,1,0:T(1,128)}), s32[4,1,512]{2,1,0:T(1,128)S(1)}, u32[]{:S(2)}, u32[]{:S(2)}) async-start(s32[4,1,512]{2,1,0:T(1,128)} %broadcast_in_dim.46), calls=%async_computation | async-start | bytes 16384 | tf_op jit(solution)/shard_map/all_to_all | solution.py:337
  14.5 1.3 broadcast_select_fusion.2
  15.9 0.3 collective-permute-start.4
  16.2 1.9 %broadcast_select_fusion = bf16[4,256,1152]{2,1,0:T(8,128)(2,1)} fusion(pred[4]{0:T(512)(128)(4,1)S(1)} %fusion.14, bf16[256,1152]{1,0:T(8,128)(2,1)S(1)} %get-tuple-element.54, bf16[256,1152]{1,0:T(8,128)(2,1)S(1)} %get-tuple-element.53), kind=kLoop, calls=%fused_computation.1 | loop fusion | flops 1179648 | bytes 3538948 | tf_op jit(solution)/shard_map/jit(_where)/select_n | solution.py:343
  18.1 13.0 %all-to-all-done = s32[4,1,512]{2,1,0:T(1,128)S(1)} async-done(((s32[4,1,512]{2,1,0:T(1,128)}), s32[4,1,512]{2,1,0:T(1,128)S(1)}, u32[]{:S(2)}, u32[]{:S(2)}) %all-to-all-start) | async-done | bytes 8224 | tf_op jit(solution)/shard_map/all_to_all | solution.py:337
  31.2 4.5 %all-to-all-start.1 = ((bf16[4,256,1152]{2,1,0:T(8,128)(2,1)}), bf16[4,256,1152]{2,1,0:T(8,128)(2,1)}, u32[]{:S(2)}, u32[]{:S(2)}) async-start(bf16[4,256,1152]{2,1,0:T(8,128)(2,1)} %broadcast_select_fusion), calls=%async_computation.1 | async-start | bytes 4718592 | tf_op jit(solution)/shard_map/all_to_all | solution.py:347
  35.8 2.2 %collective-permute-start.10 = (bf16[384,1152]{1,0:T(8,128)(2,1)S(1)}, bf16[384,1152]{1,0:T(8,128)(2,1)}, u32[]{:S(2)}, u32[]{:S(2)}) collective-permute-start(bf16[384,1152]{1,0:T(8,128)(2,1)S(1)} %constant_dynamic-update-slice_fusion.refs_1_), channel_id=1, source_target_pairs={{0,24},{4,28},{8,16},{12,20},{16,8},{20,12},{24,0},{28,4},{1,25},{... | collective-permute-start | bytes 2654216 | tf_op jit(solution)/shard_map/ppermute | solution.py:301
  38.5 1.9 %collective-permute-start.7 = (s32[4,512]{1,0:T(4,128)S(1)}, s32[4,512]{1,0:T(4,128)S(1)}, u32[]{:S(2)}, u32[]{:S(2)}) collective-permute-start(s32[4,512]{1,0:T(4,128)S(1)} %bitcast.34), channel_id=1, source_target_pairs={{0,4},{4,0},{8,12},{12,8},{16,20},{20,16},{24,28},{28,24},{1,5},{5... | collective-permute-start | bytes 24584 | tf_op jit(solution)/shard_map/ppermute | solution.py:301
  40.4 0.8 collective-permute-done.7
  41.3 0.3 collective-permute-start.12
  41.7 0.3 copy.24
  42.0 6.2 %gather_fusion = s32[1024]{0:T(1024)S(1)} fusion(s32[4096]{0:T(1024)S(1)} %copy-done, s32[1024]{0:T(1024)S(1)} %broadcast_clamp_fusion), kind=kCustom, calls=%fused_computation | custom fusion | bytes 12288 | tf_op jit(solution)/shard_map/gather | solution.py:352
  48.6 0.4 collective-permute-start.14
  49.0 1.0 fusion.5.idx_ref
  50.1 0.4 collective-permute-done.14.refs_7_
  50.5 1.0 copy-done.6
  51.4 1.0 copy-done.8
  52.4 1.0 copy-done.10
  53.3 1.0 copy-done.12
  54.3 1.0 copy-done.14
  55.3 3.0 %pick.3.refs_0_ = bf16[1024,1152]{1,0:T(8,128)(2,1)S(1)} custom-call(s32[1024,1]{1,0:T(8,128)S(1)} %fusion.5.idx_ref, bf16[128,1152]{1,0:T(8,128)(2,1)S(1)} %copy-done.4, bf16[128,1152]{1,0:T(8,128)(2,1)S(1)} %copy-done.10, bf16[128,1152]{1,0:T(8,128)(2,1)S(1)} %copy-done.8, bf16[128,1152]{1,0:T(8,128)(2,1)S(1)} %copy-done.6, ...), custom_call_target="tpu_custom_call" | custom-call | flops 1 | bytes 1 | tf_op jit(solution)/shard_map/pick/pallas_call | solution.py:48
  58.2 19.1 %collective-permute-done.9.refs_3_ = bf16[384,1152]{1,0:T(8,128)(2,1)} collective-permute-done((bf16[384,1152]{1,0:T(8,128)(2,1)S(1)}, bf16[384,1152]{1,0:T(8,128)(2,1)}, u32[]{:S(2)}, u32[]{:S(2)}) %collective-permute-start.9) | collective-permute-done | bytes 884768 | tf_op jit(solution)/shard_map/ppermute | solution.py:301
  77.4 0.6 collective-permute-start.15
  78.0 0.5 collective-permute-start.17
  78.5 0.6 reshape.277.ba_ref
  79.1 6.1 %pick.4.refs_0_ = bf16[1024,1152]{1,0:T(8,128)(2,1)S(1)} custom-call(s32[1024,1]{1,0:T(8,128)S(1)} %fusion.5.idx_ref, bf16[1024,1152]{1,0:T(8,128)(2,1)S(1)} %pick.3.refs_0_, bf16[384,1152]{1,0:T(8,128)(2,1)S(1)} %constant_dynamic-update-slice_fusion.refs_1_, bf16[384,1152]{1,0:T(8,128)(2,1)} %collective-permute-done.8.refs_2_, ...), custom_call_target="tpu_custom_call", output_to_operand_aliasing={{}: (1, {})} | custom-call | flops 1 | bytes 1 | tf_op jit(solution)/shard_map/pick/pallas_call | solution.py:48
  85.3 4.5 %pick.5.act_ref = bf16[1024,1152]{1,0:T(8,128)(2,1)S(1)} custom-call(s32[1024,1]{1,0:T(8,128)S(1)} %fusion.5.idx_ref, bf16[1024,1152]{1,0:T(8,128)(2,1)S(1)} %pick.4.refs_0_, bf16[384,1152]{1,0:T(8,128)(2,1)S(1)} %collective-permute-done.15.refs_1_, bf16[384,1152]{1,0:T(8,128)(2,1)S(1)} %collective-permute-done.16.refs_2_, ...), custom_call_target="tpu_custom_call", output_to_operand_aliasing={{}: (1, {})} | custom-call | flops 1 | bytes 1 | tf_op jit(solution)/shard_map/pick/pallas_call | solution.py:48
  89.8 1.4 copy-done.1
  91.2 20.7 %stretch.1 = (bf16[2304,1024]{1,0:T(8,128)(2,1)}, bf16[1024,1152]{1,0:T(8,128)(2,1)}) custom-call(bf16[1024,1152]{1,0:T(8,128)(2,1)} %copy-done.1, bf16[1152,3456]{1,0:T(8,128)(2,1)} %wa_ref.3, f32[1,3456]{1,0:T(1,128)} %reshape.277.ba_ref, bf16[1024,1152]{1,0:T(8,128)(2,1)} %bitcast.7.tok_ref, bf16[1152,3456]{1,0:T(8,128)(2,1)} %wq_ref.3), custom_call_target="tpu_custom_call" | custom-call | flops 1 | bytes 1 | tf_op jit(solution)/shard_map/stretch/pallas_call | solution.py:126
  111.9 0.6 collective-permute-start.19
  112.5 0.6 pad_add_fusion.place_ref
  113.0 9.7 %query.1 = (bf16[1152,512]{1,0:T(8,128)(2,1)}, bf16[512,1152]{1,0:T(8,128)(2,1)}) custom-call(s32[2]{0:T(128)} %pad_add_fusion.place_ref, bf16[1024,1152]{1,0:T(8,128)(2,1)} %copy-done.1, bf16[1024,1152]{1,0:T(8,128)(2,1)} %get-tuple-element.45.x_ref, f32[1,3456]{1,0:T(1,128)} %reshape.277.ba_ref, bf16[1152,3456]{1,0:T(8,128)(2,1)} %wa_ref.3, ...), custom_call_target="tpu_custom_call" | custom-call | flops 1 | bytes 1 | tf_op jit(solution)/shard_map/query/pallas_call | solution.py:181
  122.7 1.3 copy-done.17
  124.0 12.0 %attend.3.att_ref = bf16[1152,256]{1,0:T(8,128)(2,1)S(1)} custom-call(bf16[1152,512]{1,0:T(8,128)(2,1)S(1)} %copy-done.17, bf16[2304,1024]{1,0:T(8,128)(2,1)S(1)} %copy-done.16, bf16[2304,1024]{1,0:T(8,128)(2,1)} %collective-permute-done.19.refs_1_.refs_3_, bf16[2304,1024]{1,0:T(8,128)(2,1)S(1)} %copy-done.16, ...), custom_call_target="tpu_custom_call" | custom-call | flops 9663676416 | bytes 9437184 | tf_op jit(solution)/shard_map/attend/pallas_call | solution.py:253
  136.1 2.7 %finish.3 = bf16[256,1152]{1,0:T(8,128)(2,1)S(1)} custom-call(s32[2]{0:T(128)S(1)} %copy-done.15, bf16[1152,256]{1,0:T(8,128)(2,1)S(1)} %attend.3.att_ref, bf16[1024,1152]{1,0:T(8,128)(2,1)} %bitcast.7.tok_ref, bf16[512,1152]{1,0:T(8,128)(2,1)S(1)} %copy-done.3, bf16[1152,1152]{1,0:T(8,128)(2,1)S(1)} %copy-done.2), custom_call_target="tpu_custom_call" | custom-call | tf_op jit(solution)/shard_map/finish/pallas_call | solution.py:281
  138.9 11.6 %attend.2.att_ref = bf16[1152,256]{1,0:T(8,128)(2,1)S(1)} custom-call(bf16[1152,512]{1,0:T(8,128)(2,1)S(1)} %copy-done.17, bf16[2304,1024]{1,0:T(8,128)(2,1)S(1)} %copy-done.16, bf16[2304,1024]{1,0:T(8,128)(2,1)} %collective-permute-done.19.refs_1_.refs_3_, bf16[2304,1024]{1,0:T(8,128)(2,1)S(1)} %copy-done.16, ...), custom_call_target="tpu_custom_call" | custom-call | flops 9663676416 | bytes 9437184 | tf_op jit(solution)/shard_map/attend/pallas_call | solution.py:253
  150.5 2.7 %finish.2 = bf16[256,1152]{1,0:T(8,128)(2,1)S(1)} custom-call(s32[2]{0:T(128)S(1)} %copy-done.15, bf16[1152,256]{1,0:T(8,128)(2,1)S(1)} %attend.2.att_ref, bf16[1024,1152]{1,0:T(8,128)(2,1)} %bitcast.7.tok_ref, bf16[512,1152]{1,0:T(8,128)(2,1)S(1)} %copy-done.3, bf16[1152,1152]{1,0:T(8,128)(2,1)S(1)} %copy-done.2), custom_call_target="tpu_custom_call" | custom-call | tf_op jit(solution)/shard_map/finish/pallas_call | solution.py:281
  153.1 13.2 %collective-permute-done.20 = bf16[256,1152]{1,0:T(8,128)(2,1)S(1)} collective-permute-done((bf16[256,1152]{1,0:T(8,128)(2,1)S(1)}, bf16[256,1152]{1,0:T(8,128)(2,1)S(1)}, u32[]{:S(2)}, u32[]{:S(2)}) %collective-permute-start.20) | collective-permute-done | bytes 589856 | tf_op jit(solution)/shard_map/ppermute | solution.py:301
  166.5 0.8 collective-permute-start.21
  167.3 1.6 collective-permute-done.21
  169.1 1.1 maximum_bitcast_fusion
  (71 shorter events, 1.8 us)
Async XLA Ops:
  0.0 42.0 %copy-start = (s32[4096]{0:T(1024)S(1)}, s32[4096]{0:T(1024)}, u32[]{:S(2)}) copy-start(s32[4096]{0:T(1024)} %param.11) | copy-start | bytes 49156
  0.0 15.9 %copy-start.4 = (bf16[128,1152]{1,0:T(8,128)(2,1)S(1)}, bf16[128,1152]{1,0:T(8,128)(2,1)}, u32[]{:S(2)}) copy-start(bf16[128,1152]{1,0:T(8,128)(2,1)} %refs_0_) | copy-start | bytes 884740
  1.2 4.1 %collective-permute-start.3 = (bf16[256,1152]{1,0:T(8,128)(2,1)S(1)}, bf16[256,1152]{1,0:T(8,128)(2,1)S(1)}, u32[]{:S(2)}, u32[]{:S(2)}) collective-permute-start(bf16[256,1152]{1,0:T(8,128)(2,1)S(1)} %dynamic-slice_bitcast_fusion), channel_id=1, source_target_pairs={{0,4},{4,0},{8,12},{12,8},{16,20},{20,16},{24,28},{28,24},{1,5},{5... | collective-permute-start | bytes 1769480 | tf_op jit(solution)/shard_map/ppermute | solution.py:301
  1.9 14.0 %collective-permute-start.1 = (bf16[128,1152]{1,0:T(8,128)(2,1)}, bf16[128,1152]{1,0:T(8,128)(2,1)S(1)}, u32[]{:S(2)}, u32[]{:S(2)}) collective-permute-start(bf16[128,1152]{1,0:T(8,128)(2,1)} %refs_0_), channel_id=1, source_target_pairs={{0,2},{1,3},{2,0},{3,1},{4,6},{5,7},{6,4},{7,5},{8,10},{9,11},{10,... | collective-permute-start | bytes 884744 | tf_op jit(solution)/shard_map/ppermute | solution.py:301
  1.9 29.2 %collective-permute-start = (bf16[128,1152]{1,0:T(8,128)(2,1)}, bf16[128,1152]{1,0:T(8,128)(2,1)S(1)}, u32[]{:S(2)}, u32[]{:S(2)}) collective-permute-start(bf16[128,1152]{1,0:T(8,128)(2,1)} %refs_0_), channel_id=1, source_target_pairs={{0,1},{1,0},{2,3},{3,2},{4,5},{5,4},{6,7},{7,6},{8,9},{9,8},{10,11... | collective-permute-start | bytes 884744 | tf_op jit(solution)/shard_map/ppermute | solution.py:301
  3.3 27.8 %collective-permute-start.2 = (bf16[128,1152]{1,0:T(8,128)(2,1)}, bf16[128,1152]{1,0:T(8,128)(2,1)S(1)}, u32[]{:S(2)}, u32[]{:S(2)}) collective-permute-start(bf16[128,1152]{1,0:T(8,128)(2,1)} %refs_0_), channel_id=1, source_target_pairs={{0,3},{1,2},{2,1},{3,0},{4,7},{5,6},{6,5},{7,4},{8,11},{9,10},{10,... | collective-permute-start | bytes 884744 | tf_op jit(solution)/shard_map/ppermute | solution.py:301
  5.2 25.9 %collective-permute-start.6 = (bf16[128,1152]{1,0:T(8,128)(2,1)}, bf16[128,1152]{1,0:T(8,128)(2,1)S(1)}, u32[]{:S(2)}, u32[]{:S(2)}) collective-permute-start(bf16[128,1152]{1,0:T(8,128)(2,1)} %refs_0_), channel_id=1, source_target_pairs={{0,24},{4,28},{8,16},{12,20},{16,8},{20,12},{24,0},{28,4},{1,25},{... | collective-permute-start | bytes 884744 | tf_op jit(solution)/shard_map/ppermute | solution.py:301
  7.5 23.7 %collective-permute-start.5 = (bf16[128,1152]{1,0:T(8,128)(2,1)}, bf16[128,1152]{1,0:T(8,128)(2,1)S(1)}, u32[]{:S(2)}, u32[]{:S(2)}) collective-permute-start(bf16[128,1152]{1,0:T(8,128)(2,1)} %refs_0_), channel_id=1, source_target_pairs={{0,16},{4,20},{8,24},{12,28},{16,0},{20,4},{24,8},{28,12},{1,17},{... | collective-permute-start | bytes 884744 | tf_op jit(solution)/shard_map/ppermute | solution.py:301
  9.0 22.1 %all-to-all-start = ((s32[4,1,512]{2,1,0:T(1,128)}), s32[4,1,512]{2,1,0:T(1,128)S(1)}, u32[]{:S(2)}, u32[]{:S(2)}) async-start(s32[4,1,512]{2,1,0:T(1,128)} %broadcast_in_dim.46), calls=%async_computation | async-start | bytes 16384 | tf_op jit(solution)/shard_map/all_to_all | solution.py:337
  15.9 15.3 %collective-permute-start.4 = (bf16[128,1152]{1,0:T(8,128)(2,1)S(1)}, bf16[128,1152]{1,0:T(8,128)(2,1)S(1)}, u32[]{:S(2)}, u32[]{:S(2)}) collective-permute-start(bf16[128,1152]{1,0:T(8,128)(2,1)S(1)} %copy-done.4), channel_id=1, source_target_pairs={{0,8},{4,12},{8,0},{12,4},{16,24},{20,28},{24,16},{28,20},{1,9},{5... | collective-permute-start | bytes 884744 | tf_op jit(solution)/shard_map/ppermute | solution.py:301
  31.1 17.5 %copy-start.5 = (bf16[128,1152]{1,0:T(8,128)(2,1)}, bf16[128,1152]{1,0:T(8,128)(2,1)S(1)}, u32[]{:S(2)}) copy-start(bf16[128,1152]{1,0:T(8,128)(2,1)S(1)} %collective-permute-done.6.refs_3_) | copy-start | bytes 884740
  31.1 17.2 %copy-start.7 = (bf16[128,1152]{1,0:T(8,128)(2,1)}, bf16[128,1152]{1,0:T(8,128)(2,1)S(1)}, u32[]{:S(2)}) copy-start(bf16[128,1152]{1,0:T(8,128)(2,1)S(1)} %collective-permute-done.5.refs_2_) | copy-start | bytes 884740
  31.2 10.1 %copy-start.9 = (bf16[128,1152]{1,0:T(8,128)(2,1)}, bf16[128,1152]{1,0:T(8,128)(2,1)S(1)}, u32[]{:S(2)}) copy-start(bf16[128,1152]{1,0:T(8,128)(2,1)S(1)} %collective-permute-done.4.refs_1_) | copy-start | bytes 884740
  31.2 60.0 %all-to-all-start.1 = ((bf16[4,256,1152]{2,1,0:T(8,128)(2,1)}), bf16[4,256,1152]{2,1,0:T(8,128)(2,1)}, u32[]{:S(2)}, u32[]{:S(2)}) async-start(bf16[4,256,1152]{2,1,0:T(8,128)(2,1)} %broadcast_select_fusion), calls=%async_computation.1 | async-start | bytes 4718592 | tf_op jit(solution)/shard_map/all_to_all | solution.py:347
  35.8 22.5 %collective-permute-start.10 = (bf16[384,1152]{1,0:T(8,128)(2,1)S(1)}, bf16[384,1152]{1,0:T(8,128)(2,1)}, u32[]{:S(2)}, u32[]{:S(2)}) collective-permute-start(bf16[384,1152]{1,0:T(8,128)(2,1)S(1)} %constant_dynamic-update-slice_fusion.refs_1_), channel_id=1, source_target_pairs={{0,24},{4,28},{8,16},{12,20},{16,8},{20,12},{24,0},{28,4},{1,25},{... | collective-permute-start | bytes 2654216 | tf_op jit(solution)/shard_map/ppermute | solution.py:301
  38.0 39.4 %collective-permute-start.9 = (bf16[384,1152]{1,0:T(8,128)(2,1)S(1)}, bf16[384,1152]{1,0:T(8,128)(2,1)}, u32[]{:S(2)}, u32[]{:S(2)}) collective-permute-start(bf16[384,1152]{1,0:T(8,128)(2,1)S(1)} %constant_dynamic-update-slice_fusion.refs_1_), channel_id=1, source_target_pairs={{0,16},{4,20},{8,24},{12,28},{16,0},{20,4},{24,8},{28,12},{1,17},{... | collective-permute-start | bytes 2654216 | tf_op jit(solution)/shard_map/ppermute | solution.py:301
  38.2 39.1 %collective-permute-start.8 = (bf16[384,1152]{1,0:T(8,128)(2,1)S(1)}, bf16[384,1152]{1,0:T(8,128)(2,1)}, u32[]{:S(2)}, u32[]{:S(2)}) collective-permute-start(bf16[384,1152]{1,0:T(8,128)(2,1)S(1)} %constant_dynamic-update-slice_fusion.refs_1_), channel_id=1, source_target_pairs={{0,8},{4,12},{8,0},{12,4},{16,24},{20,28},{24,16},{28,20},{1,9},{5... | collective-permute-start | bytes 2654216 | tf_op jit(solution)/shard_map/ppermute | solution.py:301
  38.5 2.8 %collective-permute-start.7 = (s32[4,512]{1,0:T(4,128)S(1)}, s32[4,512]{1,0:T(4,128)S(1)}, u32[]{:S(2)}, u32[]{:S(2)}) collective-permute-start(s32[4,512]{1,0:T(4,128)S(1)} %bitcast.34), channel_id=1, source_target_pairs={{0,4},{4,0},{8,12},{12,8},{16,20},{20,16},{24,28},{28,24},{1,5},{5... | collective-permute-start | bytes 24584 | tf_op jit(solution)/shard_map/ppermute | solution.py:301
  40.4 7.9 %collective-permute-start.11 = (bf16[128,1152]{1,0:T(8,128)(2,1)S(1)}, bf16[128,1152]{1,0:T(8,128)(2,1)S(1)}, u32[]{:S(2)}, u32[]{:S(2)}) collective-permute-start(bf16[128,1152]{1,0:T(8,128)(2,1)S(1)} %copy-done.4), channel_id=1, source_target_pairs={{0,4},{4,0},{8,12},{12,8},{16,20},{20,16},{24,28},{28,24},{1,5},{5... | collective-permute-start | bytes 884744 | tf_op jit(solution)/shard_map/ppermute | solution.py:301
  41.3 7.4 %collective-permute-start.12 = (bf16[128,1152]{1,0:T(8,128)(2,1)S(1)}, bf16[128,1152]{1,0:T(8,128)(2,1)S(1)}, u32[]{:S(2)}, u32[]{:S(2)}) collective-permute-start(bf16[128,1152]{1,0:T(8,128)(2,1)S(1)} %collective-permute-done.4.refs_1_), channel_id=1, source_target_pairs={{0,4},{4,0},{8,12},{12,8},{16,20},{20,16},{24,28},{28,24},{1,5},{5... | collective-permute-start | bytes 884744 | tf_op jit(solution)/shard_map/ppermute | solution.py:301
  48.4 1.7 %copy-start.11 = (bf16[128,1152]{1,0:T(8,128)(2,1)}, bf16[128,1152]{1,0:T(8,128)(2,1)S(1)}, u32[]{:S(2)}) copy-start(bf16[128,1152]{1,0:T(8,128)(2,1)S(1)} %collective-permute-done.11.refs_4_) | copy-start | bytes 884740
  48.4 1.7 collective-permute-start.13
  48.6 1.5 copy-start.13
  48.6 1.8 %collective-permute-start.14 = (bf16[128,1152]{1,0:T(8,128)(2,1)S(1)}, bf16[128,1152]{1,0:T(8,128)(2,1)S(1)}, u32[]{:S(2)}, u32[]{:S(2)}) collective-permute-start(bf16[128,1152]{1,0:T(8,128)(2,1)S(1)} %collective-permute-done.6.refs_3_), channel_id=1, source_target_pairs={{0,4},{4,0},{8,12},{12,8},{16,20},{20,16},{24,28},{28,24},{1,5},{5... | collective-permute-start | bytes 884744 | tf_op jit(solution)/shard_map/ppermute | solution.py:301
  49.0 29.5 %copy-start.18 = (f32[3456]{0:T(1024)S(1)}, f32[3456]{0:T(1024)}, u32[]{:S(2)}) copy-start(f32[3456]{0:T(1024)} %param.15) | copy-start | bytes 41476
  50.5 1.0 copy-start.6
  51.4 1.0 copy-start.8
  52.4 1.0 copy-start.10
  53.3 1.0 copy-start.12
  54.3 1.0 copy-start.14
  77.4 7.9 %collective-permute-start.15 = (bf16[384,1152]{1,0:T(8,128)(2,1)S(1)}, bf16[384,1152]{1,0:T(8,128)(2,1)S(1)}, u32[]{:S(2)}, u32[]{:S(2)}) collective-permute-start(bf16[384,1152]{1,0:T(8,128)(2,1)S(1)} %constant_dynamic-update-slice_fusion.refs_1_), channel_id=1, source_target_pairs={{0,4},{4,0},{8,12},{12,8},{16,20},{20,16},{24,28},{28,24},{1,5},{5... | collective-permute-start | bytes 2654216 | tf_op jit(solution)/shard_map/ppermute | solution.py:301
  78.0 7.3 %collective-permute-start.16 = (bf16[384,1152]{1,0:T(8,128)(2,1)}, bf16[384,1152]{1,0:T(8,128)(2,1)S(1)}, u32[]{:S(2)}, u32[]{:S(2)}) collective-permute-start(bf16[384,1152]{1,0:T(8,128)(2,1)} %collective-permute-done.8.refs_2_), channel_id=1, source_target_pairs={{0,4},{4,0},{8,12},{12,8},{16,20},{20,16},{24,28},{28,24},{1,5},{5... | collective-permute-start | bytes 2654216 | tf_op jit(solution)/shard_map/ppermute | solution.py:301
  78.0 7.3 %collective-permute-start.17 = (bf16[384,1152]{1,0:T(8,128)(2,1)}, bf16[384,1152]{1,0:T(8,128)(2,1)S(1)}, u32[]{:S(2)}, u32[]{:S(2)}) collective-permute-start(bf16[384,1152]{1,0:T(8,128)(2,1)} %collective-permute-done.9.refs_3_), channel_id=1, source_target_pairs={{0,4},{4,0},{8,12},{12,8},{16,20},{20,16},{24,28},{28,24},{1,5},{5... | collective-permute-start | bytes 2654216 | tf_op jit(solution)/shard_map/ppermute | solution.py:301
  78.5 6.8 %collective-permute-start.18 = (bf16[384,1152]{1,0:T(8,128)(2,1)}, bf16[384,1152]{1,0:T(8,128)(2,1)S(1)}, u32[]{:S(2)}, u32[]{:S(2)}) collective-permute-start(bf16[384,1152]{1,0:T(8,128)(2,1)} %collective-permute-done.10.refs_4_), channel_id=1, source_target_pairs={{0,4},{4,0},{8,12},{12,8},{16,20},{20,16},{24,28},{28,24},{1,5},{5... | collective-permute-start | bytes 2654216 | tf_op jit(solution)/shard_map/ppermute | solution.py:301
  89.7 1.4 copy-start.1
  111.9 10.8 %collective-permute-start.19 = (bf16[2304,1024]{1,0:T(8,128)(2,1)}, bf16[2304,1024]{1,0:T(8,128)(2,1)}, u32[]{:S(2)}, u32[]{:S(2)}) collective-permute-start(bf16[2304,1024]{1,0:T(8,128)(2,1)} %get-tuple-element.47.refs_0_.refs_2_), channel_id=1, source_target_pairs={{0,4},{4,0},{8,12},{12,8},{16,20},{20,16},{24,28},{28,24},{1,5},{5... | collective-permute-start | bytes 14155784 | tf_op jit(solution)/shard_map/ppermute | solution.py:301
  113.0 9.7 %copy-start.16 = (bf16[2304,1024]{1,0:T(8,128)(2,1)S(1)}, bf16[2304,1024]{1,0:T(8,128)(2,1)}, u32[]{:S(2)}) copy-start(bf16[2304,1024]{1,0:T(8,128)(2,1)} %get-tuple-element.47.refs_0_.refs_2_) | copy-start | bytes 14155780
  122.7 1.3 copy-start.17
  124.0 12.0 %copy-start.2 = (bf16[1152,1152]{1,0:T(8,128)(2,1)S(1)}, bf16[1152,1152]{1,0:T(8,128)(2,1)}, u32[]{:S(2)}) copy-start(bf16[1152,1152]{1,0:T(8,128)(2,1)} %w_ref.3) | copy-start | bytes 7962628
  124.0 12.0 %copy-start.3 = (bf16[512,1152]{1,0:T(8,128)(2,1)S(1)}, bf16[512,1152]{1,0:T(8,128)(2,1)}, u32[]{:S(2)}) copy-start(bf16[512,1152]{1,0:T(8,128)(2,1)} %get-tuple-element.48.gate_ref) | copy-start | bytes 3538948
  124.0 12.1 %copy-start.15 = (s32[2]{0:T(128)S(1)}, s32[2]{0:T(128)}, u32[]{:S(2)}) copy-start(s32[2]{0:T(128)} %pad_add_fusion.place_ref) | copy-start | bytes 28
  138.7 27.7 %collective-permute-start.20 = (bf16[256,1152]{1,0:T(8,128)(2,1)S(1)}, bf16[256,1152]{1,0:T(8,128)(2,1)S(1)}, u32[]{:S(2)}, u32[]{:S(2)}) collective-permute-start(bf16[256,1152]{1,0:T(8,128)(2,1)S(1)} %finish.3), channel_id=1, source_target_pairs={{0,3},{1,2},{2,1},{3,0},{4,7},{5,6},{6,5},{7,4},{8,11},{9,10},{10,... | collective-permute-start | bytes 1769480 | tf_op jit(solution)/shard_map/ppermute | solution.py:301
  166.5 2.5 %collective-permute-start.21 = (bf16[256,1152]{1,0:T(8,128)(2,1)S(1)}, bf16[256,1152]{1,0:T(8,128)(2,1)S(1)}, u32[]{:S(2)}, u32[]{:S(2)}) collective-permute-start(bf16[256,1152]{1,0:T(8,128)(2,1)S(1)} %broadcast_select_fusion.3), channel_id=1, source_target_pairs={{0,4},{4,0},{8,12},{12,8},{16,20},{20,16},{24,28},{28,24},{1,5},{5... | collective-permute-start | bytes 1769480 | tf_op jit(solution)/shard_map/ppermute | solution.py:301

commit v6 on v5

--- a/solution.py
+++ b/solution.py
@@ -155,9 +155,8 @@
 
 
 def query_kernel(query_scale, place_ref, act_ref, x_ref, ba_ref, wa_ref, wq_ref, *refs):
-    q_ref, gate_ref, wa_buf, wq_buf, sems = refs
-    count, width = gate_ref.shape
-    half = count // 2
+    q_ref, gate_ref, late_ref, wa_buf, wq_buf, sems = refs
+    half, width = gate_ref.shape
     copies = [
         pltpu.make_async_copy(wq_ref.at[:, :width], wq_buf, sems.at[0]),
         pltpu.make_async_copy(wa_ref.at[:, 2 * width :], wa_buf, sems.at[1]),
@@ -166,8 +165,8 @@
         copy.start()
     rows = [pl.ds(pl.multiple_of(place_ref[k] * half, half), half) for k in range(2)]
     x = jnp.concatenate([x_ref[span, :] for span in rows], axis=0)
-    act = jnp.concatenate([act_ref[span, :] for span in rows], axis=0)
-    act = jax.nn.silu(act.astype(F32)).astype(BF16)
+    act = jax.nn.silu(act_ref[rows[0], :].astype(F32)).astype(BF16)
+    late_ref[...] = act_ref[rows[1], :]
     copies[0].wait()
     q_ref[...] = (contract(wq_buf[...], x, ((0,), (1,))) * query_scale).astype(BF16)
     copies[1].wait()
@@ -181,10 +180,11 @@
     return pl.pallas_call(
         functools.partial(query_kernel, query_scale),
         in_specs=[pl.BlockSpec(memory_space=pltpu.SMEM), VMEM, VMEM, VMEM, HBM, HBM],
-        out_specs=[VMEM, VMEM],
+        out_specs=[VMEM, VMEM, VMEM],
         out_shape=[
             jax.ShapeDtypeStruct((width, count), BF16),
-            jax.ShapeDtypeStruct((count, width), BF16),
+            jax.ShapeDtypeStruct((count // 2, width), BF16),
+            jax.ShapeDtypeStruct((count // 2, width), BF16),
         ],
         scratch_shapes=[
             pltpu.VMEM((width, width), BF16),
@@ -195,6 +195,30 @@
         cost_estimate=pl.CostEstimate(flops=1, bytes_accessed=1, transcendentals=0),
         name="query",
     )(place, picked, x, b_ada, w_ada, w_qkv)
+
+
+def gate_kernel(act_ref, ba_ref, wa_ref, gate_ref, wa_buf, sem):
+    width = gate_ref.shape[1]
+    copy = pltpu.make_async_copy(wa_ref.at[:, 2 * width :], wa_buf, sem.at[0])
+    copy.start()
+    act = jax.nn.silu(act_ref[...].astype(F32)).astype(BF16)
+    copy.wait()
+    gate = contract(act, wa_buf[...], ((1,), (0,))) + ba_ref[:, 2 * width :]
+    gate_ref[...] = gate.astype(BF16)
+
+
+def own_gate(rows, w_ada, b_ada):
+    block, width = rows.shape
+    return pl.pallas_call(
+        gate_kernel,
+        in_specs=[VMEM, VMEM, HBM],
+        out_specs=VMEM,
+        out_shape=jax.ShapeDtypeStruct((block, width), BF16),
+        scratch_shapes=[pltpu.VMEM((width, width), BF16), pltpu.SemaphoreType.DMA((1,))],
+        compiler_params=pltpu.CompilerParams(vmem_limit_bytes=58 * MIB),
+        cost_estimate=pl.CostEstimate(flops=1, bytes_accessed=1, transcendentals=0),
+        name="own_gate",
+    )(rows, b_ada, w_ada)
 
 
 def attend_kernel(head_dim, chunk, q_ref, *refs):
@@ -276,7 +300,7 @@
 
 def finish(place, which, attended, tok, gate, w_out):
     width, queries = attended.shape
-    at = pl.BlockSpec((queries, width), lambda i, place: (which, 0))
+    at = pl.BlockSpec((queries, width), lambda i, place: (0, 0))
     tok_at = pl.BlockSpec((queries, width), lambda i, place: (place[which], 0))
     return pl.pallas_call(
         finish_kernel,
@@ -371,11 +395,13 @@
     bias = b_ada.reshape(1, -1)
     kv, x = stretch(tok, picked, w_ada, bias, w_qkv)
     kvs = [kv, swap(kv, "region", 1)]
-    qt, gate = query(place, x, picked, w_ada, bias, w_qkv, 2 * block)
+    qt, gate, late = query(place, x, picked, w_ada, bias, w_qkv, 2 * block)
 
     there = finish(place, 0, attend(0, qt, kvs), tok, gate, w_out)
     back = swap(there, "ctx", n - 1)
-    here = finish(place, 1, attend(1, qt, kvs), tok, gate, w_out)
+    attended = attend(1, qt, kvs)
+    late = after(late, there, attended)
+    here = finish(place, 1, attended, tok, own_gate(late, w_ada, bias), w_out)
     here, back = lax.optimization_barrier((here, back))
     mine, given = jnp.where(core == upper, here, back), jnp.where(core == upper, back, here)
     other = swap(given, "region", 1)

time: 171 us -> 172 us (level)
  waiting for transfers between devices: 48.2 us -> 42.5 us
  local copies, waits for them, and re-layouts: 16.7 us -> 20.1 us
  Pallas kernels: 72.9 us -> 76 us
    ppermute x22, waiting for transfers between devices: 35.2 us -> 29.5 us  [swap(): lax.ppermute(x, axis, [(i, i ^ bits) for i in range(lax.axis_size(axis))])]
    pallas_call x0 -> x1, Pallas kernels: none -> 4.64 us  [own_gate(): pl.pallas_call(gate_kernel, in_specs=[VMEM, VMEM, HBM], out_specs=VMEM, o...]
    unnamed x44 -> x48, local copies, waits for them, and re-layouts: 7.91 us -> 11.3 us
    pallas_call x1, Pallas kernels: 9.67 us -> 7.9 us  [query(): pl.pallas_call(functools.partial(query_kernel, query_scale), in_specs=[pl...]
  transfers between devices with their start and end apart: 24 -> 24, of which waited for: 6 -> 6; matrix products, arithmetic and copies ran while one was open for 8% -> 8% of each run, Pallas kernels for 22% -> 24%
where the time goes in v6:
time: 172 us; the launch traced here: 171 us
  Pallas kernels  76 us (44%)
  waiting for transfers between devices  42.5 us (25%)
  starting transfers between devices  24.5 us (14%)
  local copies, waits for them, and re-layouts  20.1 us (12%)
  other arithmetic  6.88 us (4%)
    ppermute x22, waiting for transfers between devices, swap(): lax.ppermute(x, axis, [(i, i ^ bits) for i in range(lax.axis_size(axis))])  29.5 us
    pallas_call x2, Pallas kernels, attend(): pl.pallas_call(functools.partial(attend_kernel, head_dim, chunk), grid=(s...  23.6 us
    pallas_call x1, Pallas kernels, stretch(): pl.pallas_call(functools.partial(stretch_kernel, steps), grid=(steps + 2,...  20.7 us
    ppermute x22, starting transfers between devices, swap(): lax.ppermute(x, axis, [(i, i ^ bits) for i in range(lax.axis_size(axis))])  14.5 us
    pallas_call x3, Pallas kernels, pick_rows(): pl.pallas_call(functools.partial(pick_kernel, bases, block), in_specs=[VM...  13.5 us
    all_to_all x1, waiting for transfers between devices, per_device(): lax.all_to_all(jnp.broadcast_to(ids, (n, tok_rows)), 'ctx', split_axis=0,...  13 us
    unnamed x48, local copies, waits for them, and re-layouts  11.3 us
    pallas_call x1, Pallas kernels, query(): pl.pallas_call(functools.partial(query_kernel, query_scale), in_specs=[pl...  7.9 us
  transfers between devices with their start and end apart: 24, of which 6 were waited for; matrix products, arithmetic and copies ran while one was open for 8% of the time, Pallas kernels for 24%

profile of v6, /device:TPU:17, one launch (start us, length us, event | category | flops | bytes accessed | tf_op | source)
XLA Modules:
  0.0 171.0 jit_solution(1143084467130838553)
XLA Ops:
  0.0 1.2 dynamic-slice_bitcast_fusion
  1.2 0.7 collective-permute-start.3
  1.9 1.4 collective-permute-start
  3.3 1.3 collective-permute-start.2
  5.2 2.2 %collective-permute-start.6 = (bf16[128,1152]{1,0:T(8,128)(2,1)}, bf16[128,1152]{1,0:T(8,128)(2,1)S(1)}, u32[]{:S(2)}, u32[]{:S(2)}) collective-permute-start(bf16[128,1152]{1,0:T(8,128)(2,1)} %refs_0_), channel_id=1, source_target_pairs={{0,24},{4,28},{8,16},{12,20},{16,8},{20,12},{24,0},{28,4},{1,25},{... | collective-permute-start | bytes 884744 | tf_op jit(solution)/shard_map/ppermute | solution.py:325
  7.7 0.7 fusion.13
  8.4 0.6 broadcast_in_dim.46
  9.0 5.5 %all-to-all-start = ((s32[4,1,512]{2,1,0:T(1,128)}), s32[4,1,512]{2,1,0:T(1,128)S(1)}, u32[]{:S(2)}, u32[]{:S(2)}) async-start(s32[4,1,512]{2,1,0:T(1,128)} %broadcast_in_dim.46), calls=%async_computation | async-start | bytes 16384 | tf_op jit(solution)/shard_map/all_to_all | solution.py:361
  14.5 1.3 broadcast_select_fusion.2
  16.2 1.9 %broadcast_select_fusion = bf16[4,256,1152]{2,1,0:T(8,128)(2,1)} fusion(pred[4]{0:T(512)(128)(4,1)S(1)} %fusion.14, bf16[256,1152]{1,0:T(8,128)(2,1)S(1)} %get-tuple-element.58, bf16[256,1152]{1,0:T(8,128)(2,1)S(1)} %get-tuple-element.57), kind=kLoop, calls=%fused_computation.1 | loop fusion | flops 1179648 | bytes 3538948 | tf_op jit(solution)/shard_map/jit(_where)/select_n | solution.py:367
  18.1 13.0 %all-to-all-done = s32[4,1,512]{2,1,0:T(1,128)S(1)} async-done(((s32[4,1,512]{2,1,0:T(1,128)}), s32[4,1,512]{2,1,0:T(1,128)S(1)}, u32[]{:S(2)}, u32[]{:S(2)}) %all-to-all-start) | async-done | bytes 8224 | tf_op jit(solution)/shard_map/all_to_all | solution.py:361
  31.2 4.5 %all-to-all-start.1 = ((bf16[4,256,1152]{2,1,0:T(8,128)(2,1)}), bf16[4,256,1152]{2,1,0:T(8,128)(2,1)}, u32[]{:S(2)}, u32[]{:S(2)}) async-start(bf16[4,256,1152]{2,1,0:T(8,128)(2,1)} %broadcast_select_fusion), calls=%async_computation.1 | async-start | bytes 4718592 | tf_op jit(solution)/shard_map/all_to_all | solution.py:371
  35.8 2.2 %collective-permute-start.10 = (bf16[384,1152]{1,0:T(8,128)(2,1)S(1)}, bf16[384,1152]{1,0:T(8,128)(2,1)}, u32[]{:S(2)}, u32[]{:S(2)}) collective-permute-start(bf16[384,1152]{1,0:T(8,128)(2,1)S(1)} %constant_dynamic-update-slice_fusion.refs_1_), channel_id=1, source_target_pairs={{0,24},{4,28},{8,16},{12,20},{16,8},{20,12},{24,0},{28,4},{1,25},{... | collective-permute-start | bytes 2654216 | tf_op jit(solution)/shard_map/ppermute | solution.py:325
  38.5 1.9 %collective-permute-start.7 = (s32[4,512]{1,0:T(4,128)S(1)}, s32[4,512]{1,0:T(4,128)S(1)}, u32[]{:S(2)}, u32[]{:S(2)}) collective-permute-start(s32[4,512]{1,0:T(4,128)S(1)} %bitcast.34), channel_id=1, source_target_pairs={{0,4},{4,0},{8,12},{12,8},{16,20},{20,16},{24,28},{28,24},{1,5},{5... | collective-permute-start | bytes 24584 | tf_op jit(solution)/shard_map/ppermute | solution.py:325
  40.4 0.8 collective-permute-done.7
  42.0 6.2 %gather_fusion = s32[1024]{0:T(1024)S(1)} fusion(s32[4096]{0:T(1024)S(1)} %copy-done, s32[1024]{0:T(1024)S(1)} %broadcast_clamp_fusion), kind=kCustom, calls=%fused_computation | custom fusion | bytes 12288 | tf_op jit(solution)/shard_map/gather | solution.py:376
  48.6 0.4 collective-permute-start.14
  49.0 1.0 fusion.5.idx_ref
  50.1 0.4 collective-permute-done.14.refs_7_
  50.5 1.0 copy-done.7
  51.4 1.0 copy-done.9
  52.4 1.0 copy-done.11
  53.3 1.0 copy-done.13
  54.3 1.0 copy-done.15
  55.3 3.0 %pick.3.refs_0_ = bf16[1024,1152]{1,0:T(8,128)(2,1)S(1)} custom-call(s32[1024,1]{1,0:T(8,128)S(1)} %fusion.5.idx_ref, bf16[128,1152]{1,0:T(8,128)(2,1)S(1)} %copy-done.5, bf16[128,1152]{1,0:T(8,128)(2,1)S(1)} %copy-done.11, bf16[128,1152]{1,0:T(8,128)(2,1)S(1)} %copy-done.9, bf16[128,1152]{1,0:T(8,128)(2,1)S(1)} %copy-done.7, ...), custom_call_target="tpu_custom_call" | custom-call | flops 1 | bytes 1 | tf_op jit(solution)/shard_map/pick/pallas_call | solution.py:48
  58.2 19.2 %collective-permute-done.9.refs_3_ = bf16[384,1152]{1,0:T(8,128)(2,1)} collective-permute-done((bf16[384,1152]{1,0:T(8,128)(2,1)S(1)}, bf16[384,1152]{1,0:T(8,128)(2,1)}, u32[]{:S(2)}, u32[]{:S(2)}) %collective-permute-start.9) | collective-permute-done | bytes 884768 | tf_op jit(solution)/shard_map/ppermute | solution.py:325
  77.4 0.6 collective-permute-start.15
  78.0 0.5 collective-permute-start.17
  78.5 0.6 reshape.277.ba_ref
  79.1 6.1 %pick.4.refs_0_ = bf16[1024,1152]{1,0:T(8,128)(2,1)S(1)} custom-call(s32[1024,1]{1,0:T(8,128)S(1)} %fusion.5.idx_ref, bf16[1024,1152]{1,0:T(8,128)(2,1)S(1)} %pick.3.refs_0_, bf16[384,1152]{1,0:T(8,128)(2,1)S(1)} %constant_dynamic-update-slice_fusion.refs_1_, bf16[384,1152]{1,0:T(8,128)(2,1)} %collective-permute-done.8.refs_2_, ...), custom_call_target="tpu_custom_call", output_to_operand_aliasing={{}: (1, {})} | custom-call | flops 1 | bytes 1 | tf_op jit(solution)/shard_map/pick/pallas_call | solution.py:48
  85.3 4.4 %pick.5.act_ref = bf16[1024,1152]{1,0:T(8,128)(2,1)S(1)} custom-call(s32[1024,1]{1,0:T(8,128)S(1)} %fusion.5.idx_ref, bf16[1024,1152]{1,0:T(8,128)(2,1)S(1)} %pick.4.refs_0_, bf16[384,1152]{1,0:T(8,128)(2,1)S(1)} %collective-permute-done.15.refs_1_, bf16[384,1152]{1,0:T(8,128)(2,1)S(1)} %collective-permute-done.16.refs_2_, ...), custom_call_target="tpu_custom_call", output_to_operand_aliasing={{}: (1, {})} | custom-call | flops 1 | bytes 1 | tf_op jit(solution)/shard_map/pick/pallas_call | solution.py:48
  89.8 1.4 copy-done.1
  91.2 20.7 %stretch.1 = (bf16[2304,1024]{1,0:T(8,128)(2,1)}, bf16[1024,1152]{1,0:T(8,128)(2,1)}) custom-call(bf16[1024,1152]{1,0:T(8,128)(2,1)} %copy-done.1, bf16[1152,3456]{1,0:T(8,128)(2,1)} %wa_ref.5, f32[1,3456]{1,0:T(1,128)} %reshape.277.ba_ref, bf16[1024,1152]{1,0:T(8,128)(2,1)} %bitcast.7.tok_ref, bf16[1152,3456]{1,0:T(8,128)(2,1)} %wq_ref.3), custom_call_target="tpu_custom_call" | custom-call | flops 1 | bytes 1 | tf_op jit(solution)/shard_map/stretch/pallas_call | solution.py:126
  111.9 0.6 collective-permute-start.19
  112.4 0.6 pad_add_fusion.place_ref
  113.1 7.9 %query.1 = (bf16[1152,512]{1,0:T(8,128)(2,1)}, bf16[256,1152]{1,0:T(8,128)(2,1)}, bf16[256,1152]{1,0:T(8,128)(2,1)}) custom-call(s32[2]{0:T(128)} %pad_add_fusion.place_ref, bf16[1024,1152]{1,0:T(8,128)(2,1)} %copy-done.1, bf16[1024,1152]{1,0:T(8,128)(2,1)} %get-tuple-element.47.x_ref, f32[1,3456]{1,0:T(1,128)} %reshape.277.ba_ref, ...), custom_call_target="tpu_custom_call" | custom-call | flops 1 | bytes 1 | tf_op jit(solution)/shard_map/query/pallas_call | solution.py:180
  121.0 2.3 %copy-done.17 = bf16[2304,1024]{1,0:T(8,128)(2,1)S(1)} copy-done((bf16[2304,1024]{1,0:T(8,128)(2,1)S(1)}, bf16[2304,1024]{1,0:T(8,128)(2,1)}, u32[]{:S(2)}) %copy-start.17) | copy-done | bytes 4718616
  123.3 1.3 copy-done.19
  124.6 12.0 %attend.3.att_ref = bf16[1152,256]{1,0:T(8,128)(2,1)S(1)} custom-call(bf16[1152,512]{1,0:T(8,128)(2,1)S(1)} %copy-done.19, bf16[2304,1024]{1,0:T(8,128)(2,1)S(1)} %copy-done.17, bf16[2304,1024]{1,0:T(8,128)(2,1)} %collective-permute-done.19.refs_1_.refs_3_, bf16[2304,1024]{1,0:T(8,128)(2,1)S(1)} %copy-done.17, ...), custom_call_target="tpu_custom_call" | custom-call | flops 9663676416 | bytes 9437184 | tf_op jit(solution)/shard_map/attend/pallas_call | solution.py:277
  136.6 2.9 %finish.2 = bf16[256,1152]{1,0:T(8,128)(2,1)S(1)} custom-call(s32[2]{0:T(128)S(1)} %copy-done.16, bf16[1152,256]{1,0:T(8,128)(2,1)S(1)} %attend.3.att_ref, bf16[1024,1152]{1,0:T(8,128)(2,1)} %bitcast.7.tok_ref, bf16[256,1152]{1,0:T(8,128)(2,1)S(1)} %copy-done.4, bf16[1152,1152]{1,0:T(8,128)(2,1)S(1)} %copy-done.2), custom_call_target="tpu_custom_call" | custom-call | tf_op jit(solution)/shard_map/finish/pallas_call | solution.py:305
  139.7 11.6 %attend.2.att_ref = bf16[1152,256]{1,0:T(8,128)(2,1)S(1)} custom-call(bf16[1152,512]{1,0:T(8,128)(2,1)S(1)} %copy-done.19, bf16[2304,1024]{1,0:T(8,128)(2,1)S(1)} %copy-done.18, bf16[2304,1024]{1,0:T(8,128)(2,1)} %collective-permute-done.19.refs_1_.refs_3_, bf16[2304,1024]{1,0:T(8,128)(2,1)S(1)} %copy-done.18, ...), custom_call_target="tpu_custom_call" | custom-call | flops 9663676416 | bytes 9437184 | tf_op jit(solution)/shard_map/attend/pallas_call | solution.py:277
  151.4 4.6 %own_gate.1.gate_ref = bf16[256,1152]{1,0:T(8,128)(2,1)} custom-call(bf16[256,1152]{1,0:T(8,128)(2,1)} %get-tuple-element.52.act_ref, f32[1,3456]{1,0:T(1,128)} %reshape.277.ba_ref, bf16[1152,3456]{1,0:T(8,128)(2,1)} %wa_ref.5), custom_call_target="tpu_custom_call" | custom-call | flops 1 | bytes 1 | tf_op jit(solution)/shard_map/own_gate/pallas_call | solution.py:212
  156.0 1.1 copy-done.3
  157.1 2.6 %finish.3 = bf16[256,1152]{1,0:T(8,128)(2,1)S(1)} custom-call(s32[2]{0:T(128)S(1)} %copy-done.16, bf16[1152,256]{1,0:T(8,128)(2,1)S(1)} %attend.2.att_ref, bf16[1024,1152]{1,0:T(8,128)(2,1)} %bitcast.7.tok_ref, bf16[256,1152]{1,0:T(8,128)(2,1)S(1)} %copy-done.3, bf16[1152,1152]{1,0:T(8,128)(2,1)S(1)} %copy-done.2), custom_call_target="tpu_custom_call" | custom-call | tf_op jit(solution)/shard_map/finish/pallas_call | solution.py:305
  159.7 7.5 %collective-permute-done.20 = bf16[256,1152]{1,0:T(8,128)(2,1)S(1)} collective-permute-done((bf16[256,1152]{1,0:T(8,128)(2,1)S(1)}, bf16[256,1152]{1,0:T(8,128)(2,1)S(1)}, u32[]{:S(2)}, u32[]{:S(2)}) %collective-permute-start.20) | collective-permute-done | bytes 589856 | tf_op jit(solution)/shard_map/ppermute | solution.py:325
  167.3 0.9 collective-permute-start.21
  168.2 1.6 collective-permute-done.21
  169.9 1.1 maximum_bitcast_fusion
  (76 shorter events, 2.7 us)
Async XLA Ops:
  0.0 42.0 %copy-start = (s32[4096]{0:T(1024)S(1)}, s32[4096]{0:T(1024)}, u32[]{:S(2)}) copy-start(s32[4096]{0:T(1024)} %param.11) | copy-start | bytes 49156
  0.0 15.9 %copy-start.5 = (bf16[128,1152]{1,0:T(8,128)(2,1)S(1)}, bf16[128,1152]{1,0:T(8,128)(2,1)}, u32[]{:S(2)}) copy-start(bf16[128,1152]{1,0:T(8,128)(2,1)} %refs_0_) | copy-start | bytes 884740
  1.2 4.1 %collective-permute-start.3 = (bf16[256,1152]{1,0:T(8,128)(2,1)S(1)}, bf16[256,1152]{1,0:T(8,128)(2,1)S(1)}, u32[]{:S(2)}, u32[]{:S(2)}) collective-permute-start(bf16[256,1152]{1,0:T(8,128)(2,1)S(1)} %dynamic-slice_bitcast_fusion), channel_id=1, source_target_pairs={{0,4},{4,0},{8,12},{12,8},{16,20},{20,16},{24,28},{28,24},{1,5},{5... | collective-permute-start | bytes 1769480 | tf_op jit(solution)/shard_map/ppermute | solution.py:325
  1.9 14.0 %collective-permute-start.1 = (bf16[128,1152]{1,0:T(8,128)(2,1)}, bf16[128,1152]{1,0:T(8,128)(2,1)S(1)}, u32[]{:S(2)}, u32[]{:S(2)}) collective-permute-start(bf16[128,1152]{1,0:T(8,128)(2,1)} %refs_0_), channel_id=1, source_target_pairs={{0,2},{1,3},{2,0},{3,1},{4,6},{5,7},{6,4},{7,5},{8,10},{9,11},{10,... | collective-permute-start | bytes 884744 | tf_op jit(solution)/shard_map/ppermute | solution.py:325
  1.9 29.2 %collective-permute-start = (bf16[128,1152]{1,0:T(8,128)(2,1)}, bf16[128,1152]{1,0:T(8,128)(2,1)S(1)}, u32[]{:S(2)}, u32[]{:S(2)}) collective-permute-start(bf16[128,1152]{1,0:T(8,128)(2,1)} %refs_0_), channel_id=1, source_target_pairs={{0,1},{1,0},{2,3},{3,2},{4,5},{5,4},{6,7},{7,6},{8,9},{9,8},{10,11... | collective-permute-start | bytes 884744 | tf_op jit(solution)/shard_map/ppermute | solution.py:325
  3.3 27.8 %collective-permute-start.2 = (bf16[128,1152]{1,0:T(8,128)(2,1)}, bf16[128,1152]{1,0:T(8,128)(2,1)S(1)}, u32[]{:S(2)}, u32[]{:S(2)}) collective-permute-start(bf16[128,1152]{1,0:T(8,128)(2,1)} %refs_0_), channel_id=1, source_target_pairs={{0,3},{1,2},{2,1},{3,0},{4,7},{5,6},{6,5},{7,4},{8,11},{9,10},{10,... | collective-permute-start | bytes 884744 | tf_op jit(solution)/shard_map/ppermute | solution.py:325
  5.2 25.9 %collective-permute-start.6 = (bf16[128,1152]{1,0:T(8,128)(2,1)}, bf16[128,1152]{1,0:T(8,128)(2,1)S(1)}, u32[]{:S(2)}, u32[]{:S(2)}) collective-permute-start(bf16[128,1152]{1,0:T(8,128)(2,1)} %refs_0_), channel_id=1, source_target_pairs={{0,24},{4,28},{8,16},{12,20},{16,8},{20,12},{24,0},{28,4},{1,25},{... | collective-permute-start | bytes 884744 | tf_op jit(solution)/shard_map/ppermute | solution.py:325
  7.5 23.7 %collective-permute-start.5 = (bf16[128,1152]{1,0:T(8,128)(2,1)}, bf16[128,1152]{1,0:T(8,128)(2,1)S(1)}, u32[]{:S(2)}, u32[]{:S(2)}) collective-permute-start(bf16[128,1152]{1,0:T(8,128)(2,1)} %refs_0_), channel_id=1, source_target_pairs={{0,16},{4,20},{8,24},{12,28},{16,0},{20,4},{24,8},{28,12},{1,17},{... | collective-permute-start | bytes 884744 | tf_op jit(solution)/shard_map/ppermute | solution.py:325
  9.0 22.1 %all-to-all-start = ((s32[4,1,512]{2,1,0:T(1,128)}), s32[4,1,512]{2,1,0:T(1,128)S(1)}, u32[]{:S(2)}, u32[]{:S(2)}) async-start(s32[4,1,512]{2,1,0:T(1,128)} %broadcast_in_dim.46), calls=%async_computation | async-start | bytes 16384 | tf_op jit(solution)/shard_map/all_to_all | solution.py:361
  15.9 15.3 %collective-permute-start.4 = (bf16[128,1152]{1,0:T(8,128)(2,1)S(1)}, bf16[128,1152]{1,0:T(8,128)(2,1)S(1)}, u32[]{:S(2)}, u32[]{:S(2)}) collective-permute-start(bf16[128,1152]{1,0:T(8,128)(2,1)S(1)} %copy-done.5), channel_id=1, source_target_pairs={{0,8},{4,12},{8,0},{12,4},{16,24},{20,28},{24,16},{28,20},{1,9},{5... | collective-permute-start | bytes 884744 | tf_op jit(solution)/shard_map/ppermute | solution.py:325
  31.1 17.5 %copy-start.6 = (bf16[128,1152]{1,0:T(8,128)(2,1)}, bf16[128,1152]{1,0:T(8,128)(2,1)S(1)}, u32[]{:S(2)}) copy-start(bf16[128,1152]{1,0:T(8,128)(2,1)S(1)} %collective-permute-done.6.refs_3_) | copy-start | bytes 884740
  31.1 17.2 %copy-start.8 = (bf16[128,1152]{1,0:T(8,128)(2,1)}, bf16[128,1152]{1,0:T(8,128)(2,1)S(1)}, u32[]{:S(2)}) copy-start(bf16[128,1152]{1,0:T(8,128)(2,1)S(1)} %collective-permute-done.5.refs_2_) | copy-start | bytes 884740
  31.2 10.1 %copy-start.10 = (bf16[128,1152]{1,0:T(8,128)(2,1)}, bf16[128,1152]{1,0:T(8,128)(2,1)S(1)}, u32[]{:S(2)}) copy-start(bf16[128,1152]{1,0:T(8,128)(2,1)S(1)} %collective-permute-done.4.refs_1_) | copy-start | bytes 884740
  31.2 60.0 %all-to-all-start.1 = ((bf16[4,256,1152]{2,1,0:T(8,128)(2,1)}), bf16[4,256,1152]{2,1,0:T(8,128)(2,1)}, u32[]{:S(2)}, u32[]{:S(2)}) async-start(bf16[4,256,1152]{2,1,0:T(8,128)(2,1)} %broadcast_select_fusion), calls=%async_computation.1 | async-start | bytes 4718592 | tf_op jit(solution)/shard_map/all_to_all | solution.py:371
  35.8 22.4 %collective-permute-start.10 = (bf16[384,1152]{1,0:T(8,128)(2,1)S(1)}, bf16[384,1152]{1,0:T(8,128)(2,1)}, u32[]{:S(2)}, u32[]{:S(2)}) collective-permute-start(bf16[384,1152]{1,0:T(8,128)(2,1)S(1)} %constant_dynamic-update-slice_fusion.refs_1_), channel_id=1, source_target_pairs={{0,24},{4,28},{8,16},{12,20},{16,8},{20,12},{24,0},{28,4},{1,25},{... | collective-permute-start | bytes 2654216 | tf_op jit(solution)/shard_map/ppermute | solution.py:325
  38.0 39.4 %collective-permute-start.9 = (bf16[384,1152]{1,0:T(8,128)(2,1)S(1)}, bf16[384,1152]{1,0:T(8,128)(2,1)}, u32[]{:S(2)}, u32[]{:S(2)}) collective-permute-start(bf16[384,1152]{1,0:T(8,128)(2,1)S(1)} %constant_dynamic-update-slice_fusion.refs_1_), channel_id=1, source_target_pairs={{0,16},{4,20},{8,24},{12,28},{16,0},{20,4},{24,8},{28,12},{1,17},{... | collective-permute-start | bytes 2654216 | tf_op jit(solution)/shard_map/ppermute | solution.py:325
  38.3 39.1 %collective-permute-start.8 = (bf16[384,1152]{1,0:T(8,128)(2,1)S(1)}, bf16[384,1152]{1,0:T(8,128)(2,1)}, u32[]{:S(2)}, u32[]{:S(2)}) collective-permute-start(bf16[384,1152]{1,0:T(8,128)(2,1)S(1)} %constant_dynamic-update-slice_fusion.refs_1_), channel_id=1, source_target_pairs={{0,8},{4,12},{8,0},{12,4},{16,24},{20,28},{24,16},{28,20},{1,9},{5... | collective-permute-start | bytes 2654216 | tf_op jit(solution)/shard_map/ppermute | solution.py:325
  38.5 2.7 %collective-permute-start.7 = (s32[4,512]{1,0:T(4,128)S(1)}, s32[4,512]{1,0:T(4,128)S(1)}, u32[]{:S(2)}, u32[]{:S(2)}) collective-permute-start(s32[4,512]{1,0:T(4,128)S(1)} %bitcast.34), channel_id=1, source_target_pairs={{0,4},{4,0},{8,12},{12,8},{16,20},{20,16},{24,28},{28,24},{1,5},{5... | collective-permute-start | bytes 24584 | tf_op jit(solution)/shard_map/ppermute | solution.py:325
  40.4 7.9 %collective-permute-start.11 = (bf16[128,1152]{1,0:T(8,128)(2,1)S(1)}, bf16[128,1152]{1,0:T(8,128)(2,1)S(1)}, u32[]{:S(2)}, u32[]{:S(2)}) collective-permute-start(bf16[128,1152]{1,0:T(8,128)(2,1)S(1)} %copy-done.5), channel_id=1, source_target_pairs={{0,4},{4,0},{8,12},{12,8},{16,20},{20,16},{24,28},{28,24},{1,5},{5... | collective-permute-start | bytes 884744 | tf_op jit(solution)/shard_map/ppermute | solution.py:325
  41.3 7.4 %collective-permute-start.12 = (bf16[128,1152]{1,0:T(8,128)(2,1)S(1)}, bf16[128,1152]{1,0:T(8,128)(2,1)S(1)}, u32[]{:S(2)}, u32[]{:S(2)}) collective-permute-start(bf16[128,1152]{1,0:T(8,128)(2,1)S(1)} %collective-permute-done.4.refs_1_), channel_id=1, source_target_pairs={{0,4},{4,0},{8,12},{12,8},{16,20},{20,16},{24,28},{28,24},{1,5},{5... | collective-permute-start | bytes 884744 | tf_op jit(solution)/shard_map/ppermute | solution.py:325
  48.4 1.7 copy-start.12
  48.4 1.7 collective-permute-start.13
  48.6 1.5 copy-start.14
  48.6 1.8 %collective-permute-start.14 = (bf16[128,1152]{1,0:T(8,128)(2,1)S(1)}, bf16[128,1152]{1,0:T(8,128)(2,1)S(1)}, u32[]{:S(2)}, u32[]{:S(2)}) collective-permute-start(bf16[128,1152]{1,0:T(8,128)(2,1)S(1)} %collective-permute-done.6.refs_3_), channel_id=1, source_target_pairs={{0,4},{4,0},{8,12},{12,8},{16,20},{20,16},{24,28},{28,24},{1,5},{5... | collective-permute-start | bytes 884744 | tf_op jit(solution)/shard_map/ppermute | solution.py:325
  49.0 29.5 %copy-start.20 = (f32[3456]{0:T(1024)S(1)}, f32[3456]{0:T(1024)}, u32[]{:S(2)}) copy-start(f32[3456]{0:T(1024)} %param.15) | copy-start | bytes 41476
  50.5 1.0 copy-start.7
  51.4 1.0 copy-start.9
  52.4 1.0 copy-start.11
  53.3 1.0 copy-start.13
  54.3 1.0 copy-start.15
  77.4 7.9 %collective-permute-start.15 = (bf16[384,1152]{1,0:T(8,128)(2,1)S(1)}, bf16[384,1152]{1,0:T(8,128)(2,1)S(1)}, u32[]{:S(2)}, u32[]{:S(2)}) collective-permute-start(bf16[384,1152]{1,0:T(8,128)(2,1)S(1)} %constant_dynamic-update-slice_fusion.refs_1_), channel_id=1, source_target_pairs={{0,4},{4,0},{8,12},{12,8},{16,20},{20,16},{24,28},{28,24},{1,5},{5... | collective-permute-start | bytes 2654216 | tf_op jit(solution)/shard_map/ppermute | solution.py:325
  78.0 7.3 %collective-permute-start.16 = (bf16[384,1152]{1,0:T(8,128)(2,1)}, bf16[384,1152]{1,0:T(8,128)(2,1)S(1)}, u32[]{:S(2)}, u32[]{:S(2)}) collective-permute-start(bf16[384,1152]{1,0:T(8,128)(2,1)} %collective-permute-done.8.refs_2_), channel_id=1, source_target_pairs={{0,4},{4,0},{8,12},{12,8},{16,20},{20,16},{24,28},{28,24},{1,5},{5... | collective-permute-start | bytes 2654216 | tf_op jit(solution)/shard_map/ppermute | solution.py:325
  78.0 7.3 %collective-permute-start.17 = (bf16[384,1152]{1,0:T(8,128)(2,1)}, bf16[384,1152]{1,0:T(8,128)(2,1)S(1)}, u32[]{:S(2)}, u32[]{:S(2)}) collective-permute-start(bf16[384,1152]{1,0:T(8,128)(2,1)} %collective-permute-done.9.refs_3_), channel_id=1, source_target_pairs={{0,4},{4,0},{8,12},{12,8},{16,20},{20,16},{24,28},{28,24},{1,5},{5... | collective-permute-start | bytes 2654216 | tf_op jit(solution)/shard_map/ppermute | solution.py:325
  78.5 6.8 %collective-permute-start.18 = (bf16[384,1152]{1,0:T(8,128)(2,1)}, bf16[384,1152]{1,0:T(8,128)(2,1)S(1)}, u32[]{:S(2)}, u32[]{:S(2)}) collective-permute-start(bf16[384,1152]{1,0:T(8,128)(2,1)} %collective-permute-done.10.refs_4_), channel_id=1, source_target_pairs={{0,4},{4,0},{8,12},{12,8},{16,20},{20,16},{24,28},{28,24},{1,5},{5... | collective-permute-start | bytes 2654216 | tf_op jit(solution)/shard_map/ppermute | solution.py:325
  89.8 1.4 copy-start.1
  111.9 9.1 %collective-permute-start.19 = (bf16[2304,1024]{1,0:T(8,128)(2,1)}, bf16[2304,1024]{1,0:T(8,128)(2,1)}, u32[]{:S(2)}, u32[]{:S(2)}) collective-permute-start(bf16[2304,1024]{1,0:T(8,128)(2,1)} %get-tuple-element.49.refs_0_.refs_2_), channel_id=1, source_target_pairs={{0,4},{4,0},{8,12},{12,8},{16,20},{20,16},{24,28},{28,24},{1,5},{5... | collective-permute-start | bytes 14155784 | tf_op jit(solution)/shard_map/ppermute | solution.py:325
  121.0 2.3 %copy-start.17 = (bf16[2304,1024]{1,0:T(8,128)(2,1)S(1)}, bf16[2304,1024]{1,0:T(8,128)(2,1)}, u32[]{:S(2)}) copy-start(bf16[2304,1024]{1,0:T(8,128)(2,1)} %get-tuple-element.49.refs_0_.refs_2_) | copy-start | bytes 14155780
  123.3 1.3 copy-start.19
  124.6 12.0 %copy-start.2 = (bf16[1152,1152]{1,0:T(8,128)(2,1)S(1)}, bf16[1152,1152]{1,0:T(8,128)(2,1)}, u32[]{:S(2)}) copy-start(bf16[1152,1152]{1,0:T(8,128)(2,1)} %w_ref.3) | copy-start | bytes 7962628
  124.6 12.0 %copy-start.4 = (bf16[256,1152]{1,0:T(8,128)(2,1)S(1)}, bf16[256,1152]{1,0:T(8,128)(2,1)}, u32[]{:S(2)}) copy-start(bf16[256,1152]{1,0:T(8,128)(2,1)} %get-tuple-element.51.gate_ref) | copy-start | bytes 1769476
  124.6 12.0 %copy-start.16 = (s32[2]{0:T(128)S(1)}, s32[2]{0:T(128)}, u32[]{:S(2)}) copy-start(s32[2]{0:T(128)} %pad_add_fusion.place_ref) | copy-start | bytes 28
  136.6 3.1 %copy-start.18 = (bf16[2304,1024]{1,0:T(8,128)(2,1)S(1)}, bf16[2304,1024]{1,0:T(8,128)(2,1)}, u32[]{:S(2)}) copy-start(bf16[2304,1024]{1,0:T(8,128)(2,1)} %get-tuple-element.49.refs_0_.refs_2_) | copy-start | bytes 14155780
  139.6 27.6 %collective-permute-start.20 = (bf16[256,1152]{1,0:T(8,128)(2,1)S(1)}, bf16[256,1152]{1,0:T(8,128)(2,1)S(1)}, u32[]{:S(2)}, u32[]{:S(2)}) collective-permute-start(bf16[256,1152]{1,0:T(8,128)(2,1)S(1)} %finish.2), channel_id=1, source_target_pairs={{0,3},{1,2},{2,1},{3,0},{4,7},{5,6},{6,5},{7,4},{8,11},{9,10},{10,... | collective-permute-start | bytes 1769480 | tf_op jit(solution)/shard_map/ppermute | solution.py:325
  156.0 1.1 copy-start.3
  167.3 2.5 %collective-permute-start.21 = (bf16[256,1152]{1,0:T(8,128)(2,1)S(1)}, bf16[256,1152]{1,0:T(8,128)(2,1)S(1)}, u32[]{:S(2)}, u32[]{:S(2)}) collective-permute-start(bf16[256,1152]{1,0:T(8,128)(2,1)S(1)} %broadcast_select_fusion.3), channel_id=1, source_target_pairs={{0,4},{4,0},{8,12},{12,8},{16,20},{20,16},{24,28},{28,24},{1,5},{5... | collective-permute-start | bytes 1769480 | tf_op jit(solution)/shard_map/ppermute | solution.py:325
